TPU v7x, 32 devices: a whole 2x2x4 slice. The times are simulated.
32 devices in a mesh: fsdp: 8 (over y, x, core), blk: 4 (over z).
Axes of the slice: x: 2, y: 2, z: 4, core: 2. Of those that a mesh axis runs over, the one named last changes fastest.
Arguments:
- frames: bfloat16 [2, 4096, 1024], P(None, ('fsdp', 'blk')), may hold values from -6 to 6
- skipped: bfloat16 [2, 4096, 1024], P(None, ('fsdp', 'blk')), may hold values from -6 to 6
- lengths: int32 [2, 8, 9], P(None, 'fsdp'), may hold values from 1 to 504, as said below
- merger: bfloat16 [2048, 1024], P('fsdp'), may hold values from -0.125 to 0.125
- projector: bfloat16 [1024, 3072], P('fsdp'), may hold values from -0.1875 to 0.1875
- combiner: bfloat16 [1024, 1024], P('fsdp'), may hold values from -1 to 1
- expander: bfloat16 [1024, 4096], P('fsdp'), may hold values from -0.1875 to 0.1875
- reducer: bfloat16 [4096, 1024], P('fsdp'), may hold values from -0.09375 to 0.09375
- prenorm: bfloat16 [1024], P('fsdp'), may hold values from 0.25 to 1.75
- midnorm: bfloat16 [1024], P('fsdp'), may hold values from 0.25 to 1.75
- cotangent: bfloat16 [2, 4096, 1024], P(None, ('fsdp', 'blk')), may hold values from -6 to 6
Outputs:
- result: bfloat16 [2, 4096, 1024], P(None, ('fsdp', 'blk'))
- frames_gradient: float32 [2, 4096, 1024], P(None, ('fsdp', 'blk'))
- skipped_gradient: float32 [2, 4096, 1024], P(None, ('fsdp', 'blk'))
- merger_gradient: float32 [2048, 1024], P('fsdp')
- projector_gradient: float32 [1024, 3072], P('fsdp')
- combiner_gradient: float32 [1024, 1024], P('fsdp')
- expander_gradient: float32 [1024, 4096], P('fsdp')
- reducer_gradient: float32 [4096, 1024], P('fsdp')
- prenorm_gradient: float32 [1024], P('fsdp')
- midnorm_gradient: float32 [1024], P('fsdp')
Inputs may be any that keep to these rules, and one draw needn't show every extreme that they name: The 9 lengths of each row add up to 512; in each row one of them, at a place drawn from the seed, begins within the first 128 frames of the stream and ends within its last 128 frames; every other has at most 15 frames.
All inputs are finite; a program needn't handle non-finite values.
Results may differ from a plain program's by a relative error of at most 0.02.
Values may be sent and summed in bfloat16 or wider, within the bound.
No kernel may reach another device: no remote copies, remote signals or barrier semaphores. Data moves between devices by JAX's collectives and lax.ppermute only.
A program may use at most 256 MiB of HBM per device.

v0:
```python
import functools
import math

import jax
import jax.numpy as jnp
from jax import lax
from jax.sharding import PartitionSpec as P

D = 1024
HEADS = 16
HEAD_DIM = 64
MB = 2


NEG_BIG = -1e30


def shortened(shard):

    def short(part):
        return part.astype(jnp.bfloat16) if part.dtype == jnp.float32 else part

    return jax.tree.map(short, shard)


def rms_scale(hidden, gain):
    return hidden * lax.rsqrt(jnp.mean(hidden * hidden, -1, keepdims=True) + 1e-06) * gain


def layout(lengths_row, stream):
    ends = jnp.cumsum(lengths_row)
    offsets = jnp.arange(stream, dtype=jnp.int32)
    before = (ends[None, :] <= offsets[:, None]).astype(jnp.int32)
    segment = jnp.sum(before, 1)
    begins = jnp.sum(before * lengths_row[None, :], 1)
    return (segment, offsets - begins)


def rotary_tables(position):
    halfway = HEAD_DIM // 2
    inverse = 10000.0 ** (-jnp.arange(halfway, dtype=jnp.float32) * 2.0 / HEAD_DIM)
    angles = position.astype(jnp.float32)[:, None] * inverse[None, :]
    return (jnp.cos(angles), jnp.sin(angles))


def rotate(tensor, cosine, sine):
    halfway = tensor.shape[-1] // 2
    first = tensor[..., :halfway]
    second = tensor[..., halfway:]
    cosine = cosine[:, None, :]
    sine = sine[:, None, :]
    return jnp.concatenate([first * cosine - second * sine, second * cosine + first * sine], -1)


def unrotate(tensor, cosine, sine):
    halfway = tensor.shape[-1] // 2
    first = tensor[..., :halfway]
    second = tensor[..., halfway:]
    cosine = cosine[:, None, :]
    sine = sine[:, None, :]
    return jnp.concatenate([first * cosine + second * sine, second * cosine - first * sine], -1)


def attend_piece(carry, key_piece, value_piece, query_rot, query_seg, segments_all):
    run_max, run_sum, run_acc = carry
    count = key_piece.shape[0]
    keys_split = key_piece.reshape(count, HEADS, HEAD_DIM)
    values_split = value_piece.reshape(count, HEADS, HEAD_DIM)
    scores = jnp.einsum(
        "qhd,khd->hqk", query_rot, keys_split, preferred_element_type=jnp.float32
    ) * HEAD_DIM ** (-0.5)
    allowed = (query_seg[:, None] == segments_all[None, :])[None]
    scores = jnp.where(allowed, scores, NEG_BIG)
    new_max = jnp.maximum(run_max, jnp.max(scores, -1))
    weights = jnp.where(allowed, jnp.exp(scores - new_max[..., None]), 0.0)
    run_sum = jnp.sum(weights, -1)
    run_acc = jnp.einsum(
        "hqk,khd->hqd",
        weights.astype(jnp.bfloat16),
        values_split,
        preferred_element_type=jnp.float32,
    )
    return (new_max, run_sum, run_acc)


def attention_back(
    query_rot, grad_low, log_total, delta, query_seg, segments_all, all_keys, all_values, block
):
    stream = all_keys.shape[0]
    count = stream // block
    scale = HEAD_DIM ** (-0.5)

    def step(query_grad, index):
        start = index * block
        keys_split = lax.dynamic_slice_in_dim(all_keys, start, block).reshape(
            block, HEADS, HEAD_DIM
        )
        values_split = lax.dynamic_slice_in_dim(all_values, start, block).reshape(
            block, HEADS, HEAD_DIM
        )
        key_seg = lax.dynamic_slice_in_dim(segments_all, start, block)
        scores = (
            jnp.einsum("qhd,khd->hqk", query_rot, keys_split, preferred_element_type=jnp.float32)
            * scale
        )
        allowed = (query_seg[:, None] == key_seg[None, :])[None]
        probs = jnp.where(allowed, jnp.exp(scores - log_total[..., None]), 0.0)
        probs_grad = jnp.einsum(
            "qhd,khd->hqk", grad_low, values_split, preferred_element_type=jnp.float32
        )
        score_grad = (probs * (probs_grad - delta[..., None])).astype(jnp.bfloat16)
        value_grad = jnp.einsum(
            "hqk,qhd->khd", probs.astype(jnp.bfloat16), grad_low, preferred_element_type=jnp.float32
        )
        key_grad = (
            jnp.einsum("hqk,qhd->khd", score_grad, query_rot, preferred_element_type=jnp.float32)
            * scale
        )
        query_grad = (
            query_grad
            + jnp.einsum("hqk,khd->hqd", score_grad, keys_split, preferred_element_type=jnp.float32)
            * scale
        )
        return (query_grad, (key_grad, value_grad))

    init = jnp.zeros((HEADS, query_rot.shape[0], HEAD_DIM), jnp.float32)
    query_grad, (key_grads, value_grads) = lax.scan(step, init, jnp.arange(count, dtype=jnp.int32))
    return (
        query_grad,
        key_grads.reshape(stream, HEADS * HEAD_DIM),
        value_grads.reshape(stream, HEADS * HEAD_DIM),
    )


def local(
    frames,
    skipped,
    lengths,
    merger,
    projector,
    combiner,
    expander,
    reducer,
    prenorm,
    midnorm,
    cotangent,
):
    tok_rows = frames.shape[1]
    stream = tok_rows * lax.axis_size("blk")
    block = math.gcd(stream, 1024)
    offset = lax.axis_index("blk") * tok_rows
    shards = (merger, projector, combiner, expander, reducer, prenorm, midnorm)
    gelu_tanh = functools.partial(jax.nn.gelu, approximate=True)
    results = []
    frame_grads = []
    skip_grads = []
    sums = None
    for micro in range(MB):
        weights = (
            lax.all_gather(shards[0], "fsdp", axis=0, tiled=True),
            lax.all_gather(shards[1], "fsdp", axis=0, tiled=True),
            lax.all_gather(shards[2], "fsdp", axis=0, tiled=True),
            lax.all_gather(shards[3], "fsdp", axis=0, tiled=True),
            lax.all_gather(shards[4], "fsdp", axis=0, tiled=True),
            lax.all_gather(shards[5], "fsdp", axis=0, tiled=True),
            lax.all_gather(shards[6], "fsdp", axis=0, tiled=True),
        )
        w_merger, w_projector, w_combiner, w_expander, w_reducer, gain_low, mid_low = weights
        gain_pre = gain_low.astype(jnp.float32)
        gain_mid = mid_low.astype(jnp.float32)
        segments_all, positions_all = layout(lengths[micro, 0], stream)
        query_seg = lax.dynamic_slice_in_dim(segments_all, offset, tok_rows)
        query_pos = lax.dynamic_slice_in_dim(positions_all, offset, tok_rows)
        cosine, sine = rotary_tables(query_pos)
        joined = jnp.concatenate([frames[micro], skipped[micro]], -1)
        hidden_zero = jnp.dot(joined, w_merger, preferred_element_type=jnp.float32)
        act_first = rms_scale(hidden_zero, gain_pre).astype(jnp.bfloat16)
        united = jnp.dot(act_first, w_projector, preferred_element_type=jnp.float32)
        query_rot = rotate(united[:, :D].reshape(tok_rows, HEADS, HEAD_DIM), cosine, sine).astype(
            jnp.bfloat16
        )
        key_flat = (
            rotate(united[:, D : 2 * D].reshape(tok_rows, HEADS, HEAD_DIM), cosine, sine)
            .astype(jnp.bfloat16)
            .reshape(tok_rows, D)
        )
        value_flat = united[:, 2 * D :].astype(jnp.bfloat16)
        init = (
            jnp.full((HEADS, tok_rows), NEG_BIG, jnp.float32),
            jnp.zeros((HEADS, tok_rows), jnp.float32),
            jnp.zeros((HEADS, tok_rows, HEAD_DIM), jnp.float32),
        )
        run_max, run_sum, run_acc = attend_piece(
            init,
            lax.all_gather(key_flat, "blk", axis=0, tiled=True),
            lax.all_gather(value_flat, "blk", axis=0, tiled=True),
            query_rot,
            query_seg,
            segments_all,
        )
        log_total = run_max + jnp.log(run_sum)
        attended_f32 = jnp.transpose(run_acc / run_sum[..., None], (1, 0, 2)).reshape(tok_rows, D)
        attended_low = attended_f32.astype(jnp.bfloat16)
        hidden_one = hidden_zero + jnp.dot(
            attended_low, w_combiner, preferred_element_type=jnp.float32
        )
        act_second = rms_scale(hidden_one, gain_mid).astype(jnp.bfloat16)
        upper = jnp.dot(act_second, w_expander, preferred_element_type=jnp.float32)
        activ_low = gelu_tanh(upper).astype(jnp.bfloat16)
        output = hidden_one + jnp.dot(activ_low, w_reducer, preferred_element_type=jnp.float32)
        results.append(output.astype(jnp.bfloat16))
        weights = (
            lax.all_gather(shards[0], "fsdp", axis=0, tiled=True),
            lax.all_gather(shards[1], "fsdp", axis=0, tiled=True),
            lax.all_gather(shards[2], "fsdp", axis=0, tiled=True),
            lax.all_gather(shards[3], "fsdp", axis=0, tiled=True),
            lax.all_gather(shards[4], "fsdp", axis=0, tiled=True),
            lax.all_gather(shards[5], "fsdp", axis=0, tiled=True),
            lax.all_gather(shards[6], "fsdp", axis=0, tiled=True),
        )
        w_merger, w_projector, w_combiner, w_expander, w_reducer, gain_low, mid_low = weights
        grad_out = cotangent[micro]
        reducer_grad = jnp.dot(activ_low.T, grad_out, preferred_element_type=jnp.float32)
        activ_grad = jnp.dot(grad_out, w_reducer.T, preferred_element_type=jnp.float32)
        unused, gelu_pull = jax.vjp(gelu_tanh, upper)
        upper_grad = gelu_pull(activ_grad)[0].astype(jnp.bfloat16)
        expander_grad = jnp.dot(act_second.T, upper_grad, preferred_element_type=jnp.float32)
        second_grad = jnp.dot(upper_grad, w_expander.T, preferred_element_type=jnp.float32)
        unused, mid_pull = jax.vjp(rms_scale, hidden_one, gain_mid)
        one_norm_grad, mid_grad = mid_pull(second_grad)
        one_grad = grad_out.astype(jnp.float32) + one_norm_grad
        one_low = one_grad.astype(jnp.bfloat16)
        combiner_grad = jnp.dot(attended_low.T, one_low, preferred_element_type=jnp.float32)
        attended_grad = jnp.dot(one_low, w_combiner.T, preferred_element_type=jnp.float32).astype(
            jnp.bfloat16
        )
        grad_split = attended_grad.reshape(tok_rows, HEADS, HEAD_DIM)
        delta = jnp.sum(
            grad_split.astype(jnp.float32) * attended_f32.reshape(tok_rows, HEADS, HEAD_DIM), -1
        ).T
        all_keys, all_values = (
            lax.all_gather(key_flat, "blk", axis=0, tiled=True),
            lax.all_gather(value_flat, "blk", axis=0, tiled=True),
        )
        query_grad, key_terms, value_terms = attention_back(
            query_rot,
            grad_split,
            log_total,
            delta,
            query_seg,
            segments_all,
            all_keys,
            all_values,
            block,
        )
        key_grad, value_grad = (
            lax.psum_scatter(
                key_terms.astype(jnp.bfloat16), "blk", scatter_dimension=0, tiled=True
            ).astype(jnp.float32),
            lax.psum_scatter(
                value_terms.astype(jnp.bfloat16), "blk", scatter_dimension=0, tiled=True
            ).astype(jnp.float32),
        )
        query_back = unrotate(jnp.transpose(query_grad, (1, 0, 2)), cosine, sine).reshape(
            tok_rows, D
        )
        key_back = unrotate(key_grad.reshape(tok_rows, HEADS, HEAD_DIM), cosine, sine).reshape(
            tok_rows, D
        )
        united_grad = jnp.concatenate([query_back, key_back, value_grad], -1).astype(jnp.bfloat16)
        projector_grad = jnp.dot(act_first.T, united_grad, preferred_element_type=jnp.float32)
        first_grad = jnp.dot(united_grad, w_projector.T, preferred_element_type=jnp.float32)
        unused, pre_pull = jax.vjp(rms_scale, hidden_zero, gain_pre)
        zero_norm_grad, pre_grad = pre_pull(first_grad)
        zero_low = (one_grad + zero_norm_grad).astype(jnp.bfloat16)
        merger_grad = jnp.dot(joined.T, zero_low, preferred_element_type=jnp.float32)
        joined_grad = jnp.dot(zero_low, w_merger.T, preferred_element_type=jnp.float32)
        frame_grads.append(joined_grad[:, :D])
        skip_grads.append(joined_grad[:, D:])
        grads = (
            merger_grad,
            projector_grad,
            combiner_grad,
            expander_grad,
            reducer_grad,
            pre_grad,
            mid_grad,
        )
        sums = grads if sums is None else jax.tree.map(jnp.add, sums, grads)
    owned = jax.tree.map(
        lambda part: part.astype(jnp.float32),
        lax.psum_scatter(shortened(sums), "fsdp", scatter_dimension=0, tiled=True),
    )
    summed = jax.tree.map(lambda part: part.astype(jnp.float32), lax.psum(shortened(owned), "blk"))
    return (
        jnp.stack(results),
        jnp.stack(frame_grads),
        jnp.stack(skip_grads),
        summed[0],
        summed[1],
        summed[2],
        summed[3],
        summed[4],
        summed[5],
        summed[6],
    )


def solution(mesh):
    return jax.shard_map(
        local,
        mesh=mesh,
        in_specs=(
            P(None, ("fsdp", "blk"), None),
            P(None, ("fsdp", "blk"), None),
            P(None, "fsdp", None),
            P("fsdp", None),
            P("fsdp", None),
            P("fsdp", None),
            P("fsdp", None),
            P("fsdp", None),
            P("fsdp"),
            P("fsdp"),
            P(None, ("fsdp", "blk"), None),
        ),
        out_specs=(
            P(None, ("fsdp", "blk"), None),
            P(None, ("fsdp", "blk"), None),
            P(None, ("fsdp", "blk"), None),
            P("fsdp", None),
            P("fsdp", None),
            P("fsdp", None),
            P("fsdp", None),
            P("fsdp", None),
            P("fsdp"),
            P("fsdp"),
        ),
        check_vma=False,
    )
```

profile of v0, /device:TPU:0, one launch (start us, length us, event | category | flops | bytes accessed | tf_op | source)
XLA Modules:
  0.0 979.6 jit_solution(3806385922242203337)
XLA Ops:
  8.7 10.3 %all-gather = bf16[8,1,128]{2,1,0:T(2,128)(2,1)S(1)} all-gather(bf16[1,1,128]{2,1,0:T(2,128)(2,1)} %bitcast.211), channel_id=1, replica_groups=mesh['fsdp'=8,'blk'=4] {'fsdp'}, dimensions={0}, use_global_device_ids=true | all-gather | bytes 2304 | tf_op jit(solution)/shard_map/all_gather | solution.py:165
  20.4 29.0 %all-gather.12.cloned.1.call-done = bf16[2048,1024]{1,0:T(8,128)(2,1)} async-done(((bf16[256,1024]{1,0:T(8,128)(2,1)}), bf16[2048,1024]{1,0:T(8,128)(2,1)}) %all-gather.12.cloned.1.call-update) | async-done | bytes 4194320 | tf_op jit(solution)/shard_map/all_gather | solution.py:160
  49.3 3.0 multiply_reduce_fusion.11
  52.4 44.4 %all-gather.14.cloned.1.call-done = bf16[1024,3072]{1,0:T(8,128)(2,1)} async-done(((bf16[128,3072]{1,0:T(8,128)(2,1)}), bf16[1024,3072]{1,0:T(8,128)(2,1)}) %all-gather.14.cloned.1.call-update) | async-done | bytes 6291472 | tf_op jit(solution)/shard_map/all_gather | solution.py:161
  96.8 3.8 fusion.125
  102.0 3.0 multiply_reduce_fusion.13
  105.0 3.8 fusion.122
  111.8 2.3 fusion.127
  115.3 2.0 copy.50
  117.3 1.9 subtract_convert_fusion.7
  126.2 8.7 all-gather.1
  135.3 2.3 copy.54
  137.6 21.3 %all-gather.18.cloned.1.call-done = bf16[512,1024]{1,0:T(8,128)(2,1)} async-done(((bf16[128,1024]{1,0:T(8,128)(2,1)}), bf16[512,1024]{1,0:T(8,128)(2,1)}) %all-gather.18.cloned.1.call-update) | async-done | bytes 1048592 | tf_op jit(solution)/shard_map/all_gather | solution.py:196
  158.9 2.5 copy.51
  161.4 29.2 %all-gather.16.cloned.1.call-done = bf16[512,1024]{0,1:T(8,128)(2,1)} async-done(((bf16[128,1024]{0,1:T(8,128)(2,1)}), bf16[512,1024]{0,1:T(8,128)(2,1)}) %all-gather.16.cloned.1.call-update) | async-done | bytes 1048592 | tf_op jit(solution)/shard_map/all_gather | solution.py:195
  190.7 2.1 select_reduce_fusion.1
  194.9 2.1 fusion.130
  196.9 21.7 %all-gather.20.cloned.1.call-done = bf16[1024,1024]{1,0:T(8,128)(2,1)} async-done(((bf16[128,1024]{1,0:T(8,128)(2,1)}), bf16[1024,1024]{1,0:T(8,128)(2,1)}) %all-gather.20.cloned.1.call-update) | async-done | bytes 2097168 | tf_op jit(solution)/shard_map/all_gather | solution.py:162
  218.6 2.9 multiply_reduce_fusion.12
  222.0 29.0 %all-gather.26.cloned.1.call-done = bf16[512,1024]{0,1:T(8,128)(2,1)} async-done(((bf16[128,1024]{0,1:T(8,128)(2,1)}), bf16[512,1024]{0,1:T(8,128)(2,1)}) %all-gather.26.cloned.1.call-update) | async-done | bytes 1048592 | tf_op jit(solution)/shard_map/all_gather | solution.py:195
  251.0 2.1 select_reduce_fusion
  255.2 3.0 fusion.129
  261.8 43.8 %all-gather.22.cloned.1.call-done = bf16[1024,4096]{1,0:T(8,128)(2,1)} async-done(((bf16[128,4096]{1,0:T(8,128)(2,1)}), bf16[1024,4096]{1,0:T(8,128)(2,1)}) %all-gather.22.cloned.1.call-update) | async-done | bytes 8388624 | tf_op jit(solution)/shard_map/all_gather | solution.py:163
  305.6 6.3 fusion.124
  312.0 2.7 fusion.126
  314.6 47.3 %all-gather.24.cloned.1.call-done = bf16[4096,1024]{1,0:T(8,128)(2,1)} async-done(((bf16[512,1024]{1,0:T(8,128)(2,1)}), bf16[4096,1024]{1,0:T(8,128)(2,1)}) %all-gather.24.cloned.1.call-update) | async-done | bytes 8388624 | tf_op jit(solution)/shard_map/all_gather | solution.py:164
  361.9 8.2 fusion.12
  370.2 3.6 fusion.19
  373.8 2.9 fusion.132
  376.8 3.5 multiply_reduce_fusion.1
  386.7 4.2 multiply_convert_fusion
  393.7 2.3 copy.61
  397.5 2.6 convolution_convert_fusion.1
  402.4 4.1 multiply_convert_fusion.1
  409.7 3.3 fusion.41
  414.4 4.3 fusion.38
  418.7 2.4 copy.59
  421.2 3.0 fusion.44
  427.0 2.1 add_convert_fusion.4
  431.3 20.1 %reduce-scatter.28.cloned.1.call-done = bf16[128,1024]{1,0:T(8,128)(2,1)} async-done(((bf16[512,1024]{1,0:T(8,128)(2,1)}), bf16[128,1024]{1,0:T(8,128)(2,1)}) %reduce-scatter.28.cloned.1.call-update) | async-done | bytes 262160
  452.7 2.2 add_convert_fusion.6
  454.8 1.9 add_convert_fusion.8
  457.5 22.5 %reduce-scatter.34.cloned.1.call-done = bf16[128,1024]{1,0:T(8,128)(2,1)} async-done(((bf16[512,1024]{1,0:T(8,128)(2,1)}), bf16[128,1024]{1,0:T(8,128)(2,1)}) %reduce-scatter.34.cloned.1.call-update) | async-done | bytes 262160
  481.8 27.0 %reduce-scatter.30.cloned.1.call-done = bf16[128,1024]{1,0:T(8,128)(2,1)} async-done(((bf16[512,1024]{1,0:T(8,128)(2,1)}), bf16[128,1024]{1,0:T(8,128)(2,1)}) %reduce-scatter.30.cloned.1.call-update) | async-done | bytes 262160
  513.8 5.5 fusion.71
  519.4 2.4 multiply_reduce_fusion.3
  524.2 3.2 add_convert_fusion.3
  528.6 1.9 fusion.72
  530.5 4.7 add_convert_fusion.2
  536.9 8.2 fusion.79
  545.1 9.4 add_convert_fusion
  555.5 10.9 %fusion.123 = f32[1024,4096]{1,0:T(8,128)} fusion(bf16[128,4096]{1,0:T(8,128)(2,1)} %copy-done.27, f32[128,1024]{1,0:T(8,128)S(1)} %copy-done.6, f32[1024]{0:T(1024)S(1)} %bitcast.199, f32[128]{0:T(128)S(1)} %copy-done.72), kind=kOutput, calls=%fused_computation.230 | convolution fusion | flops 1074135040 | bytes 18354688 | tf_op jit(solution)/shard_map/dot_general | solution.py:227
  566.4 12.3 %add_convert_fusion.1 = bf16[1024,4096]{1,0:T(8,128)(2,1)} fusion(f32[1024,4096]{1,0:T(8,128)} %fusion.123, bf16[128,4096]{1,0:T(8,128)(2,1)S(1)} %copy-done.25, f32[128,1024]{1,0:T(8,128)S(1)} %copy-done.9, f32[128]{0:T(128)S(1)} %copy-done.77, f32[1024]{0:T(1024)S(1)} %bitcast.200), kind=kOutput, calls=%fused_computation.1 | convolution fusion | flops 1082523648 | bytes 26743296 | tf_op jit(solution)/shard_map/dot_general | solution.py:227
  578.8 28.0 %reduce-scatter.18.cloned.1.call-done = bf16[256,1024]{1,0:T(8,128)(2,1)} async-done(((bf16[2048,1024]{1,0:T(8,128)(2,1)}), bf16[256,1024]{1,0:T(8,128)(2,1)}) %reduce-scatter.18.cloned.1.call-update) | async-done | bytes 524304 | tf_op jit(solution)/shard_map/reduce_scatter | solution.py:292
  606.8 65.0 %reduce-scatter.20.cloned.1.call-done = bf16[128,3072]{1,0:T(8,128)(2,1)} async-done(((bf16[1024,3072]{1,0:T(8,128)(2,1)}), bf16[128,3072]{1,0:T(8,128)(2,1)}) %reduce-scatter.20.cloned.1.call-update) | async-done | bytes 786448 | tf_op jit(solution)/shard_map/reduce_scatter | solution.py:292
  671.8 75.0 %reduce-scatter.26.cloned.1.call-done = bf16[512,1024]{1,0:T(8,128)(2,1)} async-done(((bf16[4096,1024]{1,0:T(8,128)(2,1)}), bf16[512,1024]{1,0:T(8,128)(2,1)}) %reduce-scatter.26.cloned.1.call-update) | async-done | bytes 1048592 | tf_op jit(solution)/shard_map/reduce_scatter | solution.py:292
  746.8 74.6 %reduce-scatter.24.cloned.1.call-done = bf16[128,4096]{1,0:T(8,128)(2,1)} async-done(((bf16[1024,4096]{1,0:T(8,128)(2,1)}), bf16[128,4096]{1,0:T(8,128)(2,1)}) %reduce-scatter.24.cloned.1.call-update) | async-done | bytes 1048592 | tf_op jit(solution)/shard_map/reduce_scatter | solution.py:292
  822.7 5.1 fusion.55
  827.8 5.7 fusion.54
  834.4 12.8 %all-reduce.2 = (bf16[1024]{0:T(1024)(128)(2,1)S(1)}, bf16[1024]{0:T(1024)(128)(2,1)S(1)}) all-reduce(bf16[1024]{0:T(1024)(128)(2,1)S(1)} %add_convert_fusion.14, bf16[1024]{0:T(1024)(128)(2,1)S(1)} %add_convert_fusion.13), channel_id=11, replica_groups=mesh['fsdp'=8,'blk'=4] {'fsdp'}, use_global_device_ids=true, to_apply=%region_36.37.clone | all-reduce | flops 2048 | bytes 8192
  847.4 12.7 %all-reduce.3 = (bf16[128]{0:T(256)(128)(2,1)S(1)}, bf16[128]{0:T(256)(128)(2,1)S(1)}) all-reduce(bf16[128]{0:T(256)(128)(2,1)S(1)} %dynamic-slice.1, bf16[128]{0:T(256)(128)(2,1)S(1)} %dynamic-slice.3), channel_id=1, replica_groups=mesh['fsdp'=8,'blk'=4] {'blk'}, use_global_device_ids=true, to_apply=%region_37.38 | all-reduce | flops 256 | bytes 1024 | tf_op jit(solution)/shard_map/psum | solution.py:294
  861.2 3.8 fusion.133
  869.7 94.4 %all-reduce.7.cloned.1.call-done = (bf16[256,1024]{1,0:T(8,128)(2,1)}, bf16[128,3072]{1,0:T(8,128)(2,1)}, bf16[128,1024]{1,0:T(8,128)(2,1)}, bf16[128,4096]{1,0:T(8,128)(2,1)}, bf16[512,1024]{1,0:T(8,128)(2,1)}) async-done(((bf16[256,1024]{1,0:T(8,128)(2,1)}, bf16[128,3072]{1,0:T(8,128)(2,1)}, bf16[128,1024]{1,0:T(8,128)(2,1)}, bf16[128,4096]{1,0:T(8,128)(2,1)}, bf16[512,1024]{1,0:T(8,128)(2,1)}), ...) | async-done | bytes 3670032 | tf_op jit(solution)/shard_map/psum | solution.py:294
  964.1 2.3 convert_element_type.277
  (325 shorter events, 74.6 us)
Async XLA Ops:
  7.2 42.2 %all-gather.12.cloned.1.call-start = ((), (), s32[]{:S(2)}) async-start(), calls=%async_computation.9 | async-start | bytes 4718592 | tf_op jit(solution)/shard_map/all_gather | solution.py:160
  7.9 88.9 %all-gather.14.cloned.1.call-start = ((), (), s32[]{:S(2)}) async-start(), calls=%async_computation.10 | async-start | bytes 7077888 | tf_op jit(solution)/shard_map/all_gather | solution.py:161
  8.7 126.7 %all-gather.28.cloned.1.call-start = ((), (), s32[]{:S(2)}) async-start(), calls=%async_computation.17 | async-start | bytes 1310720 | tf_op jit(solution)/shard_map/all_gather | solution.py:196
  20.4 32.0 %copy-start.28 = (bf16[128,1024]{1,0:T(8,128)(2,1)}, bf16[128,1024]{1,0:T(8,128)(2,1)S(1)}, u32[]{:S(2)}) copy-start(bf16[128,1024]{1,0:T(8,128)(2,1)S(1)} %get-tuple-element.175) | copy-start | bytes 786436
  20.4 81.6 %copy-start.30 = (bf16[128,1024]{1,0:T(8,128)(2,1)}, bf16[128,1024]{1,0:T(8,128)(2,1)S(1)}, u32[]{:S(2)}) copy-start(bf16[128,1024]{1,0:T(8,128)(2,1)S(1)} %get-tuple-element.131) | copy-start | bytes 786436
  20.4 81.6 %copy-start.32 = (bf16[128,1024]{1,0:T(8,128)(2,1)}, bf16[128,1024]{1,0:T(8,128)(2,1)S(1)}, u32[]{:S(2)}) copy-start(bf16[128,1024]{1,0:T(8,128)(2,1)S(1)} %get-tuple-element.176) | copy-start | bytes 786436
  52.3 44.5 %copy-start.90 = (f32[128]{0:T(128)}, f32[128]{0:T(128)S(1)}, u32[]{:S(2)}) copy-start(f32[128]{0:T(128)S(1)} %get-tuple-element.157) | copy-start | bytes 1540
  52.4 48.3 %copy-start.80 = (f32[128]{0:T(128)}, f32[128]{0:T(128)S(1)}, u32[]{:S(2)}) copy-start(f32[128]{0:T(128)S(1)} %fusion.98) | copy-start | bytes 1540
  96.8 4.7 copy-start.84
  101.4 57.5 %all-gather.18.cloned.1.call-start = ((), (), s32[]{:S(2)}) async-start(), calls=%async_computation.12 | async-start | bytes 1310720 | tf_op jit(solution)/shard_map/all_gather | solution.py:196
  110.7 79.9 %all-gather.16.cloned.1.call-start = ((), (), s32[]{:S(2)}) async-start(), calls=%async_computation.11 | async-start | bytes 1310720 | tf_op jit(solution)/shard_map/all_gather | solution.py:195
  120.0 98.7 %all-gather.20.cloned.1.call-start = ((), (), s32[]{:S(2)}) async-start(), calls=%async_computation.13 | async-start | bytes 2359296 | tf_op jit(solution)/shard_map/all_gather | solution.py:162
  120.5 130.4 %all-gather.26.cloned.1.call-start = ((), (), s32[]{:S(2)}) async-start(), calls=%async_computation.16 | async-start | bytes 1310720 | tf_op jit(solution)/shard_map/all_gather | solution.py:195
  123.8 127.2 %copy-start.42 = (bf16[128,16,32]{0,2,1:T(8,128)(2,1)}, bf16[128,16,32]{0,2,1:T(8,128)(2,1)S(1)}, u32[]{:S(2)}) copy-start(bf16[128,16,32]{0,2,1:T(8,128)(2,1)S(1)} %get-tuple-element.123) | copy-start | bytes 393220
  123.8 127.2 %copy-start.44 = (bf16[128,16,32]{0,2,1:T(8,128)(2,1)}, bf16[128,16,32]{0,2,1:T(8,128)(2,1)S(1)}, u32[]{:S(2)}) copy-start(bf16[128,16,32]{0,2,1:T(8,128)(2,1)S(1)} %get-tuple-element.124) | copy-start | bytes 393220
  124.6 181.0 %all-gather.22.cloned.1.call-start = ((), (), s32[]{:S(2)}) async-start(), calls=%async_computation.14 | async-start | bytes 9437184 | tf_op jit(solution)/shard_map/all_gather | solution.py:163
  125.4 236.5 %all-gather.24.cloned.1.call-start = ((), (), s32[]{:S(2)}) async-start(), calls=%async_computation.15 | async-start | bytes 9437184 | tf_op jit(solution)/shard_map/all_gather | solution.py:164
  126.1 303.2 %reduce-scatter.32.cloned.1.call-start = ((), (), s32[]{:S(2)}) async-start(), calls=%async_computation.25 | async-start | bytes 1310720
  135.2 58.9 %copy-start.66 = (pred[128,512]{1,0:T(8,128)(4,1)}, pred[128,512]{1,0:T(8,128)(4,1)S(1)}, u32[]{:S(2)}) copy-start(pred[128,512]{1,0:T(8,128)(4,1)S(1)} %broadcast_compare_fusion.1) | copy-start | bytes 196612
  135.3 117.9 %copy-start.68 = (pred[128,512]{1,0:T(8,128)(4,1)}, pred[128,512]{1,0:T(8,128)(4,1)S(1)}, u32[]{:S(2)}) copy-start(pred[128,512]{1,0:T(8,128)(4,1)S(1)} %broadcast_compare_fusion) | copy-start | bytes 196612
  135.3 55.4 %copy-start.40 = (bf16[128,16,32]{0,2,1:T(8,128)(2,1)S(1)}, bf16[128,16,32]{0,2,1:T(8,128)(2,1)}, u32[]{:S(2)}) copy-start(bf16[128,16,32]{0,2,1:T(8,128)(2,1)} %get-tuple-element.120) | copy-start | bytes 393220
  196.9 56.2 %copy-start.54 = (bf16[128,16,64]{0,2,1:T(8,128)(2,1)}, bf16[128,16,64]{0,2,1:T(8,128)(2,1)S(1)}, u32[]{:S(2)}) copy-start(bf16[128,16,64]{0,2,1:T(8,128)(2,1)S(1)} %get-tuple-element.169) | copy-start | bytes 786436
  221.5 31.6 %copy-start.85 = (f32[128]{0:T(128)}, f32[128]{0:T(128)S(1)}, u32[]{:S(2)}) copy-start(f32[128]{0:T(128)S(1)} %get-tuple-element.171) | copy-start | bytes 1540
  305.6 6.3 copy-start
  305.6 6.3 copy-start.7
  305.6 6.3 copy-start.75
  361.9 8.2 copy-start.20
  361.9 8.2 copy-start.38
  361.9 8.2 copy-start.94
  361.9 11.8 %slice-start = ((s8[8388608]{0:T(1024)(128)(4,1)}), s8[4194304]{0:T(1024)(128)(4,1)S(1)}, s32[]{:S(2)}) async-start(s8[8388608]{0:T(1024)(128)(4,1)} %bitcast.155), calls=%async_computation.28 | async-start | bytes 8388608
  370.1 6.6 copy-start.27
  386.7 5.5 copy-start.43
  386.7 5.5 copy-start.45
  395.9 55.5 %reduce-scatter.28.cloned.1.call-start = ((), (), s32[]{:S(2)}) async-start(), calls=%async_computation.23 | async-start | bytes 1310720
  397.5 4.9 copy-start.83
  402.4 5.4 copy-start.41
  409.6 70.4 %reduce-scatter.34.cloned.1.call-start = ((), (), s32[]{:S(2)}) async-start(), calls=%async_computation.26 | async-start | bytes 1310720
  414.3 94.5 %reduce-scatter.30.cloned.1.call-start = ((), (), s32[]{:S(2)}) async-start(), calls=%async_computation.24 | async-start | bytes 1310720
  421.1 157.7 %reduce-scatter.22.cloned.1.call-start = ((), (), s32[]{:S(2)}) async-start(), calls=%async_computation.20 | async-start | bytes 2359296 | tf_op jit(solution)/shard_map/reduce_scatter | solution.py:292
  429.1 177.8 %reduce-scatter.18.cloned.1.call-start = ((), (), s32[]{:S(2)}) async-start(), calls=%async_computation.18 | async-start | bytes 4718592 | tf_op jit(solution)/shard_map/reduce_scatter | solution.py:292
  452.6 66.7 %slice-start.2 = ((s8[6291456]{0:T(1024)(128)(4,1)}), s8[2097152]{0:T(1024)(128)(4,1)S(1)}, s32[]{:S(2)}) async-start(s8[6291456]{0:T(1024)(128)(4,1)} %bitcast.157), calls=%async_computation.30 | async-start | bytes 4194304
  511.5 7.8 copy-start.48
  512.6 6.7 copy-start.59
  513.7 5.6 copy-start.61
  513.8 5.6 slice-start.3
  513.8 5.6 copy-start.56
  513.8 5.6 copy-start.79
  513.8 5.6 copy-start.81
  527.5 144.3 %reduce-scatter.20.cloned.1.call-start = ((), (), s32[]{:S(2)}) async-start(), calls=%async_computation.19 | async-start | bytes 7077888 | tf_op jit(solution)/shard_map/reduce_scatter | solution.py:292
  535.2 211.6 %reduce-scatter.26.cloned.1.call-start = ((), (), s32[]{:S(2)}) async-start(), calls=%async_computation.22 | async-start | bytes 9437184 | tf_op jit(solution)/shard_map/reduce_scatter | solution.py:292
  536.9 8.2 copy-start.21
  554.5 11.9 %copy-start.9 = (f32[128,1024]{1,0:T(8,128)S(1)}, f32[128,1024]{1,0:T(8,128)}, u32[]{:S(2)}) copy-start(f32[128,1024]{1,0:T(8,128)} %get-tuple-element.164) | copy-start | bytes 1572868
  554.5 11.9 %copy-start.77 = (f32[128]{0:T(128)S(1)}, f32[128]{0:T(128)}, u32[]{:S(2)}) copy-start(f32[128]{0:T(128)} %fusion.99) | copy-start | bytes 1540
  554.5 266.9 %reduce-scatter.24.cloned.1.call-start = ((), (), s32[]{:S(2)}) async-start(), calls=%async_computation.21 | async-start | bytes 9437184 | tf_op jit(solution)/shard_map/reduce_scatter | solution.py:292
  555.5 10.9 %copy-start.25 = (bf16[128,4096]{1,0:T(8,128)(2,1)S(1)}, bf16[128,4096]{1,0:T(8,128)(2,1)}, u32[]{:S(2)}) copy-start(bf16[128,4096]{1,0:T(8,128)(2,1)} %copy-done.24) | copy-start | bytes 3145732
  578.7 242.7 %copy-start.95 = (u32[32]{0:T(128)S(1)}, u32[32]{0:T(128)}, u32[]{:S(2)}) copy-start(u32[32]{0:T(128)} %constant.99) | copy-start | bytes 388
  578.8 385.4 %all-reduce.7.cloned.1.call-start = ((), (), s32[]{:S(2)}) async-start(), calls=%async_computation.27 | async-start | bytes 7340032 | tf_op jit(solution)/shard_map/psum | solution.py:294
  822.7 5.1 copy-start.22
  827.8 6.6 copy-start.73
  827.8 6.6 copy-start.74
  827.8 33.3 %copy-start.37 = (bf16[128,1024]{1,0:T(8,128)(2,1)S(1)}, bf16[128,1024]{1,0:T(8,128)(2,1)}, u32[]{:S(2)}) copy-start(bf16[128,1024]{1,0:T(8,128)(2,1)} %copy-done.36) | copy-start | bytes 786436
  861.2 4.0 copy-start.1
  964.1 4.1 copy-start.65
  964.1 5.4 copy-start.53
  (55 other events, 113.9 us)
Sparse Core Ops, SparseCore 0:
  9.9 39.4 all-gather.11
  51.2 45.5 all-gather.13
  101.5 27.9 all-gather.27
  131.5 27.4 all-gather.17
  160.9 29.6 all-gather.15
  192.4 26.1 all-gather.19
  220.8 30.1 all-gather.25
  252.9 52.6 all-gather.21
  307.5 54.3 all-gather.23
  396.1 27.1 reduce-scatter.31
  425.6 25.7 reduce-scatter.27
  454.2 25.7 reduce-scatter.33
  483.0 25.8 reduce-scatter.29
  512.0 39.8 reduce-scatter.21
  555.4 51.3 reduce-scatter.17
  610.1 61.7 reduce-scatter.19
  675.5 71.2 reduce-scatter.25
  750.1 71.2 reduce-scatter.23
  824.4 139.6 all-reduce.6
where the time goes:
time: 986 us; the launch traced here: 980 us
  waiting for transfers between devices  676 us (69%)
  matrix products  159 us (16%)
  local copies, waits for them, and re-layouts  45.4 us (5%)
  blocking collectives  44.6 us (5%)
  other arithmetic  36.4 us (4%)
  between operations  16.6 us (2%)
    reduce_scatter x5, waiting for transfers between devices, local(): lax.psum_scatter(shortened(sums), 'fsdp', scatter_dimension=0, tiled=True)  243 us
    psum x1, waiting for transfers between devices, local(): lax.psum(shortened(owned), 'blk')  94.4 us
    unnamed x23, waiting for transfers between devices  73.2 us
    all_gather x2, waiting for transfers between devices, local(): lax.all_gather(key_flat, 'blk', axis=0, tiled=True)  58.2 us
    all_gather x1, waiting for transfers between devices, local(): lax.all_gather(shards[4], 'fsdp', axis=0, tiled=True)  47.3 us
    all_gather x1, waiting for transfers between devices, local(): lax.all_gather(shards[1], 'fsdp', axis=0, tiled=True)  44.4 us
    all_gather x1, waiting for transfers between devices, local(): lax.all_gather(shards[3], 'fsdp', axis=0, tiled=True)  43.8 us
    all_gather x1, waiting for transfers between devices, local(): lax.all_gather(shards[0], 'fsdp', axis=0, tiled=True)  29 us
  transfers between devices with their start and end apart: 19, of which 16 were waited for; matrix products, arithmetic and copies ran while one was open for 19% of the time, Pallas kernels for 0%

commit v1 on v0

v1 whole, which is shorter than its diff:
```python
import functools
import itertools

import jax
import jax.numpy as jnp
from jax import lax
from jax.experimental import pallas as pl
from jax.experimental.pallas import tpu as pltpu
from jax.sharding import PartitionSpec as P

D = 1024
HEADS = 16
HEAD_DIM = 64
MB = 2
PAIR = 2 * HEAD_DIM
CHIPS = 4
INDEX = 8
NEG_BIG = -1e30
EPS = 1e-6
AXES = ("fsdp", "blk")
BF = jnp.bfloat16
F32 = jnp.float32
MEGA = 1024 * 1024
SMALL, LARGE, HUGE = 20 * MEGA, 30 * MEGA, 60 * MEGA

MERGE_ROWS = 256
OWN_ROWS = 128
HIDDEN_ROWS = 512
GAIN_ROWS = 16


def dot(left, right):
    return jnp.dot(left, right, preferred_element_type=F32)


def dot_rows(left, right):
    return lax.dot_general(left, right, (((0,), (0,)), ((), ())), preferred_element_type=F32)


def dot_cols(left, right):
    return lax.dot_general(left, right, (((1,), (1,)), ((), ())), preferred_element_type=F32)


def norm_scale(hidden):
    return lax.rsqrt(jnp.mean(hidden * hidden, -1, keepdims=True) + EPS)


def norm_back(grad, hidden, gain):
    scale = norm_scale(hidden)
    weighted = grad * gain
    inner = jnp.mean(weighted * hidden, -1, keepdims=True)
    back = scale * weighted - hidden * (scale * scale * scale * inner)
    gain_grad = jnp.sum(grad * hidden * scale, 0, keepdims=True)
    return back, gain_grad


def swap_halves(tensor):
    lane = lax.broadcasted_iota(jnp.int32, tensor.shape, 1)
    low = (lane % HEAD_DIM) < HEAD_DIM // 2
    return jnp.where(
        low,
        pltpu.roll(tensor, PAIR - HEAD_DIM // 2, 1),
        pltpu.roll(tensor, HEAD_DIM // 2, 1),
    )


def turn(tensor, cosine, sine):
    return tensor * cosine + swap_halves(tensor) * sine


def aligned(at, size):
    return pl.ds(pl.multiple_of(at * size, size), size)


def stacked(parts):
    return jnp.concatenate([part[...] for part in parts], 0)


def summed(parts):
    return functools.reduce(jnp.add, [part[...].astype(F32) for part in parts])


def owner_of(index, chip, other):
    return 2 * index[chip] + (1 - index[4] if other else index[4])


def merge_kernel(index, left, right, *refs):
    weights = refs[: 2 * CHIPS]
    hidden_ref, cot_ref, pre_ref, mid_ref = refs[2 * CHIPS :]
    rows = left.shape[0]
    total = None
    for at, weight in enumerate(weights):
        mine = aligned(owner_of(index, at % CHIPS, at >= CHIPS), MERGE_ROWS)
        part = dot(jnp.concatenate([left[:, mine], right[:, mine]], 0), weight[:MERGE_ROWS])
        total = part if total is None else total + part
        mine = aligned(owner_of(index, at % CHIPS, at >= CHIPS), OWN_ROWS)
        gains = weight[MERGE_ROWS:, :OWN_ROWS].astype(F32)
        pre_ref[:, mine] = gains[0:1]
        mid_ref[:, mine] = gains[1:2]
    hidden_ref[...] = total
    cot_ref[:rows] = left[:, 2 * D :]
    cot_ref[rows:] = right[:, 2 * D :]


def project_kernel(
    index, hidden, gain, w_query, w_key, w_value, cosine, sine, act, query_ref, key_ref, value_ref
):
    @pl.when(pl.program_id(0) == 0)
    def _():
        act[...] = (hidden[...] * norm_scale(hidden[...]) * gain[...]).astype(BF)

    joint = lambda weight: dot(act[...], weight[...].reshape(D, weight.shape[2]))
    query = joint(w_query)
    key = joint(w_key)
    value_ref[...] = joint(w_value).astype(BF)
    for block in range(query_ref.shape[1] // PAIR):
        cols = slice(block * PAIR, (block + 1) * PAIR)
        turned = turn(query[:, cols], cosine[...], sine[...]).astype(BF)
        query_ref[:, cols] = turned * HEAD_DIM ** (-0.5)
        key_ref[:, cols] = turn(key[:, cols], cosine[...], sine[...]).astype(BF)


def head_mask(shape, head):
    lane = lax.broadcasted_iota(jnp.int32, shape, 1)
    return (lane // HEAD_DIM) == head


def attend_kernel(pieces, index, *refs):
    query, query_seg, key_segs = refs[:3]
    keys = refs[3 : 3 + pieces]
    values = refs[3 + pieces : 3 + 2 * pieces]
    weight, hidden_zero, gain = refs[3 + 2 * pieces : 6 + 2 * pieces]
    attended_ref, hidden_ref, act_ref, probs_ref = refs[6 + 2 * pieces :]
    allowed = [key_segs[piece] == query_seg[...] for piece in range(pieces)]
    step = pl.program_id(0)
    wide = query.shape[1]
    for block in range(wide // PAIR):
        cols = slice(block * PAIR, (block + 1) * PAIR)
        query_block = query[:, cols]
        key_blocks = [key[:, cols] for key in keys]
        value_blocks = [value[:, cols] for value in values]
        mixed = None
        for head in range(2):
            mask = head_mask(query_block.shape, head)
            one_query = jnp.where(mask, query_block, jnp.zeros_like(query_block))
            scores = [
                jnp.where(a, dot_cols(key, one_query), NEG_BIG)
                for key, a in zip(key_blocks, allowed)
            ]
            peak = functools.reduce(jnp.maximum, [jnp.max(s, 0, keepdims=True) for s in scores])
            expo = [jnp.exp(s - peak) for s in scores]
            inverse = 1.0 / functools.reduce(jnp.add, [jnp.sum(e, 0, keepdims=True) for e in expo])
            for piece in range(pieces):
                probs = (expo[piece] * inverse).astype(BF)
                probs_ref[2 * block + head, piece] = probs
                value = value_blocks[piece]
                part = dot_rows(jnp.where(mask, value, jnp.zeros_like(value)), probs)
                mixed = part if mixed is None else mixed + part
        attended_ref[:, aligned(step * (wide // PAIR) + block, PAIR)] = mixed.T.astype(BF)

    @pl.when(step == pl.num_programs(0) - 1)
    def _():
        hidden = hidden_zero[...] + dot(attended_ref[...], weight[...].reshape(D, D))
        hidden_ref[...] = hidden
        act_ref[...] = (hidden * norm_scale(hidden) * gain[...]).astype(BF)


GELU_ROOT = 0.7978845608028654
GELU_CUBE = 0.044715


def feed_kernel(index, act, cot, w_up, w_down, second_ref, activ_ref, upper_ref):
    cut = 256
    for at in range(w_up.shape[1] // cut):
        cols = slice(at * cut, (at + 1) * cut)
        upper = dot(act[...], w_up[:, cols])
        square = upper * upper
        bent = jnp.tanh(GELU_ROOT * upper * (1.0 + GELU_CUBE * square))
        half = 0.5 * (1.0 + bent)
        activ_ref[:, cols] = (upper * half).astype(BF)
        slope = half + 0.5 * upper * (1.0 - bent * bent) * (
            GELU_ROOT * (1.0 + 3.0 * GELU_CUBE * square)
        )
        upper_ref[:, cols] = (dot_cols(cot[...], w_down[cols, :]) * slope).astype(BF)
    second_ref[...] = dot_cols(upper_ref[...], w_up[...]).astype(BF)


def result_parts_kernel(index, own, other, w_down, own_ref, other_ref):
    own_ref[...] = dot(own[...], w_down[...]).astype(BF)
    other_ref[...] = dot(other[...], w_down[...]).astype(BF)


def down_grad_kernel(index, activ, activ_x, cot, cot_x, keep_ref, send_ref):
    core = index[4]
    step = pl.program_id(0)
    down = dot_rows(stacked((activ, activ_x)), stacked((cot, cot_x))).astype(BF)

    @pl.when(step % 2 == core)
    def _():
        keep_ref[0] = down

    @pl.when(step % 2 != core)
    def _():
        send_ref[0] = down


def up_grad_kernel(index, act, act_x, upper, upper_x, keep_ref, send_ref, total):
    core = index[4]
    column = pl.program_id(0) % 2
    total[...] = dot_rows(stacked((act, act_x)), stacked((upper, upper_x)))
    for ref, half in ((keep_ref, core), (send_ref, 1 - core)):
        mine = aligned(half, OWN_ROWS)
        for side in range(2):
            ref[0, column, side] = total[mine, side * D : (side + 1) * D].astype(BF)


def up_chip_kernel(index, own, got, own_ref, send_ref):
    for column, ref in enumerate((own_ref, send_ref)):
        for side in range(2):
            ref[side] = summed((own.at[column, side], got.at[column, 1 - side])).astype(BF)


def feed_total_kernel(index, down, up, reducer_ref, expander_ref):
    reducer_ref[...] = down[...].astype(F32)
    for column in range(2):
        for side in range(2):
            expander_ref[:, aligned(index[column + 2 * side], D)] = up[column, side].astype(F32)


def feed_send_kernel(index, expander, reducer, own_ref, send_ref, reducer_ref):
    reducer_ref[...] = reducer[...]
    for side in range(2):
        own_ref[side] = expander[:, aligned(index[2 * side], D)]
        send_ref[side] = expander[:, aligned(index[1 + 2 * side], D)]


def up_kernel(index, own, own_y, other, other_y, out_ref):
    for core, parts in enumerate(((own, own_y), (other, other_y))):
        here = 1 - index[4] if core else index[4]
        for row, part in enumerate(parts):
            for column in range(2):
                owner = 2 * index[column + 2 * row] + here
                for side in range(2):
                    cols = slice(side * D, (side + 1) * D)
                    out_ref[owner, :, cols] = part[column, side if row == 0 else 1 - side]


def down_kernel(index, own, own_y, other, other_y, out_ref):
    for side, (mine, theirs) in enumerate(((own, other), (own_y, other_y))):
        out_ref[2 * side + index[4]] = mine[...]
        out_ref[2 * side + 1 - index[4]] = theirs[...]


def attend_back_kernel(pieces, index, *refs):
    query, probs_ref = refs[:2]
    keys = refs[2 : 2 + pieces]
    values = refs[2 + pieces : 2 + 2 * pieces]
    at = 2 + 2 * pieces
    weight, hidden_one, cot, gain, cosine, sine = refs[at : at + 6]
    seconds = refs[at + 6 : at + 8]
    at += 8
    one_ref, low_ref, gain_ref, query_ref = refs[at : at + 4]
    pair_refs = refs[at + 4 : at + 4 + pieces]
    swap_ref = pair_refs[1]
    step = pl.program_id(0)

    @pl.when(step == 0)
    def _():
        back, gain_grad = norm_back(summed(seconds), hidden_one[...], gain[...])
        one = cot[...].astype(F32) + back
        one_ref[...] = one
        gain_ref[...] = gain_grad
        low_ref[...] = one.astype(BF)

    wide = query.shape[1]
    swap_ref[3] = low_ref[:, aligned(step, wide)]
    attended_grad = dot_cols(low_ref[...], weight[...].reshape(wide, D)).astype(BF)
    for block in range(wide // PAIR):
        cols = slice(block * PAIR, (block + 1) * PAIR)
        query_block = query[:, cols]
        grad_block = attended_grad[:, cols]
        key_blocks = [key[:, cols] for key in keys]
        value_blocks = [value[:, cols] for value in values]
        query_grad = None
        key_grads = [None] * pieces
        value_grads = [None] * pieces
        for head in range(2):
            mask = head_mask(query_block.shape, head)
            one_query = jnp.where(mask, query_block, jnp.zeros_like(query_block))
            one_grad = jnp.where(mask, grad_block, jnp.zeros_like(grad_block))
            low = [probs_ref[2 * block + head, piece] for piece in range(pieces)]
            probs = [p.astype(F32) for p in low]
            probs_grad = [dot_cols(value, one_grad) for value in value_blocks]
            delta = functools.reduce(
                jnp.add,
                [jnp.sum(p * g, 0, keepdims=True) for p, g in zip(probs, probs_grad)],
            )
            for piece in range(pieces):
                scores_grad = (probs[piece] * (probs_grad[piece] - delta)).astype(BF)
                key = key_blocks[piece]
                part = dot_rows(jnp.where(mask, key, jnp.zeros_like(key)), scores_grad)
                query_grad = part if query_grad is None else query_grad + part
                key_part = dot(scores_grad, one_query)
                value_part = dot(low[piece], one_grad)
                if head:
                    key_part += key_grads[piece]
                    value_part += value_grads[piece]
                key_grads[piece] = key_part
                value_grads[piece] = value_part
        query_grad = query_grad.T * HEAD_DIM ** (-0.5)
        query_grad = turn(query_grad, cosine[0], -sine[0]).astype(BF)
        query_ref[:, cols] = query_grad
        swap_ref[2, :, cols] = query_grad
        for piece in range(pieces):
            turned = turn(key_grads[piece], cosine[piece], -sine[piece])
            pair_refs[piece][0, :, cols] = turned.astype(BF)
            pair_refs[piece][1, :, cols] = value_grads[piece].astype(BF)


def united_kernel(pieces, index, *refs):
    query_grad, mid = refs[:2]
    pairs = refs[2 : 2 + pieces]
    at = 2 + pieces
    w_query, w_key, w_value, hidden_zero, one_grad, gain = refs[at : at + 6]
    swap_ref, left_ref, right_ref, first = refs[at + 6 :]
    step = pl.program_id(0)
    tok = query_grad.shape[0]
    place = lambda which: slice(which * tok, (which + 1) * tok)

    @pl.when(step == 0)
    def _():
        for which in range(2):
            total = functools.reduce(jnp.add, [part[which].astype(F32) for part in pairs])
            swap_ref[place(which)] = total.astype(BF)

    grads = (query_grad[...], swap_ref[place(0)], swap_ref[place(1)])
    first[step] = functools.reduce(
        jnp.add,
        [
            dot_cols(grad, weight[...].reshape(2 * OWN_ROWS, D))
            for grad, weight in zip(grads, (w_query, w_key, w_value))
        ],
    )

    @pl.when(step == CHIPS - 1)
    def _():
        grad = jnp.concatenate([first[chip] for chip in range(CHIPS)], 1)
        back, gain_grad = norm_back(grad, hidden_zero[...], gain[...])
        low = (one_grad[...] + back).astype(BF)
        swap_ref[place(2)] = low
        left_ref[...] = low[: tok // 2]
        right_ref[...] = low[tok // 2 :]
        rest = jnp.zeros((GAIN_ROWS - 2, D), F32)
        swap_ref[3 * tok :] = jnp.concatenate([gain_grad, mid[...], rest], 0).astype(BF)


def of_core(ref, index, size):
    return jnp.concatenate(
        [ref[:, aligned(2 * index[chip] + index[4], size)] for chip in range(CHIPS)], 1
    )


def put_slabs(total, rows, at, order, keep_ref, send_ref):
    for ref, chips in ((keep_ref, order[:2]), (send_ref, order[2:])):
        for place, chip in enumerate(chips):
            ref[place, at : at + rows] = total[chip * rows : (chip + 1) * rows].astype(BF)


X_FIRST = (0, 2, 1, 3)
Y_FIRST = (0, 1, 2, 3)


def query_grad_kernel(
    index, act, act_c, attended, attended_c, grad, low, swapped, keep_ref, send_ref
):
    lefts = ((act, act_c), (attended, attended_c))
    rights = ((grad[...], swapped[2]), (low[...], swapped[3]))
    for which, (left, right) in enumerate(zip(lefts, rights)):
        both = jnp.concatenate([of_core(part, index, OWN_ROWS) for part in left], 0)
        total = dot_rows(both, jnp.concatenate(right, 0))
        put_slabs(total, OWN_ROWS, which * OWN_ROWS, X_FIRST, keep_ref, send_ref)


def pair_grad_kernel(index, act, act_c, own, swapped, keep_ref, send_ref):
    tok = act.shape[0]
    both = jnp.concatenate([of_core(part, index, OWN_ROWS) for part in (act, act_c)], 0)
    for which in range(2):
        place = slice(which * tok, (which + 1) * tok)
        total = dot_rows(both, jnp.concatenate([own[place], swapped[place]], 0))
        put_slabs(total, OWN_ROWS, which * OWN_ROWS, Y_FIRST, keep_ref, send_ref)


def merge_grad_kernel(index, left, right, left_c, right_c, own, swapped, keep_ref, send_ref):
    tok = 2 * left.shape[0]
    both = jnp.concatenate(
        [of_core(part, index, MERGE_ROWS) for part in (left, right, left_c, right_c)], 0
    )
    low = slice(2 * tok, 3 * tok)
    total = dot_rows(both, jnp.concatenate([own[low], swapped[low]], 0))
    put_slabs(total, MERGE_ROWS, 0, X_FIRST, keep_ref, send_ref)
    gains = own[3 * tok :].astype(F32) + swapped[3 * tok :].astype(F32)
    keep_ref[:, MERGE_ROWS:] = jnp.zeros((2, GAIN_ROWS, D), BF)
    send_ref[:, MERGE_ROWS:] = jnp.zeros((2, GAIN_ROWS, D), BF)
    for ref, chips in ((keep_ref, X_FIRST[:2]), (send_ref, X_FIRST[2:])):
        for place, chip in enumerate(chips):
            owner = 2 * index[chip] + index[4]
            lane = lax.broadcasted_iota(jnp.int32, gains.shape, 1)
            mine = jnp.where(lane // OWN_ROWS == owner, gains, 0.0)
            chosen = functools.reduce(
                jnp.add,
                [mine[:, at * OWN_ROWS : (at + 1) * OWN_ROWS] for at in range(D // OWN_ROWS)],
            )
            ref[place, MERGE_ROWS:, :OWN_ROWS] = chosen.astype(BF)


def joined_grad_kernel(index, first, second, *refs):
    weights = refs[: 2 * CHIPS]
    rows = first.shape[0]
    low = jnp.concatenate([first[...], second[...]], 0)
    micro = index[5]
    for at, weight in enumerate(weights):
        grad = dot_cols(low, weight[:MERGE_ROWS])
        owner = owner_of(index, at % CHIPS, at >= CHIPS)
        cols = aligned(owner % CHIPS, MERGE_ROWS)
        for half, out_ref in enumerate(refs[2 * CHIPS :]):

            @pl.when(owner // CHIPS == half)
            def _():
                out_ref[micro, :, cols] = grad[:rows]
                out_ref[1 - micro, :, cols] = grad[rows:]


def add_kernel(index, *refs):
    refs[-1][...] = summed(refs[:-1]).astype(BF)


def add_two_kernel(index, keep, got, own_ref, other_ref):
    own_ref[...] = summed((keep.at[0], got.at[0])).astype(BF)
    other_ref[...] = summed((keep.at[1], got.at[1])).astype(BF)


def stack_kernel(index, *refs):
    for at, part in enumerate(refs[:-1]):
        refs[-1][at] = part[...]


def result_kernel(index, *refs):
    left, right = refs[-2:]
    rows = left.shape[0]
    total = summed(refs[:-2])
    left[...] = total[:rows].astype(BF)
    right[...] = total[rows:].astype(BF)


def by_micro_kernel(index, first, second, out_ref):
    out_ref[index[5]] = first[...]
    out_ref[1 - index[5]] = second[...]


def chosen(index, array, got, ends):
    here = functools.reduce(jnp.logical_or, [index[6] == end for end in ends])
    return jnp.where(here, got[...], array[...])


def choose_kernel(ends, index, array, got, out_ref):
    out_ref[...] = chosen(index, array, got, ends)


def query_total_kernel(ends, index, array, got, query_ref, combiner_ref):
    total = chosen(index, array, got, ends).astype(F32)
    query_ref[...] = total[:OWN_ROWS]
    combiner_ref[...] = total[OWN_ROWS:]


def pair_total_kernel(ends, index, array, got, query, out_ref):
    total = chosen(index, array, got, ends).astype(F32)
    out_ref[:, :D] = query[...]
    out_ref[:, D : 2 * D] = total[:OWN_ROWS]
    out_ref[:, 2 * D :] = total[OWN_ROWS:]


def merge_total_kernel(ends, index, array, got, out_ref, gain_ref):
    total = chosen(index, array, got, ends).astype(F32)
    out_ref[...] = total[:MERGE_ROWS]
    gain_ref[...] = total[MERGE_ROWS : MERGE_ROWS + 8, :OWN_ROWS]


def call(kernel, vmem, grid, in_specs, out_specs, out_shape, scratch, index, *arrays):
    def passing(index_ref, *refs):
        inputs = len(in_specs)
        for at in range(INDEX):
            refs[inputs][at] = index_ref[at]
        kernel(index_ref, *refs[:inputs], *refs[inputs + 1 :])

    return pl.pallas_call(
        passing,
        grid_spec=pltpu.PrefetchScalarGridSpec(
            num_scalar_prefetch=1,
            grid=(grid,),
            in_specs=in_specs,
            out_specs=[pl.BlockSpec(memory_space=pltpu.SMEM)] + out_specs,
            scratch_shapes=scratch,
        ),
        out_shape=[jax.ShapeDtypeStruct((INDEX,), jnp.int32)] + out_shape,
        name=getattr(kernel, "func", kernel).__name__,
        compiler_params=pltpu.CompilerParams(
            dimension_semantics=("arbitrary",), vmem_limit_bytes=vmem
        ),
        cost_estimate=pl.CostEstimate(flops=10**12, bytes_accessed=0, transcendentals=0),
    )(index, *arrays)


def shape(*dims, dtype=BF):
    return jax.ShapeDtypeStruct(dims, dtype)


def whole(*dims):
    return pl.BlockSpec(dims, lambda *_: (0,) * len(dims))


def local(
    frames,
    skipped,
    lengths,
    merger,
    projector,
    combiner,
    expander,
    reducer,
    prenorm,
    midnorm,
    cotangent,
):
    rows = frames.shape[1]
    tok = 2 * rows
    blocks = lax.axis_size("blk")
    fsdp = lax.axis_size("fsdp")
    quarter = blocks // 4
    pieces = blocks // 2
    stream = rows * blocks

    me = lax.axis_index("fsdp")
    spot = lax.axis_index("blk")
    core = me % 2
    chip = me // 2
    unit = spot // quarter
    micro = unit // 2
    source_core = unit % 2
    half = (spot % quarter) * 2 + core

    def send(array, route, name="send"):
        pairs = []
        for y, x, c, b in itertools.product(range(2), range(2), range(2), range(blocks)):
            target = route(y, x, c, b)
            if target is not None:
                ty, tx, tc, tb = target
                pairs.append((((y * 2 + x) * 2 + c) * blocks + b, ((ty * 2 + tx) * 2 + tc) * blocks + tb))
        with jax.named_scope(name):
            return lax.ppermute(array, AXES, pairs)

    to_x = lambda y, x, c, b: (y, 1 - x, c, b)
    to_y = lambda y, x, c, b: (1 - y, x, c, b)
    to_diagonal = lambda y, x, c, b: (1 - y, 1 - x, c, b)
    to_core = lambda y, x, c, b: (y, x, 1 - c, b)
    around = (to_x, to_y, to_diagonal)

    def holder(micro_at, c, pair):
        return (2 * micro_at + c) * quarter + pair // 2, pair % 2

    def inward(other):
        def route(y, x, c, b):
            tb, tc = holder((b + other) % 2, c, b // 2)
            return (y, x, tc, tb)

        return route

    def outward(other):
        forward = inward(other)
        table = {}
        for y, x, c, b in itertools.product(range(2), range(2), range(2), range(blocks)):
            table[forward(y, x, c, b)] = (y, x, c, b)
        return lambda *at: table[at]

    def among(by):
        def route(y, x, c, b):
            at = ((b % quarter) * 2 + c) ^ by
            return (y, x, at % 2, (b // quarter) * quarter + at // 2)

        return route

    def take_in(pick, name):
        return tuple(send(pick((spot + other) % 2), inward(other), name) for other in range(2))

    def sum_blocks(array, name, last):
        middle = blocks // 2
        plans = [{step: step + 1, blocks - 1 - step: blocks - 2 - step} for step in range(middle - 1)]
        plans.append({middle - 1: middle, middle: middle - 1})
        for moves in plans:
            got = send(array, lambda y, x, c, b: (y, x, c, moves[b]) if b in moves else None, name)
            yield
            array = add(array, got)
        for step in range(middle - 1):
            moves = {middle - 1 - step: middle - 2 - step, middle + step: middle + 1 + step}
            got = send(array, lambda y, x, c, b: (y, x, c, moves[b]) if b in moves else None, name)
            yield
            ends = tuple(moves.values())
            if step == middle - 2:
                array = last(ends, array, got)
            else:
                choose = functools.partial(choose_kernel, ends)
                array = simple(choose, [shape(*array.shape)], array, got)
        yield array

    def finish(steps):
        array = None
        while array is None:
            array = next(steps)
        return array

    gathered = lax.all_gather(jnp.concatenate([projector, combiner], 1), "fsdp", axis=0)

    gain_rows = jnp.pad(jnp.stack([prenorm, midnorm]), ((0, GAIN_ROWS - 2), (0, D - OWN_ROWS)))
    merger_own = jnp.concatenate([merger, gain_rows], 0)
    mergers = [merger_own] + [send(merger_own, route, "merger_around") for route in around]
    mergers += [send(part, to_core, "merger_core") for part in mergers]

    left, right = take_in(
        lambda m: jnp.concatenate([frames[m], skipped[m], cotangent[m]], -1), "tokens_in"
    )
    other_lengths = send(lengths, to_core, "lengths_core")
    half_chunk = expander.shape[1] // 2

    mine = jnp.where(source_core == core, lengths, other_lengths)[:, 0]
    row_lengths = jnp.where(micro == 0, mine[0], mine[1])
    ends = jnp.cumsum(row_lengths)
    within = jnp.arange(rows, dtype=jnp.int32)

    def layout(at):
        offsets = jnp.concatenate(
            [(2 * at + micro) * rows + within, (2 * at + 1 - micro) * rows + within]
        )
        before = (ends[None, :] <= offsets[:, None]).astype(jnp.int32)
        return jnp.sum(before, 1), offsets - jnp.sum(before * row_lengths[None, :], 1)

    layouts = [layout(half ^ by) for by in range(pieces)]
    query_seg = layouts[0][0][None]
    key_segs = jnp.stack([segment for segment, _ in layouts])[:, :, None]
    inverse = 10000.0 ** (-jnp.arange(HEAD_DIM // 2, dtype=F32) * 2.0 / HEAD_DIM)
    positions = jnp.stack([position for _, position in layouts]).astype(F32)
    angles = positions[:, :, None] * inverse
    cosine = jnp.tile(jnp.cos(angles), (1, 1, 4))
    sine = jnp.sin(angles)
    sine = jnp.concatenate([-sine, sine, -sine, sine], -1)

    index = jnp.stack(
        [chip, chip ^ 1, chip ^ 2, chip ^ 3, core, spot % 2, spot, spot]
    ).astype(jnp.int32)
    last_index = [index]

    def run(kernel, grid, in_specs, out_specs, out_shape, scratch, *arrays, vmem=SMALL):
        last_index[0], *results = call(
            kernel, vmem, grid, in_specs, out_specs, out_shape, scratch, last_index[0], *arrays
        )
        return results[0] if len(results) == 1 else results

    def simple(kernel, outs, *arrays):
        return run(
            kernel,
            1,
            [whole(*array.shape) for array in arrays],
            [whole(*out.shape) for out in outs],
            outs,
            [],
            *arrays,
        )

    def to_total(kernel, outs):
        return lambda ends, array, got: simple(functools.partial(kernel, ends), outs, array, got)

    def add(*arrays):
        return simple(add_kernel, [shape(*arrays[0].shape)], *arrays)

    def first_step(keep, got):
        return simple(add_two_kernel, [shape(*keep.shape[1:])] * 2, keep, got)

    wide = 2 * OWN_ROWS
    cols_at = lambda height, width: pl.BlockSpec((height, width), lambda s, i: (0, s))
    cols_of = lambda height, width: pl.BlockSpec((height, width), lambda s, i: (0, i[s]))
    slab_at = lambda at: pl.BlockSpec((2, OWN_ROWS, D), lambda s, i: (s, 0, at))
    column_at = lambda at: pl.BlockSpec(
        (fsdp, OWN_ROWS, wide), lambda s, i: (0, 0, at * (D // wide) + s)
    )
    table = whole(tok, PAIR)
    tables = whole(pieces, tok, PAIR)
    own_cols = cols_at(tok, wide)

    hidden_zero, cot, gain_pre, gain_mid = simple(
        merge_kernel,
        [shape(tok, D, dtype=F32), shape(tok, D)] + [shape(1, D, dtype=F32)] * 2,
        left,
        right,
        *mergers,
    )
    cot_x = send(cot, to_x, "cot_x")

    up_own, up_send, down_own = simple(
        feed_send_kernel,
        [shape(2, OWN_ROWS, D), shape(2, OWN_ROWS, D), shape(*reducer.shape)],
        expander,
        reducer,
    )
    up_x = send(up_send, to_x, "w_up_x")
    down_y = send(down_own, to_y, "w_down_y")
    down_c = send(down_own, to_core, "w_down_core")
    act_first, query, key, value = run(
        project_kernel,
        CHIPS,
        [whole(tok, D), whole(1, D)] + [column_at(at) for at in range(3)] + [table, table],
        [whole(tok, D)] + [own_cols] * 3,
        [shape(tok, D)] * 4,
        [],
        hidden_zero,
        gain_pre,
        gathered,
        gathered,
        gathered,
        cosine[0],
        sine[0],
        vmem=LARGE,
    )
    up_pair = jnp.stack([up_own, up_x])
    up_y = send(up_pair, to_y, "w_up_y")
    up_c = send(up_pair, to_core, "w_up_core")
    keys = [key] + [send(key, among(by), "keys_core") for by in range(1, pieces)]
    values = [value] + [send(value, among(by), "values_core") for by in range(1, pieces)]
    act_first_c = send(act_first, to_core, "act_core")
    left_c = send(left, to_core, "joined_core")
    right_c = send(right, to_core, "joined_core")
    steps, vmem = (1, LARGE) if pieces == 2 else (CHIPS * 2, HUGE)
    head_cols = cols_at(tok, D // steps)
    probs_spec = pl.BlockSpec((HEADS // steps, pieces, tok, tok), lambda s, i: (s, 0, 0, 0))
    attended, hidden_one, act_second, probs = run(
        functools.partial(attend_kernel, pieces),
        steps,
        [head_cols, whole(1, tok), whole(pieces, tok, 1)]
        + [head_cols] * (2 * pieces)
        + [pl.BlockSpec((fsdp, OWN_ROWS, D), lambda s, i: (0, 0, 3)), whole(tok, D), whole(1, D)],
        [whole(tok, D), whole(tok, D), whole(tok, D), probs_spec],
        [
            shape(tok, D),
            shape(tok, D, dtype=F32),
            shape(tok, D),
            shape(HEADS, pieces, tok, tok),
        ],
        [],
        query,
        query_seg,
        key_segs,
        *keys,
        *values,
        gathered,
        hidden_zero,
        gain_mid,
        vmem=vmem,
    )
    attended_c = send(attended, to_core, "attended_core")

    down_yc = send(down_y, to_core, "w_down_core")
    w_down = simple(
        down_kernel, [shape(4, HIDDEN_ROWS, D)], reducer, down_y, down_c, down_yc
    ).reshape(half_chunk, D)

    act_x = send(act_second, to_x, "act_x")
    up_yc = send(up_y, to_core, "w_up_core")
    w_up = simple(
        up_kernel, [shape(fsdp, OWN_ROWS, half_chunk)], up_pair, up_y, up_c, up_yc
    ).reshape(D, half_chunk)

    def feed(act, grad):
        return simple(
            feed_kernel,
            [shape(tok, D), shape(tok, half_chunk), shape(tok, half_chunk)],
            act,
            grad,
            w_up,
            w_down,
        )

    second, activ, upper = feed(act_second, cot)
    second_x, activ_x, upper_x = feed(act_x, cot_x)
    second_got = send(second_x, to_x, "second_x")
    many_cols = cols_at(tok, half_chunk // CHIPS)
    near_cols = cols_of(tok, wide)
    down_half = pl.BlockSpec((1, HIDDEN_ROWS, D), lambda s, i: (s // 2, 0, 0))
    down_keep, down_send = run(
        down_grad_kernel,
        CHIPS,
        [many_cols, many_cols, whole(tok, D), whole(tok, D)],
        [down_half, down_half],
        [shape(2, HIDDEN_ROWS, D)] * 2,
        [],
        activ,
        activ_x,
        cot,
        cot_x,
    )
    down_got = send(down_send, to_core, "down_core")
    up_half = pl.BlockSpec((1, 2, 2, OWN_ROWS, D), lambda s, i: (s // 2, 0, 0, 0, 0))
    up_keep, up_send = run(
        up_grad_kernel,
        CHIPS,
        [near_cols, near_cols, whole(tok, half_chunk), whole(tok, half_chunk)],
        [up_half, up_half],
        [shape(2, 2, 2, OWN_ROWS, D)] * 2,
        [pltpu.VMEM((wide, half_chunk), F32)],
        act_second,
        act_x,
        upper,
        upper_x,
    )
    up_got = send(up_send, to_core, "up_core")
    down_one, down_two = first_step(down_keep, down_got)
    down_y = send(down_two, to_y, "down_y")

    steps = CHIPS if pieces == 2 else 2 * CHIPS
    head_cols = cols_at(tok, D // steps)
    probs_spec = pl.BlockSpec((HEADS // steps, pieces, tok, tok), lambda s, i: (s, 0, 0, 0))
    pair_cols = lambda count: pl.BlockSpec((count, tok, D // steps), lambda s, i: (0, 0, s))
    counts = [4 if by == 1 else 2 for by in range(pieces)]
    back = run(
        functools.partial(attend_back_kernel, pieces),
        steps,
        [head_cols, probs_spec]
        + [head_cols] * (2 * pieces)
        + [pl.BlockSpec((fsdp // steps, OWN_ROWS, D), lambda s, i: (s, 0, 3))]
        + [whole(tok, D), whole(tok, D), whole(1, D)]
        + [tables, tables]
        + [whole(tok, D)] * 2,
        [whole(tok, D), whole(tok, D), whole(1, D), head_cols] + [pair_cols(n) for n in counts],
        [
            shape(tok, D, dtype=F32),
            shape(tok, D),
            shape(1, D, dtype=F32),
            shape(tok, D),
        ]
        + [shape(n, tok, D) for n in counts],
        [],
        query,
        probs,
        *keys,
        *values,
        gathered,
        hidden_one,
        cot,
        gain_mid,
        cosine,
        sine,
        second,
        second_got,
        vmem=vmem,
    )
    one_grad, one_low, mid_grad, query_grad = back[:4]
    pairs = [back[4]] + [
        send(part, among(by), "pair_grads_core") for by, part in enumerate(back[5:], 1)
    ]
    up_one, up_two = first_step(up_keep, up_got)
    up_y = send(up_two, to_y, "up_y")
    swapped, zero_left, zero_right = run(
        functools.partial(united_kernel, pieces),
        CHIPS,
        [whole(tok, D), whole(1, D)]
        + [whole(n, tok, D) for n in counts]
        + [slab_at(at) for at in range(3)]
        + [whole(tok, D), whole(tok, D), whole(1, D)],
        [whole(3 * tok + GAIN_ROWS, D), whole(rows, D), whole(rows, D)],
        [shape(3 * tok + GAIN_ROWS, D), shape(rows, D), shape(rows, D)],
        [pltpu.VMEM((CHIPS, tok, wide), F32)],
        query_grad,
        mid_grad,
        *pairs,
        gathered,
        gathered,
        gathered,
        hidden_zero,
        one_grad,
        gain_pre,
        vmem=LARGE,
    )
    swapped_c = send(swapped, to_core, "zero_core")
    zero_back = [
        send(part, outward(other), "zero_out") for other, part in enumerate([zero_left, zero_right])
    ]

    def slabs_of(kernel, height, *arrays):
        return simple(kernel, [shape(2, height, D)] * 2, *arrays)

    query_keep, query_send = slabs_of(
        query_grad_kernel,
        2 * OWN_ROWS,
        act_first,
        act_first_c,
        attended,
        attended_c,
        query_grad,
        one_low,
        pairs[1],
    )
    query_got = send(query_send, to_x, "query_x")
    merge_keep, merge_send = slabs_of(
        merge_grad_kernel,
        MERGE_ROWS + GAIN_ROWS,
        left,
        right,
        left_c,
        right_c,
        swapped,
        swapped_c,
    )
    merge_got = send(merge_send, to_x, "merge_x")
    pair_keep, pair_send = slabs_of(
        pair_grad_kernel, 2 * OWN_ROWS, act_first, act_first_c, swapped, swapped_c
    )
    pair_got = send(pair_send, to_y, "pair_y")
    up_own, up_send = simple(up_chip_kernel, [shape(2, OWN_ROWS, D)] * 2, up_one, up_y)
    up_x = send(up_send, to_x, "up_x")
    down_sum = add(down_one, down_y)
    query_own, query_other = first_step(query_keep, query_got)
    query_y = send(query_other, to_y, "query_y")
    frames_grad, skipped_grad = simple(
        joined_grad_kernel, [shape(MB, rows, D, dtype=F32)] * 2, *zero_back, *mergers
    )
    up_sum = simple(stack_kernel, [shape(2, 2, OWN_ROWS, D)], up_own, up_x)
    down_total, up_total = lax.psum((down_sum, up_sum), "blk")
    merge_own, merge_other = first_step(merge_keep, merge_got)
    merge_y = send(merge_other, to_y, "merge_y")
    pair_own, pair_other = first_step(pair_keep, pair_got)
    pair_x = send(pair_other, to_x, "pair_x")
    result_own, result_other = simple(
        result_parts_kernel, [shape(tok, D)] * 2, activ, activ_x, w_down
    )
    result_x = send(result_other, to_x, "result_x")
    query_steps = sum_blocks(
        add(query_own, query_y),
        "query_blocks",
        to_total(query_total_kernel, [shape(OWN_ROWS, D, dtype=F32)] * 2),
    )
    next(query_steps)
    merge_steps = sum_blocks(
        add(merge_own, merge_y),
        "merge_blocks",
        to_total(
            merge_total_kernel,
            [shape(*merger.shape, dtype=F32), shape(8, OWN_ROWS, dtype=F32)],
        ),
    )
    next(merge_steps)
    to_projector = lambda ends, array, got: simple(
        functools.partial(pair_total_kernel, ends),
        [shape(*projector.shape, dtype=F32)],
        array,
        got,
        query_total,
    )
    pair_steps = sum_blocks(add(pair_own, pair_x), "pair_blocks", to_projector)
    next(pair_steps)
    next(query_steps)
    next(merge_steps)
    next(pair_steps)
    results = simple(result_kernel, [shape(rows, D)] * 2, result_own, result_x, hidden_one)
    results = [send(part, outward(other), "result_out") for other, part in enumerate(results)]
    next(query_steps)
    next(merge_steps)
    next(pair_steps)
    query_total, combiner_grad = finish(query_steps)
    merger_grad, gain_grads = finish(merge_steps)
    result_out = simple(by_micro_kernel, [shape(MB, rows, D)], *results)
    projector_grad = finish(pair_steps)
    reducer_grad, expander_grad = simple(
        feed_total_kernel,
        [shape(*reducer.shape, dtype=F32), shape(*expander.shape, dtype=F32)],
        down_total,
        up_total,
    )
    return (
        result_out,
        frames_grad,
        skipped_grad,
        merger_grad,
        projector_grad,
        combiner_grad,
        expander_grad,
        reducer_grad,
        gain_grads[0],
        gain_grads[1],
    )


def solution(mesh):
    tokens = P(None, ("fsdp", "blk"), None)
    weight = P("fsdp", None)
    gain = P("fsdp")
    return jax.shard_map(
        local,
        mesh=mesh,
        in_specs=(tokens, tokens, P(None, "fsdp", None))
        + (weight,) * 5
        + (gain, gain, tokens),
        out_specs=(tokens, tokens, tokens) + (weight,) * 5 + (gain, gain),
        check_vma=False,
    )
```

time: 986 us -> 449 us (0.46)
  waiting for transfers between devices: 676 us -> 174 us
  Pallas kernels: 0 us -> 165 us
  matrix products: 159 us -> 0 us
  starting transfers between devices: 1.41 us -> 61.8 us
  blocking collectives: 44.6 us -> 0 us
  local copies, waits for them, and re-layouts: 45.4 us -> 15.4 us
  other arithmetic: 36.4 us -> 11 us
    reduce_scatter x5 -> x0, waiting for transfers between devices: 243 us -> none  [local(): lax.psum_scatter(shortened(sums), 'fsdp', scatter_dimension=0, tiled=True)]
    all_gather x9 -> x1, waiting for transfers between devices: 266 us -> 37.3 us  [local(): lax.all_gather(jnp.concatenate([projector, combiner], 1), 'fsdp', axis=0)]
    pallas_call x0 -> x40, Pallas kernels: none -> 165 us  [call(): pl.pallas_call(passing, grid_spec=pltpu.PrefetchScalarGridSpec(num_scalar...]
    dot_general x42 -> x0, matrix products: 159 us -> none  [the longest x2 23.2 us: local(): jnp.dot(act_second.T, upper_grad, preferred_element_type=jnp.float32)]
    ppermute x0 -> x53, waiting for transfers between devices: none -> 137 us  [send(): return lax.ppermute(array, AXES, pairs)]
    psum x1, waiting for transfers between devices: 94.4 us -> 0.01 us  [local(): down_total, up_total = lax.psum((down_sum, up_sum), 'blk')]
    unnamed x23 -> x2, waiting for transfers between devices: 73.2 us -> 0.03 us
    ppermute x0 -> x53, starting transfers between devices: none -> 61.7 us  [send(): return lax.ppermute(array, AXES, pairs)]
  transfers between devices with their start and end apart: 19 -> 55, of which waited for: 16 -> 20; matrix products, arithmetic and copies ran while one was open for 19% -> 3% of each run, Pallas kernels for 0% -> 37%
where the time goes in v1:
time: 449 us; the launch traced here: 443 us
  waiting for transfers between devices  174 us (39%)
  Pallas kernels  165 us (37%)
  starting transfers between devices  61.8 us (14%)
  between operations  15.6 us (3%)
  local copies, waits for them, and re-layouts  15.4 us (3%)
  other arithmetic  11 us (2%)
    pallas_call x40, Pallas kernels, call(): pl.pallas_call(passing, grid_spec=pltpu.PrefetchScalarGridSpec(num_scalar...  165 us
    ppermute x53, waiting for transfers between devices, send(): return lax.ppermute(array, AXES, pairs)  137 us
    ppermute x53, starting transfers between devices, send(): return lax.ppermute(array, AXES, pairs)  61.7 us
    all_gather x1, waiting for transfers between devices, local(): lax.all_gather(jnp.concatenate([projector, combiner], 1), 'fsdp', axis=0)  37.3 us
    unnamed x94, local copies, waits for them, and re-layouts  13.2 us
  transfers between devices with their start and end apart: 55, of which 20 were waited for; matrix products, arithmetic and copies ran while one was open for 3% of the time, Pallas kernels for 37%

profile of v1, /device:TPU:0, one launch (start us, length us, event | category | flops | bytes accessed | tf_op | source)
XLA Modules:
  0.0 443.0 jit_solution(13631959604959038058)
XLA Ops:
  9.1 3.0 collective-permute-start.2
  20.3 3.1 collective-permute-start.1
  25.5 7.5 %collective-permute-start = (bf16[128,3072]{1,0:T(8,128)(2,1)}, bf16[128,3072]{1,0:T(8,128)(2,1)}, u32[]{:S(2)}, u32[]{:S(2)}) collective-permute-start(bf16[128,3072]{1,0:T(8,128)(2,1)} %pad_maximum_fusion.2), channel_id=1, source_target_pairs={{0,0},{1,2},{2,4},{3,6},{4,1},{5,3},{6,5},{7,7},{8,8},{9,10},{10,1... | collective-permute-start | bytes 2359304 | tf_op jit(solution)/shard_map/tokens_in/ppermute | solution.py:559
  35.1 12.2 %collective-permute-done.4.refs_5_ = bf16[272,1024]{1,0:T(8,128)(2,1)S(1)} collective-permute-done((bf16[272,1024]{1,0:T(8,128)(2,1)S(1)}, bf16[272,1024]{1,0:T(8,128)(2,1)S(1)}, u32[]{:S(2)}, u32[]{:S(2)}) %collective-permute-start.4) | collective-permute-done | bytes 557088 | tf_op jit(solution)/shard_map/merger_around/ppermute | solution.py:559
  50.7 4.7 %merge_kernel.1 = (s32[8]{0:T(128)S(1)}, f32[256,1024]{1,0:T(8,128)S(1)}, bf16[256,1024]{1,0:T(8,128)(2,1)}, f32[1,1024]{1,0:T(1,128)S(1)}, f32[1,1024]{1,0:T(1,128)S(1)}) custom-call(s32[8]{0:T(128)S(1)} %stack.62.index_ref, bf16[128,3072]{1,0:T(8,128)(2,1)} %collective-permute-done.refs_0_, bf16[128,3072]{1,0:T(8,128)(2,1)} %collective-permute-done.1.refs_1_, ...), custom_call_target="tpu_custom_call" | custom-call | flops 999999995904 | tf_op jit(solution)/shard_map/merge_kernel/pallas_call | solution.py:495
  57.9 2.8 collective-permute-start.15
  60.7 37.3 %all-gather.3.cloned.1.call-done = bf16[1024,4096]{1,0:T(8,128)(2,1)} async-done(((bf16[128,4096]{1,0:T(8,128)(2,1)}), bf16[1024,4096]{1,0:T(8,128)(2,1)}) %all-gather.3.cloned.1.call-update) | async-done | bytes 8388624 | tf_op jit(solution)/shard_map/all_gather | solution.py:620
  98.0 3.4 copy-done.3
  102.6 5.7 %project_kernel.1 = (s32[8]{0:T(128)S(1)}, bf16[256,1024]{1,0:T(8,128)(2,1)}, bf16[256,1024]{1,0:T(8,128)(2,1)S(1)}, bf16[256,1024]{1,0:T(8,128)(2,1)S(1)}, bf16[256,1024]{1,0:T(8,128)(2,1)}) custom-call(s32[8]{0:T(128)S(1)} %get-tuple-element.129.index_ref, f32[256,1024]{1,0:T(8,128)S(1)} %copy-done.27, f32[1,1024]{1,0:T(1,128)S(1)} %get-tuple-element.131.refs_1_.refs_9_, ...), custom_call_target="tpu_custom_call" | custom-call | flops 999999995904 | tf_op jit(solution)/shard_map/project_kernel/pallas_call | solution.py:495
  113.4 3.4 copy-done.4
  116.8 8.6 %attend_kernel.1 = (s32[8]{0:T(128)S(1)}, bf16[256,1024]{1,0:T(8,128)(2,1)}, f32[256,1024]{1,0:T(8,128)S(1)}, bf16[256,1024]{1,0:T(8,128)(2,1)}, bf16[16,2,256,256]{3,2,1,0:T(8,128)(2,1)S(1)}) custom-call(s32[8]{0:T(128)S(1)} %get-tuple-element.132.index_ref, bf16[256,1024]{1,0:T(8,128)(2,1)S(1)} %copy-done.39, s32[1,256]{1,0:T(1,128)S(1)} %bitcast.57, ...), custom_call_target="tpu_custom_call" | custom-call | flops 999999995904 | tf_op jit(solution)/shard_map/attend_kernel/pallas_call | solution.py:495
  126.4 12.3 %collective-permute-done.16.refs_1_ = bf16[2,2,128,1024]{3,2,1,0:T(8,128)(2,1)} collective-permute-done((bf16[2,2,128,1024]{3,2,1,0:T(8,128)(2,1)}, bf16[2,2,128,1024]{3,2,1,0:T(8,128)(2,1)}, u32[]{:S(2)}, u32[]{:S(2)}) %collective-permute-start.16) | collective-permute-done | bytes 1048608 | tf_op jit(solution)/shard_map/w_up_y/ppermute | solution.py:559
  139.2 3.0 down_kernel.1
  144.1 3.4 up_kernel.1
  147.5 6.0 %feed_kernel.2 = (s32[8]{0:T(128)S(1)}, bf16[256,1024]{1,0:T(8,128)(2,1)S(1)}, bf16[256,2048]{1,0:T(8,128)(2,1)S(1)}, bf16[256,2048]{1,0:T(8,128)(2,1)S(1)}) custom-call(s32[8]{0:T(128)S(1)} %get-tuple-element.142.index_ref, bf16[256,1024]{1,0:T(8,128)(2,1)} %get-tuple-element.143.refs_0_, bf16[256,1024]{1,0:T(8,128)(2,1)} %get-tuple-element.144.refs_1_.refs_2_.refs_8_, ...), custom_call_target="tpu_custom_call" | custom-call | flops 999999995904 | tf_op jit(solution)/shard_map/feed_kernel/pallas_call | solution.py:495
  153.7 3.9 collective-permute-done.19.refs_0_.refs_1_
  157.5 7.0 %feed_kernel.3 = (s32[8]{0:T(128)S(1)}, bf16[256,1024]{1,0:T(8,128)(2,1)}, bf16[256,2048]{1,0:T(8,128)(2,1)S(1)}, bf16[256,2048]{1,0:T(8,128)(2,1)S(1)}) custom-call(s32[8]{0:T(128)S(1)} %get-tuple-element.147.index_ref, bf16[256,1024]{1,0:T(8,128)(2,1)} %collective-permute-done.19.refs_0_.refs_1_, ...), custom_call_target="tpu_custom_call" | custom-call | flops 999999995904 | tf_op jit(solution)/shard_map/feed_kernel/pallas_call | solution.py:495
  164.6 6.4 %down_grad_kernel.1 = (s32[8]{0:T(128)S(1)}, bf16[2,512,1024]{2,1,0:T(8,128)(2,1)S(1)}, bf16[2,512,1024]{2,1,0:T(8,128)(2,1)}) custom-call(s32[8]{0:T(128)S(1)} %get-tuple-element.148.index_ref, bf16[256,2048]{1,0:T(8,128)(2,1)S(1)} %get-tuple-element.149.refs_0_, bf16[256,2048]{1,0:T(8,128)(2,1)S(1)} %get-tuple-element.150.refs_1_, ...), custom_call_target="tpu_custom_call" | custom-call | flops 999999995904 | tf_op jit(solution)/shard_map/down_grad_kernel/pallas_call | solution.py:495
  170.9 6.4 %up_grad_kernel.1 = (s32[8]{0:T(128)S(1)}, bf16[2,2,2,128,1024]{4,3,2,1,0:T(8,128)(2,1)S(1)}, bf16[2,2,2,128,1024]{4,3,2,1,0:T(8,128)(2,1)}) custom-call(s32[8]{0:T(128)S(1)} %get-tuple-element.151.index_ref, bf16[256,1024]{1,0:T(8,128)(2,1)} %get-tuple-element.143.refs_0_, bf16[256,1024]{1,0:T(8,128)(2,1)} %collective-permute-done.19.refs_0_.refs_1_, ...), custom_call_target="tpu_custom_call" | custom-call | flops 999999995904 | tf_op jit(solution)/shard_map/up_grad_kernel/pallas_call | solution.py:495
  178.3 3.6 add_two_kernel.5
  181.8 10.2 %collective-permute-done.22.refs_13_ = bf16[256,1024]{1,0:T(8,128)(2,1)} collective-permute-done((bf16[256,1024]{1,0:T(8,128)(2,1)}, bf16[256,1024]{1,0:T(8,128)(2,1)}, u32[]{:S(2)}, u32[]{:S(2)}) %collective-permute-start.22) | collective-permute-done | bytes 524320 | tf_op jit(solution)/shard_map/second_x/ppermute | solution.py:559
  192.1 15.0 %attend_back_kernel.1 = (s32[8]{0:T(128)S(1)}, f32[256,1024]{1,0:T(8,128)S(1)}, bf16[256,1024]{1,0:T(8,128)(2,1)S(1)}, f32[1,1024]{1,0:T(1,128)S(1)}, bf16[256,1...) custom-call(s32[8]{0:T(128)S(1)} %get-tuple-element.157.index_ref, ...), custom_call_target="tpu_custom_call" | custom-call | flops 999999995904 | tf_op jit(solution)/shard_map/attend_back_kernel/pallas_call | solution.py:495
  207.5 3.6 add_two_kernel.6
  212.1 7.1 %united_kernel.1 = (s32[8]{0:T(128)S(1)}, bf16[784,1024]{1,0:T(8,128)(2,1)}, bf16[128,1024]{1,0:T(8,128)(2,1)}, bf16[128,1024]{1,0:T(8,128)(2,1)}) custom-call(s32[8]{0:T(128)S(1)} %get-tuple-element.165.index_ref, bf16[256,1024]{1,0:T(8,128)(2,1)S(1)} %get-tuple-element.166.refs_0_.refs_4_, f32[1,1024]{1,0:T(1,128)S(1)} %get-tuple-element.167.refs_1_, ...), custom_call_target="tpu_custom_call" | custom-call | flops 999999995904 | tf_op jit(solution)/shard_map/united_kernel/pallas_call | solution.py:495
  220.9 5.1 %query_grad_kernel.1 = (s32[8]{0:T(128)S(1)}, bf16[2,256,1024]{2,1,0:T(8,128)(2,1)S(1)}, bf16[2,256,1024]{2,1,0:T(8,128)(2,1)}) custom-call(s32[8]{0:T(128)S(1)} %get-tuple-element.171.index_ref, bf16[256,1024]{1,0:T(8,128)(2,1)} %get-tuple-element.172.refs_0_, bf16[256,1024]{1,0:T(8,128)(2,1)} %collective-permute-done.25.refs_1_, ...), custom_call_target="tpu_custom_call" | custom-call | flops 999999995904 | tf_op jit(solution)/shard_map/query_grad_kernel/pallas_call | solution.py:495
  227.0 3.9 collective-permute-start.33
  231.1 5.7 %merge_grad_kernel.1 = (s32[8]{0:T(128)S(1)}, bf16[2,272,1024]{2,1,0:T(8,128)(2,1)S(1)}, bf16[2,272,1024]{2,1,0:T(8,128)(2,1)}) custom-call(s32[8]{0:T(128)S(1)} %get-tuple-element.175.index_ref, bf16[128,3072]{1,0:T(8,128)(2,1)} %collective-permute-done.refs_0_, bf16[128,3072]{1,0:T(8,128)(2,1)} %collective-permute-done.1.refs_1_, ...), custom_call_target="tpu_custom_call" | custom-call | flops 999999995904 | tf_op jit(solution)/shard_map/merge_grad_kernel/pallas_call | solution.py:495
  236.8 5.1 %pair_grad_kernel.1 = (s32[8]{0:T(128)S(1)}, bf16[2,256,1024]{2,1,0:T(8,128)(2,1)S(1)}, bf16[2,256,1024]{2,1,0:T(8,128)(2,1)}) custom-call(s32[8]{0:T(128)S(1)} %get-tuple-element.177.index_ref, bf16[256,1024]{1,0:T(8,128)(2,1)} %get-tuple-element.172.refs_0_, bf16[256,1024]{1,0:T(8,128)(2,1)} %collective-permute-done.25.refs_1_, ...), custom_call_target="tpu_custom_call" | custom-call | flops 999999995904 | tf_op jit(solution)/shard_map/pair_grad_kernel/pallas_call | solution.py:495
  241.9 2.7 up_chip_kernel.1
  245.8 14.0 %collective-permute-done.31.refs_1_ = bf16[512,1024]{1,0:T(8,128)(2,1)} collective-permute-done((bf16[512,1024]{1,0:T(8,128)(2,1)}, bf16[512,1024]{1,0:T(8,128)(2,1)}, u32[]{:S(2)}, u32[]{:S(2)}) %collective-permute-start.31) | collective-permute-done | bytes 1048608 | tf_op jit(solution)/shard_map/down_y/ppermute | solution.py:559
  260.8 3.0 add_kernel.10
  264.1 2.8 add_two_kernel.7
  268.8 6.8 %joined_grad_kernel.1 = (s32[8]{0:T(128)S(1)}, f32[2,128,1024]{2,1,0:T(8,128)}, f32[2,128,1024]{2,1,0:T(8,128)}) custom-call(s32[8]{0:T(128)S(1)} %get-tuple-element.187.index_ref, bf16[128,1024]{1,0:T(8,128)(2,1)} %collective-permute-done.33.refs_0_, bf16[128,1024]{1,0:T(8,128)(2,1)} %collective-permute-done.34.refs_1_, ...), custom_call_target="tpu_custom_call" | custom-call | flops 999999995904 | tf_op jit(solution)/shard_map/joined_grad_kernel/pallas_call | solution.py:495
  275.6 2.6 stack_kernel.1
  278.3 8.8 %collective-permute-done.36.refs_1_ = bf16[2,272,1024]{2,1,0:T(8,128)(2,1)} collective-permute-done((bf16[2,272,1024]{2,1,0:T(8,128)(2,1)}, bf16[2,272,1024]{2,1,0:T(8,128)(2,1)}, u32[]{:S(2)}, u32[]{:S(2)}) %collective-permute-start.36) | collective-permute-done | bytes 1114144 | tf_op jit(solution)/shard_map/merge_x/ppermute | solution.py:559
  287.1 2.7 add_two_kernel.8
  290.2 3.0 add_two_kernel.9
  293.4 3.7 result_parts_kernel.1
  300.2 2.5 add_kernel.11
  306.2 5.4 %collective-permute-done.39.refs_1_ = bf16[272,1024]{1,0:T(8,128)(2,1)} collective-permute-done((bf16[272,1024]{1,0:T(8,128)(2,1)}, bf16[272,1024]{1,0:T(8,128)(2,1)}, u32[]{:S(2)}, u32[]{:S(2)}) %collective-permute-start.39) | collective-permute-done | bytes 557088 | tf_op jit(solution)/shard_map/merge_y/ppermute | solution.py:559
  311.7 2.5 add_kernel.12
  314.2 2.1 collective-permute-start.42
  316.3 2.5 add_kernel.13
  318.8 2.1 collective-permute-start.43
  321.0 7.1 %collective-permute-done.41.refs_1_ = bf16[256,1024]{1,0:T(8,128)(2,1)} collective-permute-done((bf16[256,1024]{1,0:T(8,128)(2,1)}, bf16[256,1024]{1,0:T(8,128)(2,1)}, u32[]{:S(2)}, u32[]{:S(2)}) %collective-permute-start.41) | collective-permute-done | bytes 524320 | tf_op jit(solution)/shard_map/query_blocks/ppermute | solution.py:559
  328.1 2.7 add_kernel.14
  332.2 9.2 %collective-permute-done.42.refs_1_ = bf16[272,1024]{1,0:T(8,128)(2,1)} collective-permute-done((bf16[272,1024]{1,0:T(8,128)(2,1)}, bf16[272,1024]{1,0:T(8,128)(2,1)}, u32[]{:S(2)}, u32[]{:S(2)}) %collective-permute-start.42) | collective-permute-done | bytes 557088 | tf_op jit(solution)/shard_map/merge_blocks/ppermute | solution.py:559
  341.4 2.8 add_kernel.15
  345.7 16.2 %collective-permute-done.43.refs_1_ = bf16[256,1024]{1,0:T(8,128)(2,1)} collective-permute-done((bf16[256,1024]{1,0:T(8,128)(2,1)}, bf16[256,1024]{1,0:T(8,128)(2,1)}, u32[]{:S(2)}, u32[]{:S(2)}) %collective-permute-start.43) | collective-permute-done | bytes 524320 | tf_op jit(solution)/shard_map/pair_blocks/ppermute | solution.py:559
  361.9 2.7 add_kernel.16
  366.0 2.5 result_kernel.1
  368.5 2.7 add_kernel.17
  372.5 3.6 collective-permute-start.50
  376.1 4.3 collective-permute-start.51
  380.4 2.7 add_kernel.18
  384.4 2.7 add_kernel.19
  388.4 6.9 %collective-permute-done.48.refs_1_ = bf16[256,1024]{1,0:T(8,128)(2,1)} collective-permute-done((bf16[256,1024]{1,0:T(8,128)(2,1)}, bf16[256,1024]{1,0:T(8,128)(2,1)}, u32[]{:S(2)}, u32[]{:S(2)}) %collective-permute-start.48) | collective-permute-done | bytes 524320 | tf_op jit(solution)/shard_map/query_blocks/ppermute | solution.py:559
  395.3 2.6 query_total_kernel.1
  397.9 19.4 %collective-permute-done.49.refs_1_ = bf16[272,1024]{1,0:T(8,128)(2,1)} collective-permute-done((bf16[272,1024]{1,0:T(8,128)(2,1)}, bf16[272,1024]{1,0:T(8,128)(2,1)}, u32[]{:S(2)}, u32[]{:S(2)}) %collective-permute-start.49) | collective-permute-done | bytes 557088 | tf_op jit(solution)/shard_map/merge_blocks/ppermute | solution.py:559
  417.3 2.8 merge_total_kernel.1
  420.2 2.4 by_micro_kernel.1
  422.6 4.4 collective-permute-done.52.refs_1_
  427.0 3.0 pair_total_kernel.1
  432.9 2.8 feed_total_kernel.1
  (222 shorter events, 57.5 us)
Async XLA Ops:
  7.2 90.8 %all-gather.3.cloned.1.call-start = ((), (), s32[]{:S(2)}) async-start(), calls=%async_computation | async-start | bytes 9437184 | tf_op jit(solution)/shard_map/all_gather | solution.py:620
  9.1 16.5 %collective-permute-start.2 = (bf16[272,1024]{1,0:T(8,128)(2,1)S(1)}, bf16[272,1024]{1,0:T(8,128)(2,1)S(1)}, u32[]{:S(2)}, u32[]{:S(2)}) collective-permute-start(bf16[272,1024]{1,0:T(8,128)(2,1)S(1)} %pad_maximum_fusion.4.refs_2_), channel_id=1, source_target_pairs={{0,8},{1,9},{2,10},{3,11},{4,12},{5,13},{6,14},{7,15},{8,0},{9,1},... | collective-permute-start | bytes 1671176 | tf_op jit(solution)/shard_map/merger_around/ppermute | solution.py:559
  12.1 23.0 %collective-permute-start.3 = (bf16[272,1024]{1,0:T(8,128)(2,1)S(1)}, bf16[272,1024]{1,0:T(8,128)(2,1)S(1)}, u32[]{:S(2)}, u32[]{:S(2)}) collective-permute-start(bf16[272,1024]{1,0:T(8,128)(2,1)S(1)} %pad_maximum_fusion.4.refs_2_), channel_id=1, source_target_pairs={{0,16},{1,17},{2,18},{3,19},{4,20},{5,21},{6,22},{7,23},{8,24},{9,... | collective-permute-start | bytes 1671176 | tf_op jit(solution)/shard_map/merger_around/ppermute | solution.py:559
  13.6 33.7 %collective-permute-start.4 = (bf16[272,1024]{1,0:T(8,128)(2,1)S(1)}, bf16[272,1024]{1,0:T(8,128)(2,1)S(1)}, u32[]{:S(2)}, u32[]{:S(2)}) collective-permute-start(bf16[272,1024]{1,0:T(8,128)(2,1)S(1)} %pad_maximum_fusion.4.refs_2_), channel_id=1, source_target_pairs={{0,24},{1,25},{2,26},{3,27},{4,28},{5,29},{6,30},{7,31},{8,16},{9,... | collective-permute-start | bytes 1671176 | tf_op jit(solution)/shard_map/merger_around/ppermute | solution.py:559
  13.6 33.7 %collective-permute-start.5 = (bf16[272,1024]{1,0:T(8,128)(2,1)S(1)}, bf16[272,1024]{1,0:T(8,128)(2,1)}, u32[]{:S(2)}, u32[]{:S(2)}) collective-permute-start(bf16[272,1024]{1,0:T(8,128)(2,1)S(1)} %pad_maximum_fusion.4.refs_2_), channel_id=1, source_target_pairs={{0,4},{1,5},{2,6},{3,7},{4,0},{5,1},{6,2},{7,3},{8,12},{9,13},{10,... | collective-permute-start | bytes 1671176 | tf_op jit(solution)/shard_map/merger_core/ppermute | solution.py:559
  13.6 6.6 %collective-permute-start.9 = (s32[2,1,9]{2,1,0:T(1,128)}, s32[2,1,9]{2,1,0:T(1,128)S(1)}, u32[]{:S(2)}, u32[]{:S(2)}) collective-permute-start(s32[2,1,9]{2,1,0:T(1,128)} %param.13), channel_id=1, source_target_pairs={{0,4},{1,5},{2,6},{3,7},{4,0},{5,1},{6,2},{7,3},{8,12},{9,13},{10,... | collective-permute-start | bytes 224 | tf_op jit(solution)/shard_map/lengths_core/ppermute | solution.py:559
  16.2 414.3 %all-reduce.4.cloned.1.call-start = ((), (), s32[]{:S(2)}) async-start(), calls=%async_computation.1 | async-start | bytes 4194304 | tf_op jit(solution)/shard_map/psum | solution.py:933
  20.3 30.3 %collective-permute-start.1 = (bf16[128,3072]{1,0:T(8,128)(2,1)}, bf16[128,3072]{1,0:T(8,128)(2,1)}, u32[]{:S(2)}, u32[]{:S(2)}) collective-permute-start(bf16[128,3072]{1,0:T(8,128)(2,1)} %pad_maximum_fusion.3), channel_id=1, source_target_pairs={{0,2},{1,0},{2,6},{3,4},{4,3},{5,1},{6,7},{7,5},{8,10},{9,8},{10,1... | collective-permute-start | bytes 2359304 | tf_op jit(solution)/shard_map/tokens_in/ppermute | solution.py:559
  25.5 29.9 %copy-start.12 = (bf16[272,1024]{1,0:T(8,128)(2,1)}, bf16[272,1024]{1,0:T(8,128)(2,1)S(1)}, u32[]{:S(2)}) copy-start(bf16[272,1024]{1,0:T(8,128)(2,1)S(1)} %collective-permute-done.2.refs_3_) | copy-start | bytes 1671172
  25.5 25.1 %collective-permute-start = (bf16[128,3072]{1,0:T(8,128)(2,1)}, bf16[128,3072]{1,0:T(8,128)(2,1)}, u32[]{:S(2)}, u32[]{:S(2)}) collective-permute-start(bf16[128,3072]{1,0:T(8,128)(2,1)} %pad_maximum_fusion.2), channel_id=1, source_target_pairs={{0,0},{1,2},{2,4},{3,6},{4,1},{5,3},{6,5},{7,7},{8,8},{9,10},{10,1... | collective-permute-start | bytes 2359304 | tf_op jit(solution)/shard_map/tokens_in/ppermute | solution.py:559
  35.1 15.5 %collective-permute-start.6 = (bf16[272,1024]{1,0:T(8,128)(2,1)S(1)}, bf16[272,1024]{1,0:T(8,128)(2,1)S(1)}, u32[]{:S(2)}, u32[]{:S(2)}) collective-permute-start(bf16[272,1024]{1,0:T(8,128)(2,1)S(1)} %collective-permute-done.2.refs_3_), channel_id=1, source_target_pairs={{0,4},{1,5},{2,6},{3,7},{4,0},{5,1},{6,2},{7,3},{8,12},{9,13},{10,... | collective-permute-start | bytes 1671176 | tf_op jit(solution)/shard_map/merger_core/ppermute | solution.py:559
  47.3 3.3 collective-permute-start.7
  47.3 3.3 collective-permute-start.8
  57.4 55.4 %collective-permute-start.12 = (bf16[512,1024]{1,0:T(8,128)(2,1)}, bf16[512,1024]{1,0:T(8,128)(2,1)}, u32[]{:S(2)}, u32[]{:S(2)}) collective-permute-start(bf16[512,1024]{1,0:T(8,128)(2,1)} %get-tuple-element.138), channel_id=1, source_target_pairs={{0,16},{1,17},{2,18},{3,19},{4,20},{5,21},{6,22},{7,23},{8,24},{9,... | collective-permute-start | bytes 3145736 | tf_op jit(solution)/shard_map/w_down_y/ppermute | solution.py:559
  57.9 52.6 %collective-permute-start.15 = (bf16[2,128,1024]{2,1,0:T(8,128)(2,1)}, bf16[2,128,1024]{2,1,0:T(8,128)(2,1)}, u32[]{:S(2)}, u32[]{:S(2)}) collective-permute-start(bf16[2,128,1024]{2,1,0:T(8,128)(2,1)} %get-tuple-element.141), channel_id=1, source_target_pairs={{0,8},{1,9},{2,10},{3,11},{4,12},{5,13},{6,14},{7,15},{8,0},{9,1},... | collective-permute-start | bytes 1572872 | tf_op jit(solution)/shard_map/w_up_x/ppermute | solution.py:559
  109.2 3.9 collective-permute-start.10
  109.4 3.7 collective-permute-start.11
  110.1 115.9 %collective-permute-start.28 = (bf16[128,3072]{1,0:T(8,128)(2,1)}, bf16[128,3072]{1,0:T(8,128)(2,1)}, u32[]{:S(2)}, u32[]{:S(2)}) collective-permute-start(bf16[128,3072]{1,0:T(8,128)(2,1)} %collective-permute-done.1.refs_1_), channel_id=1, source_target_pairs={{0,4},{1,5},{2,6},{3,7},{4,0},{5,1},{6,2},{7,3},{8,12},{9,13},{10,... | collective-permute-start | bytes 2359304 | tf_op jit(solution)/shard_map/joined_core/ppermute | solution.py:559
  110.5 116.5 %collective-permute-start.27 = (bf16[128,3072]{1,0:T(8,128)(2,1)}, bf16[128,3072]{1,0:T(8,128)(2,1)}, u32[]{:S(2)}, u32[]{:S(2)}) collective-permute-start(bf16[128,3072]{1,0:T(8,128)(2,1)} %collective-permute-done.refs_0_), channel_id=1, source_target_pairs={{0,4},{1,5},{2,6},{3,7},{4,0},{5,1},{6,2},{7,3},{8,12},{9,13},{10,... | collective-permute-start | bytes 2359304 | tf_op jit(solution)/shard_map/joined_core/ppermute | solution.py:559
  112.8 12.6 %collective-permute-start.13 = (bf16[512,1024]{1,0:T(8,128)(2,1)}, bf16[512,1024]{1,0:T(8,128)(2,1)}, u32[]{:S(2)}, u32[]{:S(2)}) collective-permute-start(bf16[512,1024]{1,0:T(8,128)(2,1)} %get-tuple-element.138), channel_id=1, source_target_pairs={{0,4},{1,5},{2,6},{3,7},{4,0},{5,1},{6,2},{7,3},{8,12},{9,13},{10,... | collective-permute-start | bytes 3145736 | tf_op jit(solution)/shard_map/w_down_core/ppermute | solution.py:559
  113.1 25.6 %collective-permute-start.16 = (bf16[2,2,128,1024]{3,2,1,0:T(8,128)(2,1)}, bf16[2,2,128,1024]{3,2,1,0:T(8,128)(2,1)}, u32[]{:S(2)}, u32[]{:S(2)}) collective-permute-start(bf16[2,2,128,1024]{3,2,1,0:T(8,128)(2,1)} %pad_maximum_fusion.1.refs_0_), channel_id=1, source_target_pairs={{0,16},{1,17},{2,18},{3,19},{4,20},{5,21},{6,22},{7,23},{8,24},{9,... | collective-permute-start | bytes 3145736 | tf_op jit(solution)/shard_map/w_up_y/ppermute | solution.py:559
  113.1 25.6 %collective-permute-start.14 = (bf16[512,1024]{1,0:T(8,128)(2,1)}, bf16[512,1024]{1,0:T(8,128)(2,1)}, u32[]{:S(2)}, u32[]{:S(2)}) collective-permute-start(bf16[512,1024]{1,0:T(8,128)(2,1)} %collective-permute-done.12.refs_1_), channel_id=1, source_target_pairs={{0,4},{1,5},{2,6},{3,7},{4,0},{5,1},{6,2},{7,3},{8,12},{9,13},{10,... | collective-permute-start | bytes 3145736 | tf_op jit(solution)/shard_map/w_down_core/ppermute | solution.py:559
  116.8 22.4 %copy-start.9 = (bf16[512,1024]{1,0:T(8,128)(2,1)S(1)}, bf16[512,1024]{1,0:T(8,128)(2,1)}, u32[]{:S(2)}) copy-start(bf16[512,1024]{1,0:T(8,128)(2,1)} %refs_0_.3) | copy-start | bytes 3145732
  125.4 16.8 %copy-start.22 = (bf16[16,2,256,256]{3,2,1,0:T(8,128)(2,1)}, bf16[16,2,256,256]{3,2,1,0:T(8,128)(2,1)S(1)}, u32[]{:S(2)}) copy-start(bf16[16,2,256,256]{3,2,1,0:T(8,128)(2,1)S(1)} %get-tuple-element.158.refs_1_) | copy-start | bytes 12582916
  125.4 66.6 %copy-start.30 = (f32[256,1024]{1,0:T(8,128)}, f32[256,1024]{1,0:T(8,128)S(1)}, u32[]{:S(2)}) copy-start(f32[256,1024]{1,0:T(8,128)S(1)} %get-tuple-element.159.refs_7_.refs_2_) | copy-start | bytes 3145732
  125.4 28.1 %collective-permute-start.20 = (bf16[256,1024]{1,0:T(8,128)(2,1)}, bf16[256,1024]{1,0:T(8,128)(2,1)}, u32[]{:S(2)}, u32[]{:S(2)}) collective-permute-start(bf16[256,1024]{1,0:T(8,128)(2,1)} %get-tuple-element.144.refs_1_.refs_2_.refs_8_), channel_id=1, source_target_pairs={{0,8},{1,9},{2,10},{3,11},{4,12},{5,13},{6,14},{7,15},{8,0},{9,1},... | collective-permute-start | bytes 1572872 | tf_op jit(solution)/shard_map/cot_x/ppermute | solution.py:559
  138.7 3.5 collective-permute-start.17
  138.7 4.5 %collective-permute-start.18 = (bf16[2,2,128,1024]{3,2,1,0:T(8,128)(2,1)}, bf16[2,2,128,1024]{3,2,1,0:T(8,128)(2,1)}, u32[]{:S(2)}, u32[]{:S(2)}) collective-permute-start(bf16[2,2,128,1024]{3,2,1,0:T(8,128)(2,1)} %collective-permute-done.16.refs_1_), channel_id=1, source_target_pairs={{0,4},{1,5},{2,6},{3,7},{4,0},{5,1},{6,2},{7,3},{8,12},{9,13},{10,... | collective-permute-start | bytes 3145736 | tf_op jit(solution)/shard_map/w_up_core/ppermute | solution.py:559
  142.3 15.3 %copy-start.20 = (bf16[4,512,1024]{2,1,0:T(8,128)(2,1)}, bf16[4,512,1024]{2,1,0:T(8,128)(2,1)S(1)}, u32[]{:S(2)}) copy-start(bf16[4,512,1024]{2,1,0:T(8,128)(2,1)S(1)} %get-tuple-element.146) | copy-start | bytes 12582916
  142.3 77.0 %collective-permute-start.25 = (bf16[256,1024]{1,0:T(8,128)(2,1)}, bf16[256,1024]{1,0:T(8,128)(2,1)}, u32[]{:S(2)}, u32[]{:S(2)}) collective-permute-start(bf16[256,1024]{1,0:T(8,128)(2,1)} %get-tuple-element.172.refs_0_), channel_id=1, source_target_pairs={{0,4},{1,5},{2,6},{3,7},{4,0},{5,1},{6,2},{7,3},{8,12},{9,13},{10,... | collective-permute-start | bytes 1572872 | tf_op jit(solution)/shard_map/act_core/ppermute | solution.py:559
  143.2 14.3 %collective-permute-start.19 = (bf16[256,1024]{1,0:T(8,128)(2,1)}, bf16[256,1024]{1,0:T(8,128)(2,1)}, u32[]{:S(2)}, u32[]{:S(2)}) collective-permute-start(bf16[256,1024]{1,0:T(8,128)(2,1)} %get-tuple-element.143.refs_0_), channel_id=1, source_target_pairs={{0,8},{1,9},{2,10},{3,11},{4,12},{5,13},{6,14},{7,15},{8,0},{9,1},... | collective-permute-start | bytes 1572872 | tf_op jit(solution)/shard_map/act_x/ppermute | solution.py:559
  153.6 67.3 %collective-permute-start.26 = (bf16[256,1024]{1,0:T(8,128)(2,1)}, bf16[256,1024]{1,0:T(8,128)(2,1)}, u32[]{:S(2)}, u32[]{:S(2)}) collective-permute-start(bf16[256,1024]{1,0:T(8,128)(2,1)} %get-tuple-element.173.refs_2_), channel_id=1, source_target_pairs={{0,4},{1,5},{2,6},{3,7},{4,0},{5,1},{6,2},{7,3},{8,12},{9,13},{10,... | collective-permute-start | bytes 1572872 | tf_op jit(solution)/shard_map/attended_core/ppermute | solution.py:559
  170.9 6.4 %collective-permute-start.21 = (bf16[2,512,1024]{2,1,0:T(8,128)(2,1)}, bf16[2,512,1024]{2,1,0:T(8,128)(2,1)}, u32[]{:S(2)}, u32[]{:S(2)}) collective-permute-start(bf16[2,512,1024]{2,1,0:T(8,128)(2,1)} %get-tuple-element.156), channel_id=1, source_target_pairs={{0,4},{1,5},{2,6},{3,7},{4,0},{5,1},{6,2},{7,3},{8,12},{9,13},{10,... | collective-permute-start | bytes 6291464 | tf_op jit(solution)/shard_map/down_core/ppermute | solution.py:559
  177.4 14.7 %collective-permute-start.22 = (bf16[256,1024]{1,0:T(8,128)(2,1)}, bf16[256,1024]{1,0:T(8,128)(2,1)}, u32[]{:S(2)}, u32[]{:S(2)}) collective-permute-start(bf16[256,1024]{1,0:T(8,128)(2,1)} %get-tuple-element.161), channel_id=1, source_target_pairs={{0,8},{1,9},{2,10},{3,11},{4,12},{5,13},{6,14},{7,15},{8,0},{9,1},... | collective-permute-start | bytes 1572872 | tf_op jit(solution)/shard_map/second_x/ppermute | solution.py:559
  178.2 13.8 %copy-start.1 = (f32[2,256,128]{2,1,0:T(8,128)S(1)}, f32[2,256,128]{2,1,0:T(8,128)}, u32[]{:S(2)}) copy-start(f32[2,256,128]{2,1,0:T(8,128)} %copy-done) | copy-start | bytes 786436
  178.2 13.8 %copy-start.5 = (bf16[1024,4096]{1,0:T(8,128)(2,1)S(1)}, bf16[1024,4096]{1,0:T(8,128)(2,1)}, u32[]{:S(2)}) copy-start(bf16[1024,4096]{1,0:T(8,128)(2,1)} %all-gather.3.cloned.1.call-done) | copy-start | bytes 25165828
  178.2 13.8 %copy-start.23 = (bf16[16,2,256,256]{3,2,1,0:T(8,128)(2,1)S(1)}, bf16[16,2,256,256]{3,2,1,0:T(8,128)(2,1)}, u32[]{:S(2)}) copy-start(bf16[16,2,256,256]{3,2,1,0:T(8,128)(2,1)} %copy-done.22) | copy-start | bytes 12582916
  178.2 13.8 %copy-start.40 = (bf16[256,1024]{1,0:T(8,128)(2,1)S(1)}, bf16[256,1024]{1,0:T(8,128)(2,1)}, u32[]{:S(2)}) copy-start(bf16[256,1024]{1,0:T(8,128)(2,1)} %copy-done.38) | copy-start | bytes 1572868
  192.0 15.0 %collective-permute-start.23 = (bf16[2,2,2,128,1024]{4,3,2,1,0:T(8,128)(2,1)}, bf16[2,2,2,128,1024]{4,3,2,1,0:T(8,128)(2,1)}, u32[]{:S(2)}, u32[]{:S(2)}) collective-permute-start(bf16[2,2,2,128,1024]{4,3,2,1,0:T(8,128)(2,1)} %get-tuple-element.164), channel_id=1, source_target_pairs={{0,4},{1,5},{2,6},{3,7},{4,0},{5,1},{6,2},{7,3},{8,12},{9,13},{10,... | collective-permute-start | bytes 6291464 | tf_op jit(solution)/shard_map/up_core/ppermute | solution.py:559
  207.0 4.6 %collective-permute-start.24 = (bf16[4,256,1024]{2,1,0:T(8,128)(2,1)}, bf16[4,256,1024]{2,1,0:T(8,128)(2,1)}, u32[]{:S(2)}, u32[]{:S(2)}) collective-permute-start(bf16[4,256,1024]{2,1,0:T(8,128)(2,1)} %get-tuple-element.169), channel_id=1, source_target_pairs={{0,4},{1,5},{2,6},{3,7},{4,0},{5,1},{6,2},{7,3},{8,12},{9,13},{10,... | collective-permute-start | bytes 6291464 | tf_op jit(solution)/shard_map/pair_grads_core/ppermute | solution.py:559
  211.7 30.3 %collective-permute-start.30 = (bf16[2,2,128,1024]{3,2,1,0:T(8,128)(2,1)}, bf16[2,2,128,1024]{3,2,1,0:T(8,128)(2,1)}, u32[]{:S(2)}, u32[]{:S(2)}) collective-permute-start(bf16[2,2,128,1024]{3,2,1,0:T(8,128)(2,1)} %get-tuple-element.180), channel_id=1, source_target_pairs={{0,16},{1,17},{2,18},{3,19},{4,20},{5,21},{6,22},{7,23},{8,24},{9,... | collective-permute-start | bytes 3145736 | tf_op jit(solution)/shard_map/up_y/ppermute | solution.py:559
  219.3 40.6 %collective-permute-start.31 = (bf16[512,1024]{1,0:T(8,128)(2,1)}, bf16[512,1024]{1,0:T(8,128)(2,1)}, u32[]{:S(2)}, u32[]{:S(2)}) collective-permute-start(bf16[512,1024]{1,0:T(8,128)(2,1)} %get-tuple-element.183), channel_id=1, source_target_pairs={{0,16},{1,17},{2,18},{3,19},{4,20},{5,21},{6,22},{7,23},{8,24},{9,... | collective-permute-start | bytes 3145736 | tf_op jit(solution)/shard_map/down_y/ppermute | solution.py:559
  220.9 9.9 %collective-permute-start.29 = (bf16[784,1024]{1,0:T(8,128)(2,1)}, bf16[784,1024]{1,0:T(8,128)(2,1)}, u32[]{:S(2)}, u32[]{:S(2)}) collective-permute-start(bf16[784,1024]{1,0:T(8,128)(2,1)} %get-tuple-element.176.refs_4_.refs_2_), channel_id=1, source_target_pairs={{0,4},{1,5},{2,6},{3,7},{4,0},{5,1},{6,2},{7,3},{8,12},{9,13},{10,... | collective-permute-start | bytes 4816904 | tf_op jit(solution)/shard_map/zero_core/ppermute | solution.py:559
  226.0 37.7 %collective-permute-start.32 = (bf16[2,256,1024]{2,1,0:T(8,128)(2,1)}, bf16[2,256,1024]{2,1,0:T(8,128)(2,1)}, u32[]{:S(2)}, u32[]{:S(2)}) collective-permute-start(bf16[2,256,1024]{2,1,0:T(8,128)(2,1)} %get-tuple-element.186), channel_id=1, source_target_pairs={{0,8},{1,9},{2,10},{3,11},{4,12},{5,13},{6,14},{7,15},{8,0},{9,1},... | collective-permute-start | bytes 3145736 | tf_op jit(solution)/shard_map/query_x/ppermute | solution.py:559
  227.0 40.0 %collective-permute-start.33 = (bf16[128,1024]{1,0:T(8,128)(2,1)}, bf16[128,1024]{1,0:T(8,128)(2,1)}, u32[]{:S(2)}, u32[]{:S(2)}) collective-permute-start(bf16[128,1024]{1,0:T(8,128)(2,1)} %get-tuple-element.188), channel_id=1, source_target_pairs={{0,0},{1,4},{2,1},{3,5},{4,2},{5,6},{6,3},{7,7},{8,8},{9,12},{10,9... | collective-permute-start | bytes 786440 | tf_op jit(solution)/shard_map/zero_out/ppermute | solution.py:559
  230.8 37.9 %collective-permute-start.34 = (bf16[128,1024]{1,0:T(8,128)(2,1)}, bf16[128,1024]{1,0:T(8,128)(2,1)}, u32[]{:S(2)}, u32[]{:S(2)}) collective-permute-start(bf16[128,1024]{1,0:T(8,128)(2,1)} %get-tuple-element.189), channel_id=1, source_target_pairs={{0,1},{1,5},{2,0},{3,4},{4,3},{5,7},{6,2},{7,6},{8,9},{9,13},{10,8... | collective-permute-start | bytes 786440 | tf_op jit(solution)/shard_map/zero_out/ppermute | solution.py:559
  244.6 30.9 %collective-permute-start.35 = (bf16[2,128,1024]{2,1,0:T(8,128)(2,1)}, bf16[2,128,1024]{2,1,0:T(8,128)(2,1)}, u32[]{:S(2)}, u32[]{:S(2)}) collective-permute-start(bf16[2,128,1024]{2,1,0:T(8,128)(2,1)} %get-tuple-element.192), channel_id=1, source_target_pairs={{0,8},{1,9},{2,10},{3,11},{4,12},{5,13},{6,14},{7,15},{8,0},{9,1},... | collective-permute-start | bytes 1572872 | tf_op jit(solution)/shard_map/up_x/ppermute | solution.py:559
  259.9 27.2 %collective-permute-start.36 = (bf16[2,272,1024]{2,1,0:T(8,128)(2,1)}, bf16[2,272,1024]{2,1,0:T(8,128)(2,1)}, u32[]{:S(2)}, u32[]{:S(2)}) collective-permute-start(bf16[2,272,1024]{2,1,0:T(8,128)(2,1)} %get-tuple-element.195), channel_id=1, source_target_pairs={{0,8},{1,9},{2,10},{3,11},{4,12},{5,13},{6,14},{7,15},{8,0},{9,1},... | collective-permute-start | bytes 3342344 | tf_op jit(solution)/shard_map/merge_x/ppermute | solution.py:559
  263.8 26.5 %collective-permute-start.37 = (bf16[2,256,1024]{2,1,0:T(8,128)(2,1)}, bf16[2,256,1024]{2,1,0:T(8,128)(2,1)}, u32[]{:S(2)}, u32[]{:S(2)}) collective-permute-start(bf16[2,256,1024]{2,1,0:T(8,128)(2,1)} %get-tuple-element.198), channel_id=1, source_target_pairs={{0,16},{1,17},{2,18},{3,19},{4,20},{5,21},{6,22},{7,23},{8,24},{9,... | collective-permute-start | bytes 3145736 | tf_op jit(solution)/shard_map/pair_y/ppermute | solution.py:559
  266.9 33.3 %collective-permute-start.38 = (bf16[256,1024]{1,0:T(8,128)(2,1)}, bf16[256,1024]{1,0:T(8,128)(2,1)}, u32[]{:S(2)}, u32[]{:S(2)}) collective-permute-start(bf16[256,1024]{1,0:T(8,128)(2,1)} %get-tuple-element.202), channel_id=1, source_target_pairs={{0,16},{1,17},{2,18},{3,19},{4,20},{5,21},{6,22},{7,23},{8,24},{9,... | collective-permute-start | bytes 1572872 | tf_op jit(solution)/shard_map/query_y/ppermute | solution.py:559
  297.1 14.6 %collective-permute-start.39 = (bf16[272,1024]{1,0:T(8,128)(2,1)}, bf16[272,1024]{1,0:T(8,128)(2,1)}, u32[]{:S(2)}, u32[]{:S(2)}) collective-permute-start(bf16[272,1024]{1,0:T(8,128)(2,1)} %get-tuple-element.205), channel_id=1, source_target_pairs={{0,16},{1,17},{2,18},{3,19},{4,20},{5,21},{6,22},{7,23},{8,24},{9,... | collective-permute-start | bytes 1671176 | tf_op jit(solution)/shard_map/merge_y/ppermute | solution.py:559
  297.5 18.8 %collective-permute-start.40 = (bf16[256,1024]{1,0:T(8,128)(2,1)}, bf16[256,1024]{1,0:T(8,128)(2,1)}, u32[]{:S(2)}, u32[]{:S(2)}) collective-permute-start(bf16[256,1024]{1,0:T(8,128)(2,1)} %get-tuple-element.208), channel_id=1, source_target_pairs={{0,8},{1,9},{2,10},{3,11},{4,12},{5,13},{6,14},{7,15},{8,0},{9,1},... | collective-permute-start | bytes 1572872 | tf_op jit(solution)/shard_map/pair_x/ppermute | solution.py:559
  302.7 25.3 %collective-permute-start.41 = (bf16[256,1024]{1,0:T(8,128)(2,1)}, bf16[256,1024]{1,0:T(8,128)(2,1)}, u32[]{:S(2)}, u32[]{:S(2)}) collective-permute-start(bf16[256,1024]{1,0:T(8,128)(2,1)} %get-tuple-element.210.refs_0_), channel_id=1, source_target_pairs={{0,1},{3,2},{4,5},{7,6},{8,9},{11,10},{12,13},{15,14},{16,17},{19,... | collective-permute-start | bytes 1572872 | tf_op jit(solution)/shard_map/query_blocks/ppermute | solution.py:559
  304.8 61.2 %collective-permute-start.44 = (bf16[256,1024]{1,0:T(8,128)(2,1)}, bf16[256,1024]{1,0:T(8,128)(2,1)}, u32[]{:S(2)}, u32[]{:S(2)}) collective-permute-start(bf16[256,1024]{1,0:T(8,128)(2,1)} %get-tuple-element.217), channel_id=1, source_target_pairs={{0,8},{1,9},{2,10},{3,11},{4,12},{5,13},{6,14},{7,15},{8,0},{9,1},... | collective-permute-start | bytes 1572872 | tf_op jit(solution)/shard_map/result_x/ppermute | solution.py:559
  314.2 27.2 %collective-permute-start.42 = (bf16[272,1024]{1,0:T(8,128)(2,1)}, bf16[272,1024]{1,0:T(8,128)(2,1)}, u32[]{:S(2)}, u32[]{:S(2)}) collective-permute-start(bf16[272,1024]{1,0:T(8,128)(2,1)} %get-tuple-element.212.refs_0_), channel_id=1, source_target_pairs={{0,1},{3,2},{4,5},{7,6},{8,9},{11,10},{12,13},{15,14},{16,17},{19,... | collective-permute-start | bytes 1671176 | tf_op jit(solution)/shard_map/merge_blocks/ppermute | solution.py:559
  318.8 43.0 %collective-permute-start.43 = (bf16[256,1024]{1,0:T(8,128)(2,1)}, bf16[256,1024]{1,0:T(8,128)(2,1)}, u32[]{:S(2)}, u32[]{:S(2)}) collective-permute-start(bf16[256,1024]{1,0:T(8,128)(2,1)} %get-tuple-element.214.refs_0_), channel_id=1, source_target_pairs={{0,1},{3,2},{4,5},{7,6},{8,9},{11,10},{12,13},{15,14},{16,17},{19,... | collective-permute-start | bytes 1572872 | tf_op jit(solution)/shard_map/pair_blocks/ppermute | solution.py:559
  330.8 37.7 %collective-permute-start.45 = (bf16[256,1024]{1,0:T(8,128)(2,1)}, bf16[256,1024]{1,0:T(8,128)(2,1)}, u32[]{:S(2)}, u32[]{:S(2)}) collective-permute-start(bf16[256,1024]{1,0:T(8,128)(2,1)} %get-tuple-element.219.refs_0_), channel_id=1, source_target_pairs={{1,2},{2,1},{5,6},{6,5},{9,10},{10,9},{13,14},{14,13},{17,18},{18,... | collective-permute-start | bytes 1572872 | tf_op jit(solution)/shard_map/query_blocks/ppermute | solution.py:559
  344.2 36.2 %collective-permute-start.46 = (bf16[272,1024]{1,0:T(8,128)(2,1)}, bf16[272,1024]{1,0:T(8,128)(2,1)}, u32[]{:S(2)}, u32[]{:S(2)}) collective-permute-start(bf16[272,1024]{1,0:T(8,128)(2,1)} %get-tuple-element.221.refs_0_), channel_id=1, source_target_pairs={{1,2},{2,1},{5,6},{6,5},{9,10},{10,9},{13,14},{14,13},{17,18},{18,... | collective-permute-start | bytes 1671176 | tf_op jit(solution)/shard_map/merge_blocks/ppermute | solution.py:559
  364.5 19.9 %collective-permute-start.47 = (bf16[256,1024]{1,0:T(8,128)(2,1)}, bf16[256,1024]{1,0:T(8,128)(2,1)}, u32[]{:S(2)}, u32[]{:S(2)}) collective-permute-start(bf16[256,1024]{1,0:T(8,128)(2,1)} %get-tuple-element.223.refs_0_), channel_id=1, source_target_pairs={{1,2},{2,1},{5,6},{6,5},{9,10},{10,9},{13,14},{14,13},{17,18},{18,... | collective-permute-start | bytes 1572872 | tf_op jit(solution)/shard_map/pair_blocks/ppermute | solution.py:559
  371.2 24.1 %collective-permute-start.48 = (bf16[256,1024]{1,0:T(8,128)(2,1)}, bf16[256,1024]{1,0:T(8,128)(2,1)}, u32[]{:S(2)}, u32[]{:S(2)}) collective-permute-start(bf16[256,1024]{1,0:T(8,128)(2,1)} %get-tuple-element.225.refs_0_), channel_id=1, source_target_pairs={{1,0},{2,3},{5,4},{6,7},{9,8},{10,11},{13,12},{14,15},{17,16},{18,... | collective-permute-start | bytes 1572872 | tf_op jit(solution)/shard_map/query_blocks/ppermute | solution.py:559
  372.5 47.7 %collective-permute-start.50 = (bf16[128,1024]{1,0:T(8,128)(2,1)}, bf16[128,1024]{1,0:T(8,128)(2,1)}, u32[]{:S(2)}, u32[]{:S(2)}) collective-permute-start(bf16[128,1024]{1,0:T(8,128)(2,1)} %get-tuple-element.229), channel_id=1, source_target_pairs={{0,0},{1,4},{2,1},{3,5},{4,2},{5,6},{6,3},{7,7},{8,8},{9,12},{10,9... | collective-permute-start | bytes 786440 | tf_op jit(solution)/shard_map/result_out/ppermute | solution.py:559
  376.1 44.1 %collective-permute-start.51 = (bf16[128,1024]{1,0:T(8,128)(2,1)}, bf16[128,1024]{1,0:T(8,128)(2,1)}, u32[]{:S(2)}, u32[]{:S(2)}) collective-permute-start(bf16[128,1024]{1,0:T(8,128)(2,1)} %get-tuple-element.230), channel_id=1, source_target_pairs={{0,1},{1,5},{2,0},{3,4},{4,3},{5,7},{6,2},{7,6},{8,9},{9,13},{10,8... | collective-permute-start | bytes 786440 | tf_op jit(solution)/shard_map/result_out/ppermute | solution.py:559
  383.1 34.3 %collective-permute-start.49 = (bf16[272,1024]{1,0:T(8,128)(2,1)}, bf16[272,1024]{1,0:T(8,128)(2,1)}, u32[]{:S(2)}, u32[]{:S(2)}) collective-permute-start(bf16[272,1024]{1,0:T(8,128)(2,1)} %get-tuple-element.227.refs_0_), channel_id=1, source_target_pairs={{1,0},{2,3},{5,4},{6,7},{9,8},{10,11},{13,12},{14,15},{17,16},{18,... | collective-permute-start | bytes 1671176 | tf_op jit(solution)/shard_map/merge_blocks/ppermute | solution.py:559
  387.1 39.9 %collective-permute-start.52 = (bf16[256,1024]{1,0:T(8,128)(2,1)}, bf16[256,1024]{1,0:T(8,128)(2,1)}, u32[]{:S(2)}, u32[]{:S(2)}) collective-permute-start(bf16[256,1024]{1,0:T(8,128)(2,1)} %get-tuple-element.236.refs_0_), channel_id=1, source_target_pairs={{1,0},{2,3},{5,4},{6,7},{9,8},{10,11},{13,12},{14,15},{17,16},{18,... | collective-permute-start | bytes 1572872 | tf_op jit(solution)/shard_map/pair_blocks/ppermute | solution.py:559
  (38 other events, 164.5 us)
Sparse Core Ops, SparseCore 0:
  16.3 81.6 all-gather.2
  278.4 121.1 all-reduce.3

commit v2 on v1

v2 whole, which is shorter than its diff:
```python
import functools
import itertools

import jax
import jax.numpy as jnp
from jax import lax
from jax.experimental import pallas as pl
from jax.experimental.pallas import tpu as pltpu
from jax.sharding import PartitionSpec as P

D = 1024
HEADS = 16
HEAD_DIM = 64
MB = 2
PAIR = 2 * HEAD_DIM
CHIPS = 4
NEG_BIG = -1e30
EPS = 1e-6
AXES = ("fsdp", "blk")
BF = jnp.bfloat16
F32 = jnp.float32
MEGA = 1024 * 1024
SMALL, LARGE, HUGE = 20 * MEGA, 30 * MEGA, 60 * MEGA

MERGE_ROWS = 256
OWN_ROWS = 128
HIDDEN_ROWS = 512
GAIN_ROWS = 16


def dot(left, right):
    return jnp.dot(left, right, preferred_element_type=F32)


def dot_rows(left, right):
    return lax.dot_general(left, right, (((0,), (0,)), ((), ())), preferred_element_type=F32)


def dot_cols(left, right):
    return lax.dot_general(left, right, (((1,), (1,)), ((), ())), preferred_element_type=F32)


def norm_scale(hidden):
    return lax.rsqrt(jnp.mean(hidden * hidden, -1, keepdims=True) + EPS)


def norm_back(grad, hidden, gain):
    scale = norm_scale(hidden)
    weighted = grad * gain
    inner = jnp.mean(weighted * hidden, -1, keepdims=True)
    back = scale * weighted - hidden * (scale * scale * scale * inner)
    gain_grad = jnp.sum(grad * hidden * scale, 0, keepdims=True)
    return back, gain_grad


def swap_halves(tensor):
    lane = lax.broadcasted_iota(jnp.int32, tensor.shape, 1)
    low = (lane % HEAD_DIM) < HEAD_DIM // 2
    return jnp.where(
        low,
        pltpu.roll(tensor, PAIR - HEAD_DIM // 2, 1),
        pltpu.roll(tensor, HEAD_DIM // 2, 1),
    )


def turn(tensor, cosine, sine):
    return tensor * cosine + swap_halves(tensor) * sine


def aligned(at, size):
    return pl.ds(pl.multiple_of(at * size, size), size)


def stacked(parts):
    return jnp.concatenate([part[...] for part in parts], 0)


def summed(parts):
    return functools.reduce(jnp.add, [part[...].astype(F32) for part in parts])


def owner_of(index, chip, other):
    return 2 * index[chip] + (1 - index[4] if other else index[4])


def merge_kernel(index, left, right, *refs):
    weights = refs[: 2 * CHIPS]
    hidden_ref, cot_ref, joined_ref, pre_ref, mid_ref = refs[2 * CHIPS :]
    rows = left.shape[0]
    joined_ref[:rows] = left[:, : 2 * D]
    joined_ref[rows:] = right[:, : 2 * D]
    total = None
    for at, weight in enumerate(weights):
        mine = aligned(owner_of(index, at % CHIPS, at >= CHIPS), MERGE_ROWS)
        part = dot(joined_ref[:, mine], weight[:MERGE_ROWS])
        total = part if total is None else total + part
        mine = aligned(owner_of(index, at % CHIPS, at >= CHIPS), OWN_ROWS)
        gains = weight[MERGE_ROWS:, :OWN_ROWS].astype(F32)
        pre_ref[:, mine] = gains[0:1]
        mid_ref[:, mine] = gains[1:2]
    hidden_ref[...] = total
    cot_ref[:rows] = left[:, 2 * D :]
    cot_ref[rows:] = right[:, 2 * D :]


def fetch(array, at, held, sem):
    copies = [
        pltpu.make_async_copy(
            array.at[:, :, (at + which) * D : (at + which + 1) * D], held.at[which], sem.at[which]
        )
        for which in range(held.shape[0])
    ]
    for copy in copies:
        copy.start()
    return copies


def project_kernel(
    index, hidden, gain, gathered, cosine, sine, cot, act_ref, query_ref, pair_ref, cot_ref, held, sem
):
    copies = fetch(gathered, 0, held, sem)
    cot_ref[...] = cot[...]
    act = (hidden[...] * norm_scale(hidden[...]) * gain[...]).astype(BF)
    act_ref[...] = act
    for which, copy in enumerate(copies):
        copy.wait()
        for part in range(CHIPS):
            wide = slice(part * 2 * PAIR, (part + 1) * 2 * PAIR)
            united = dot(act, held[which, :, :, wide].reshape(D, 2 * PAIR))
            if which == 2:
                pair_ref[1, :, wide] = united.astype(BF)
                continue
            for block in range(2):
                cols = slice(block * PAIR, (block + 1) * PAIR)
                turned = turn(united[:, cols], cosine[...], sine[...]).astype(BF)
                cols = slice((2 * part + block) * PAIR, (2 * part + block + 1) * PAIR)
                if which == 0:
                    query_ref[:, cols] = turned * HEAD_DIM ** (-0.5)
                else:
                    pair_ref[0, :, cols] = turned


def head_mask(shape, head):
    lane = lax.broadcasted_iota(jnp.int32, shape, 1)
    return (lane // HEAD_DIM) == head


def attend_kernel(pieces, index, *refs):
    query, query_seg, key_segs = refs[:3]
    pairs = refs[3 : 3 + pieces]
    act_first, gathered, hidden_zero, gain = refs[3 + pieces : 7 + pieces]
    both_ref, hidden_ref, act_ref, probs_ref, held, sem = refs[7 + pieces :]
    weight = pltpu.make_async_copy(gathered.at[:, :, 3 * D :], held, sem)
    allowed = [key_segs[piece] == query_seg[...] for piece in range(pieces)]
    step = pl.program_id(0)

    @pl.when(step == 0)
    def _():
        weight.start()
        both_ref[0] = act_first[...]

    wide = query.shape[1]
    for block in range(wide // PAIR):
        cols = slice(block * PAIR, (block + 1) * PAIR)
        query_block = query[:, cols]
        key_blocks = [pair[0, :, cols] for pair in pairs]
        value_blocks = [pair[1, :, cols] for pair in pairs]
        mixed = None
        for head in range(2):
            mask = head_mask(query_block.shape, head)
            one_query = jnp.where(mask, query_block, jnp.zeros_like(query_block))
            scores = [
                jnp.where(a, dot_cols(key, one_query), NEG_BIG)
                for key, a in zip(key_blocks, allowed)
            ]
            peak = functools.reduce(jnp.maximum, [jnp.max(s, 0, keepdims=True) for s in scores])
            expo = [jnp.exp(s - peak) for s in scores]
            inverse = 1.0 / functools.reduce(jnp.add, [jnp.sum(e, 0, keepdims=True) for e in expo])
            for piece in range(pieces):
                probs = (expo[piece] * inverse).astype(BF)
                probs_ref[2 * block + head, piece] = probs
                value = value_blocks[piece]
                part = dot_rows(jnp.where(mask, value, jnp.zeros_like(value)), probs)
                mixed = part if mixed is None else mixed + part
        both_ref[1, :, aligned(step * (wide // PAIR) + block, PAIR)] = mixed.T.astype(BF)

    @pl.when(step == pl.num_programs(0) - 1)
    def _():
        weight.wait()
        hidden = hidden_zero[...] + dot(both_ref[1], held[...].reshape(D, D))
        hidden_ref[...] = hidden
        act_ref[...] = (hidden * norm_scale(hidden) * gain[...]).astype(BF)


GELU_ROOT = 0.7978845608028654
GELU_CUBE = 0.044715


def feed_kernel(index, act, cot, w_up, w_down, second_ref, activ_ref, upper_ref):
    cut = 256
    for at in range(w_up.shape[1] // cut):
        cols = slice(at * cut, (at + 1) * cut)
        upper = dot(act[...], w_up[:, cols])
        square = upper * upper
        bent = jnp.tanh(GELU_ROOT * upper * (1.0 + GELU_CUBE * square))
        half = 0.5 * (1.0 + bent)
        activ_ref[:, cols] = (upper * half).astype(BF)
        slope = half + 0.5 * upper * (1.0 - bent * bent) * (
            GELU_ROOT * (1.0 + 3.0 * GELU_CUBE * square)
        )
        upper_ref[:, cols] = (dot_cols(cot[...], w_down[cols, :]) * slope).astype(BF)
    second_ref[...] = dot_cols(upper_ref[...], w_up[...]).astype(BF)


def result_parts_kernel(index, *refs):
    activs, w_down = refs[:CHIPS], refs[CHIPS]
    for activ, out_ref in zip(activs, refs[CHIPS + 1 :]):
        out_ref[...] = dot(activ[...], w_down[...]).astype(BF)


def down_grad_kernel(index, *refs):
    activs, cots = stacked(refs[:CHIPS]), stacked(refs[CHIPS : 2 * CHIPS])
    keep_ref, send_ref = refs[2 * CHIPS :]
    down = [
        dot_rows(activs[:, at * HIDDEN_ROWS : (at + 1) * HIDDEN_ROWS], cots).astype(BF)
        for at in range(2)
    ]
    even = index[4] == 0
    keep_ref[...] = jnp.where(even, down[0], down[1])
    send_ref[...] = jnp.where(even, down[1], down[0])


def up_grad_kernel(index, *refs):
    acts, uppers = stacked(refs[:CHIPS]), stacked(refs[CHIPS : 2 * CHIPS])
    keep_ref, send_ref = refs[2 * CHIPS :]
    even = index[4] == 0
    for chip in range(CHIPS):
        rows = slice(chip * 2 * OWN_ROWS, (chip + 1) * 2 * OWN_ROWS)
        total = dot_rows(acts[:, rows], uppers).astype(BF)
        keep_ref[chip] = jnp.where(even, total[:OWN_ROWS], total[OWN_ROWS:])
        send_ref[chip] = jnp.where(even, total[OWN_ROWS:], total[:OWN_ROWS])


def feed_send_kernel(index, expander, up_ref):
    for chip in range(CHIPS):
        up_ref[chip] = expander[:, chip * D : (chip + 1) * D]


def three_kernel(index, *refs):
    for array, out_ref in zip(refs[:3], refs[3:]):
        out_ref[...] = array[...]


def rest_kernel(index):
    pass


def copy_kernel(index, array, out_ref):
    out_ref[...] = array[...]


def feed_total_kernel(index, down, up, reducer_ref, expander_ref):
    reducer_ref[...] = down[...].astype(F32)
    for chip in range(CHIPS):
        expander_ref[:, chip * D : (chip + 1) * D] = up[chip].astype(F32)


def up_kernel(index, mine, other, out_ref):
    for chip in range(CHIPS):
        out_ref[2 * chip + index[4]] = mine[chip]
        out_ref[2 * chip + 1 - index[4]] = other[chip]


def down_kernel(index, mine, other, out_ref):
    out_ref[index[4]] = mine[...]
    out_ref[1 - index[4]] = other[...]


def attend_back_kernel(pieces, index, *refs):
    query, probs_ref = refs[:2]
    pairs = refs[2 : 2 + pieces]
    at = 2 + pieces
    gathered, hidden_one, cot, gain, cosine, sine = refs[at : at + 6]
    seconds = refs[at + 6 : at + 8]
    at += 8
    one_ref, low_ref, gain_ref, query_ref = refs[at : at + 4]
    pair_refs = refs[at + 4 : at + 4 + pieces]
    held, sem = refs[at + 4 + pieces :]
    swap_ref = pair_refs[1]
    step = pl.program_id(0)
    weight = pltpu.make_async_copy(gathered.at[:, :, 3 * D :], held, sem)

    @pl.when(step == 0)
    def _():
        weight.start()
        back, gain_grad = norm_back(summed(seconds), hidden_one[...], gain[...])
        one = cot[...].astype(F32) + back
        one_ref[...] = one
        gain_ref[...] = gain_grad
        low_ref[...] = one.astype(BF)
        weight.wait()

    wide = query.shape[1]
    swap_ref[3] = low_ref[:, aligned(step, wide)]
    attended_grad = dot_cols(low_ref[...], held.reshape(D, D)[aligned(step, wide), :]).astype(BF)
    for block in range(wide // PAIR):
        cols = slice(block * PAIR, (block + 1) * PAIR)
        query_block = query[:, cols]
        grad_block = attended_grad[:, cols]
        key_blocks = [pair[0, :, cols] for pair in pairs]
        value_blocks = [pair[1, :, cols] for pair in pairs]
        query_grad = None
        key_grads = [None] * pieces
        value_grads = [None] * pieces
        for head in range(2):
            mask = head_mask(query_block.shape, head)
            one_query = jnp.where(mask, query_block, jnp.zeros_like(query_block))
            one_grad = jnp.where(mask, grad_block, jnp.zeros_like(grad_block))
            low = [probs_ref[2 * block + head, piece] for piece in range(pieces)]
            probs = [p.astype(F32) for p in low]
            probs_grad = [dot_cols(value, one_grad) for value in value_blocks]
            delta = functools.reduce(
                jnp.add,
                [jnp.sum(p * g, 0, keepdims=True) for p, g in zip(probs, probs_grad)],
            )
            for piece in range(pieces):
                scores_grad = (probs[piece] * (probs_grad[piece] - delta)).astype(BF)
                key = key_blocks[piece]
                part = dot_rows(jnp.where(mask, key, jnp.zeros_like(key)), scores_grad)
                query_grad = part if query_grad is None else query_grad + part
                key_part = dot(scores_grad, one_query)
                value_part = dot(low[piece], one_grad)
                if head:
                    key_part += key_grads[piece]
                    value_part += value_grads[piece]
                key_grads[piece] = key_part
                value_grads[piece] = value_part
        query_grad = query_grad.T * HEAD_DIM ** (-0.5)
        query_grad = turn(query_grad, cosine[0], -sine[0]).astype(BF)
        query_ref[:, cols] = query_grad
        swap_ref[2, :, cols] = query_grad
        for piece in range(pieces):
            turned = turn(key_grads[piece], cosine[piece], -sine[piece])
            pair_refs[piece][0, :, cols] = turned.astype(BF)
            pair_refs[piece][1, :, cols] = value_grads[piece].astype(BF)


def united_kernel(pieces, index, *refs):
    query_grad, mid = refs[:2]
    pairs = refs[2 : 2 + pieces]
    at = 2 + pieces
    gathered, hidden_zero, one_grad, gain = refs[at : at + 4]
    swap_ref, held, sem = refs[at + 4 :]
    copies = fetch(gathered, 0, held, sem)
    tok = query_grad.shape[0]
    place = lambda which: slice(which * tok, (which + 1) * tok)
    for which in range(2):
        total = functools.reduce(jnp.add, [part[which].astype(F32) for part in pairs])
        swap_ref[place(which)] = total.astype(BF)
    grads = (query_grad[...], swap_ref[place(0)], swap_ref[place(1)])
    grad = None
    for which, copy in enumerate(copies):
        copy.wait()
        part = dot_cols(grads[which], held[which].reshape(D, D))
        grad = part if grad is None else grad + part
    back, gain_grad = norm_back(grad, hidden_zero[...], gain[...])
    swap_ref[place(2)] = (one_grad[...] + back).astype(BF)
    rest = jnp.zeros((GAIN_ROWS - 2, D), F32)
    swap_ref[3 * tok :] = jnp.concatenate([gain_grad, mid[...], rest], 0).astype(BF)


def of_core(ref, index, size):
    return jnp.concatenate(
        [ref[:, aligned(2 * index[chip] + index[4], size)] for chip in range(CHIPS)], 1
    )


def put_slabs(total, rows, at, order, keep_ref, send_ref):
    for ref, chips in ((keep_ref, order[:2]), (send_ref, order[2:])):
        for place, chip in enumerate(chips):
            ref[place, at : at + rows] = total[chip * rows : (chip + 1) * rows].astype(BF)


X_FIRST = (0, 2, 1, 3)
Y_FIRST = (0, 1, 2, 3)


def query_grad_kernel(index, both, both_c, grad, low, swapped, keep_ref, send_ref):
    rights = ((grad[...], swapped[2]), (low[...], swapped[3]))
    for which, right in enumerate(rights):
        left = [of_core(part.at[which], index, OWN_ROWS) for part in (both, both_c)]
        total = dot_rows(jnp.concatenate(left, 0), jnp.concatenate(right, 0))
        put_slabs(total, OWN_ROWS, which * OWN_ROWS, X_FIRST, keep_ref, send_ref)


def pair_grad_kernel(index, both, both_c, own, swapped, keep_ref, send_ref):
    tok = both.shape[1]
    left = jnp.concatenate([of_core(part.at[0], index, OWN_ROWS) for part in (both, both_c)], 0)
    for which in range(2):
        place = slice(which * tok, (which + 1) * tok)
        total = dot_rows(left, jnp.concatenate([own[place], swapped[place]], 0))
        put_slabs(total, OWN_ROWS, which * OWN_ROWS, Y_FIRST, keep_ref, send_ref)


def merge_grad_kernel(index, joined, joined_c, own, swapped, keep_ref, send_ref):
    tok = joined.shape[0]
    both = jnp.concatenate(
        [of_core(part, index, MERGE_ROWS) for part in (joined, joined_c)], 0
    )
    low = slice(2 * tok, 3 * tok)
    total = dot_rows(both, jnp.concatenate([own[low], swapped[low]], 0))
    put_slabs(total, MERGE_ROWS, 0, X_FIRST, keep_ref, send_ref)
    gains = own[3 * tok :].astype(F32) + swapped[3 * tok :].astype(F32)
    keep_ref[:, MERGE_ROWS:] = jnp.zeros((2, GAIN_ROWS, D), BF)
    send_ref[:, MERGE_ROWS:] = jnp.zeros((2, GAIN_ROWS, D), BF)
    for ref, chips in ((keep_ref, X_FIRST[:2]), (send_ref, X_FIRST[2:])):
        for place, chip in enumerate(chips):
            owner = 2 * index[chip] + index[4]
            lane = lax.broadcasted_iota(jnp.int32, gains.shape, 1)
            mine = jnp.where(lane // OWN_ROWS == owner, gains, 0.0)
            chosen = functools.reduce(
                jnp.add,
                [mine[:, at * OWN_ROWS : (at + 1) * OWN_ROWS] for at in range(D // OWN_ROWS)],
            )
            ref[place, MERGE_ROWS:, :OWN_ROWS] = chosen.astype(BF)


def joined_grad_kernel(index, first, second, *refs):
    weights = refs[: 2 * CHIPS]
    rows = first.shape[0]
    low = jnp.concatenate([first[...], second[...]], 0)
    micro = index[5]
    for at, weight in enumerate(weights):
        grad = dot_cols(low, weight[:MERGE_ROWS])
        owner = owner_of(index, at % CHIPS, at >= CHIPS)
        cols = aligned(owner % CHIPS, MERGE_ROWS)
        for half, out_ref in enumerate(refs[2 * CHIPS :]):

            @pl.when(owner // CHIPS == half)
            def _():
                out_ref[micro, :, cols] = grad[:rows]
                out_ref[1 - micro, :, cols] = grad[rows:]


def sum_kernel(index, *refs):
    refs[-1][...] = summed(refs[:-1])


def add_kernel(index, *refs):
    refs[-1][...] = summed(refs[:-1]).astype(BF)


def add_two_kernel(index, keep, got, own_ref, other_ref):
    own_ref[...] = summed((keep.at[0], got.at[0])).astype(BF)
    other_ref[...] = summed((keep.at[1], got.at[1])).astype(BF)


def stack_kernel(index, *refs):
    for at, part in enumerate(refs[:-1]):
        refs[-1][at] = part[...]


def result_kernel(index, *refs):
    left, right = refs[-2:]
    rows = left.shape[0]
    total = summed(refs[:-2])
    left[...] = total[:rows].astype(BF)
    right[...] = total[rows:].astype(BF)


def zero_kernel(index, swapped, left_ref, right_ref):
    rows = left_ref.shape[0]
    left_ref[...] = swapped[4 * rows : 5 * rows]
    right_ref[...] = swapped[5 * rows : 6 * rows]


def by_micro_kernel(index, first, second, out_ref):
    out_ref[index[5]] = first[...]
    out_ref[1 - index[5]] = second[...]


def total_kernel(index, query, merge, pair, merger_ref, projector_ref, combiner_ref, gain_ref):
    merger_ref[...] = merge[:MERGE_ROWS].astype(F32)
    gain_ref[...] = merge[MERGE_ROWS : MERGE_ROWS + 16, :OWN_ROWS].astype(F32)[:8]
    combiner_ref[...] = query[OWN_ROWS:].astype(F32)
    parts = (query[:OWN_ROWS], pair[:OWN_ROWS], pair[OWN_ROWS:])
    for which, part in enumerate(parts):
        projector_ref[:, which * D : (which + 1) * D] = part.astype(F32)


def call(kernel, vmem, grid, in_specs, out_specs, out_shape, scratch, index, token, *arrays):
    scalars = 0 if index is None else 1

    def passing(*refs):
        index_ref, refs = (refs[0], refs[1:]) if scalars else (None, refs)
        inputs = 1 + len(in_specs)
        kernel(index_ref, *refs[1:inputs], *refs[inputs + 1 :])

    anywhere = pl.BlockSpec(memory_space=pl.ANY)
    return pl.pallas_call(
        passing,
        grid_spec=pltpu.PrefetchScalarGridSpec(
            num_scalar_prefetch=scalars,
            grid=grid,
            in_specs=[anywhere] + in_specs,
            out_specs=[anywhere] + out_specs,
            scratch_shapes=scratch,
        ),
        out_shape=[jax.ShapeDtypeStruct(token.shape, token.dtype)] + out_shape,
        input_output_aliases={scalars: 0},
        name=getattr(kernel, "func", kernel).__name__,
        compiler_params=pltpu.CompilerParams(
            dimension_semantics=("arbitrary",) * len(grid), vmem_limit_bytes=vmem
        ),
        cost_estimate=pl.CostEstimate(flops=10**12, bytes_accessed=0, transcendentals=0),
    )(*([index] if scalars else []), token, *arrays)


def shape(*dims, dtype=BF):
    return jax.ShapeDtypeStruct(dims, dtype)


def whole(*dims):
    return pl.BlockSpec(dims, lambda *_: (0,) * len(dims))


def local(
    frames,
    skipped,
    lengths,
    merger,
    projector,
    combiner,
    expander,
    reducer,
    prenorm,
    midnorm,
    cotangent,
):
    rows = frames.shape[1]
    tok = 2 * rows
    blocks = lax.axis_size("blk")
    fsdp = lax.axis_size("fsdp")
    quarter = blocks // 4
    pieces = blocks // 2
    stream = rows * blocks

    me = lax.axis_index("fsdp")
    spot = lax.axis_index("blk")
    core = me % 2
    chip = me // 2
    unit = spot // quarter
    micro = unit // 2
    source_core = unit % 2
    half = (spot % quarter) * 2 + core

    def send(array, route, name="send"):
        pairs = []
        for y, x, c, b in itertools.product(range(2), range(2), range(2), range(blocks)):
            target = route(y, x, c, b)
            if target is not None:
                ty, tx, tc, tb = target
                pairs.append((((y * 2 + x) * 2 + c) * blocks + b, ((ty * 2 + tx) * 2 + tc) * blocks + tb))
        with jax.named_scope(name):
            return lax.ppermute(array, AXES, pairs)

    to_x = lambda y, x, c, b: (y, 1 - x, c, b)
    to_y = lambda y, x, c, b: (1 - y, x, c, b)
    to_diagonal = lambda y, x, c, b: (1 - y, 1 - x, c, b)
    to_core = lambda y, x, c, b: (y, x, 1 - c, b)
    around = (to_x, to_y, to_diagonal)
    over_plane = (to_x, to_diagonal, to_y)

    def holder(micro_at, c, pair):
        return (2 * micro_at + c) * quarter + pair // 2, pair % 2

    def inward(other):
        def route(y, x, c, b):
            tb, tc = holder((b + other) % 2, c, b // 2)
            return (y, x, tc, tb)

        return route

    def outward(other):
        forward = inward(other)
        table = {}
        for y, x, c, b in itertools.product(range(2), range(2), range(2), range(blocks)):
            table[forward(y, x, c, b)] = (y, x, c, b)
        return lambda *at: table[at]

    def among(by):
        def route(y, x, c, b):
            at = ((b % quarter) * 2 + c) ^ by
            return (y, x, at % 2, (b // quarter) * quarter + at // 2)

        return route

    def take_in(pick, name):
        return tuple(send(pick((spot + other) % 2), inward(other), name) for other in range(2))

    gathered = lax.all_gather(jnp.concatenate([projector, combiner], 1), "fsdp", axis=0)

    gain_rows = jnp.pad(jnp.stack([prenorm, midnorm]), ((0, GAIN_ROWS - 2), (0, D - OWN_ROWS)))
    merger_own = jnp.concatenate([merger, gain_rows], 0)
    mergers = [merger_own] + [send(merger_own, route, "merger_around") for route in around]
    mergers += [send(part, to_core, "merger_core") for part in mergers]

    left, right = take_in(
        lambda m: jnp.concatenate([frames[m], skipped[m], cotangent[m]], -1), "tokens_in"
    )
    other_lengths = send(lengths, to_core, "lengths_core")

    mine = jnp.where(source_core == core, lengths, other_lengths)[:, 0]
    row_lengths = jnp.where(micro == 0, mine[0], mine[1])
    ends = jnp.cumsum(row_lengths)
    within = jnp.arange(rows, dtype=jnp.int32)

    def layout(at):
        offsets = jnp.concatenate(
            [(2 * at + micro) * rows + within, (2 * at + 1 - micro) * rows + within]
        )
        before = (ends[None, :] <= offsets[:, None]).astype(jnp.int32)
        return jnp.sum(before, 1), offsets - jnp.sum(before * row_lengths[None, :], 1)

    layouts = [layout(half ^ by) for by in range(pieces)]
    query_seg = layouts[0][0][None]
    key_segs = jnp.stack([segment for segment, _ in layouts])[:, :, None]
    inverse = 10000.0 ** (-jnp.arange(HEAD_DIM // 2, dtype=F32) * 2.0 / HEAD_DIM)
    positions = jnp.stack([position for _, position in layouts]).astype(F32)
    angles = positions[:, :, None] * inverse
    cosine = jnp.tile(jnp.cos(angles), (1, 1, 4))
    sine = jnp.sin(angles)
    sine = jnp.concatenate([-sine, sine, -sine, sine], -1)

    index = jnp.stack(
        [chip, chip ^ 1, chip ^ 2, chip ^ 3, core, spot % 2, spot, spot]
    ).astype(jnp.int32)
    last_token = [jnp.zeros((8, 128), F32)]

    def run(
        kernel, grid, in_specs, out_specs, out_shape, scratch, *arrays, vmem=SMALL, scalars=index
    ):
        last_token[0], *results = call(
            kernel,
            vmem,
            (grid,) if grid else (),
            in_specs,
            out_specs,
            out_shape,
            scratch,
            scalars,
            last_token[0],
            *arrays,
        )
        return results[0] if len(results) == 1 else results

    def rest():
        run(rest_kernel, 0, [], [], [], [], scalars=None)

    def meet():
        last_token[0] = send(last_token[0], to_core, "order")

    def simple(kernel, outs, *arrays, scalars=index):
        held = pl.BlockSpec(memory_space=pltpu.VMEM)
        return run(
            kernel,
            0,
            [held] * len(arrays),
            [held] * len(outs),
            outs,
            [],
            *arrays,
            scalars=scalars,
        )

    def add(*arrays):
        return simple(add_kernel, [shape(*arrays[0].shape)], *arrays, scalars=None)

    def first_step(keep, got):
        return simple(add_two_kernel, [shape(*keep.shape[1:])] * 2, keep, got, scalars=None)

    wide = 2 * OWN_ROWS
    cols_at = lambda height, width: pl.BlockSpec((height, width), lambda s, *_: (0, s))
    cols_of = lambda height, width: pl.BlockSpec((height, width), lambda s, i: (0, i[s]))
    table = whole(tok, PAIR)
    tables = whole(pieces, tok, PAIR)

    down_c = send(reducer, to_core, "w_down_core")
    chunk = expander.shape[1] // CHIPS
    w_down = simple(down_kernel, [shape(2, HIDDEN_ROWS, D)], reducer, down_c).reshape(chunk, D)
    hidden_zero, cot, joined, gain_pre, gain_mid = simple(
        merge_kernel,
        [shape(tok, D, dtype=F32), shape(tok, D), shape(tok, 2 * D)]
        + [shape(1, D, dtype=F32)] * 2,
        left,
        right,
        *mergers,
    )
    joined_c = send(joined, to_core, "joined_core")

    groups = [[c + 2 * at for at in range(CHIPS)] for c in range(2)]
    swap_chunks = lambda parts: lax.all_to_all(
        parts, "fsdp", 0, 0, axis_index_groups=groups, tiled=True
    )
    up_swapped = swap_chunks(
        simple(feed_send_kernel, [shape(CHIPS, OWN_ROWS, chunk)], expander, scalars=None)
    )
    fetched = pl.BlockSpec(memory_space=pltpu.HBM)
    act_first, query, pair, cot_again = run(
        project_kernel,
        1,
        [whole(tok, D), whole(1, D), fetched, table, table, whole(tok, D)],
        [whole(tok, D), whole(tok, D), whole(2, tok, D), whole(tok, D)],
        [shape(tok, D), shape(tok, D), shape(2, tok, D), shape(tok, D)],
        [pltpu.VMEM((3, fsdp, OWN_ROWS, D), BF), pltpu.SemaphoreType.DMA((3,))],
        hidden_zero,
        gain_pre,
        gathered,
        cosine[0],
        sine[0],
        cot,
        vmem=LARGE,
        scalars=None,
    )
    cots = [send(cot_again, route, "cot_around") for route in over_plane]
    up_mine = simple(copy_kernel, [shape(CHIPS, OWN_ROWS, chunk)], up_swapped, scalars=None)
    up_c = send(up_mine, to_core, "w_up_core")
    pairs = [pair] + [send(pair, among(by), "pair_core") for by in range(1, pieces)]
    steps, vmem = (1, LARGE) if pieces == 2 else (CHIPS * 2, HUGE)
    head_cols = cols_at(tok, D // steps)
    pair_cols = lambda count: pl.BlockSpec((count, tok, D // steps), lambda s, *_: (0, 0, s))
    probs_spec = pl.BlockSpec((HEADS // steps, pieces, tok, tok), lambda s, *_: (s, 0, 0, 0))
    combiner_held = [pltpu.VMEM((fsdp, OWN_ROWS, D), BF), pltpu.SemaphoreType.DMA]
    attended, hidden_one, act_second, probs = run(
        functools.partial(attend_kernel, pieces),
        steps,
        [head_cols, whole(1, tok), whole(pieces, tok, 1)]
        + [pair_cols(2)] * pieces
        + [whole(tok, D), fetched, whole(tok, D), whole(1, D)],
        [whole(2, tok, D), whole(tok, D), whole(tok, D), probs_spec],
        [
            shape(2, tok, D),
            shape(tok, D, dtype=F32),
            shape(tok, D),
            shape(HEADS, pieces, tok, tok),
        ],
        combiner_held,
        query,
        query_seg,
        key_segs,
        *pairs,
        act_first,
        gathered,
        hidden_zero,
        gain_mid,
        vmem=vmem,
        scalars=None,
    )
    acts = [act_second] + [send(act_second, route, "act_around") for route in over_plane]
    attended_c = send(attended, to_core, "attended_core")
    w_up = simple(up_kernel, [shape(fsdp, OWN_ROWS, chunk)], up_mine, up_c).reshape(D, chunk)
    cots = [cot] + simple(three_kernel, [shape(tok, D)] * 3, *cots, scalars=None)

    fed = [
        simple(
            feed_kernel,
            [shape(tok, D), shape(tok, chunk), shape(tok, chunk)],
            act,
            grad,
            w_up,
            w_down,
            scalars=None,
        )
        for act, grad in zip(acts, cots)
    ]
    seconds = [fed[0][0]] + [
        send(part[0], route, "second_around") for part, route in zip(fed[1:], over_plane)
    ]
    activs = [part[1] for part in fed]
    down_keep, down_send = simple(
        down_grad_kernel, [shape(HIDDEN_ROWS, D)] * 2, *activs, *cots
    )
    down_got = send(down_send, to_core, "down_core")
    up_keep, up_send = simple(
        up_grad_kernel, [shape(CHIPS, OWN_ROWS, chunk)] * 2, *acts, *[part[2] for part in fed]
    )
    up_got = send(up_send, to_core, "up_core")

    second = simple(
        sum_kernel, [shape(tok, D, dtype=F32)], seconds[0], seconds[1], scalars=None
    )
    second = simple(sum_kernel, [shape(tok, D, dtype=F32)], second, seconds[2], scalars=None)

    steps = CHIPS if pieces == 2 else 2 * CHIPS
    head_cols = cols_at(tok, D // steps)
    pair_cols = lambda count: pl.BlockSpec((count, tok, D // steps), lambda s, *_: (0, 0, s))
    probs_spec = pl.BlockSpec((HEADS // steps, pieces, tok, tok), lambda s, *_: (s, 0, 0, 0))
    counts = [4 if by == 1 else 2 for by in range(pieces)]
    back = run(
        functools.partial(attend_back_kernel, pieces),
        steps,
        [head_cols, probs_spec]
        + [pair_cols(2)] * pieces
        + [fetched, whole(tok, D), whole(tok, D), whole(1, D)]
        + [tables, tables]
        + [whole(tok, D)] * 2,
        [whole(tok, D), whole(tok, D), whole(1, D), head_cols] + [pair_cols(n) for n in counts],
        [
            shape(tok, D, dtype=F32),
            shape(tok, D),
            shape(1, D, dtype=F32),
            shape(tok, D),
        ]
        + [shape(n, tok, D) for n in counts],
        combiner_held,
        query,
        probs,
        *pairs,
        gathered,
        hidden_one,
        cot,
        gain_mid,
        cosine,
        sine,
        second,
        seconds[3],
        vmem=vmem,
        scalars=None,
    )
    one_grad, one_low, mid_grad, query_grad = back[:4]
    pair_grads = [back[4]] + [
        send(part, among(by), "pair_grads_core") for by, part in enumerate(back[5:], 1)
    ]
    reversed_blocks = [list(reversed(range(blocks)))]
    down_total = lax.psum(add(down_keep, down_got), "blk", axis_index_groups=reversed_blocks)
    swapped = run(
        functools.partial(united_kernel, pieces),
        1,
        [whole(tok, D), whole(1, D)]
        + [whole(n, tok, D) for n in counts]
        + [fetched, whole(tok, D), whole(tok, D), whole(1, D)],
        [whole(3 * tok + GAIN_ROWS, D)],
        [shape(3 * tok + GAIN_ROWS, D)],
        [pltpu.VMEM((3, fsdp, OWN_ROWS, D), BF), pltpu.SemaphoreType.DMA((3,))],
        query_grad,
        mid_grad,
        *pair_grads,
        gathered,
        hidden_zero,
        one_grad,
        gain_pre,
        vmem=LARGE if pieces == 2 else HUGE,
        scalars=None,
    )
    swapped_c = send(swapped, to_core, "zero_core")
    up_swapped = swap_chunks(add(up_keep, up_got))

    def slabs_of(kernel, height, *arrays):
        return simple(kernel, [shape(2, height, D)] * 2, *arrays)

    query_keep, query_send = slabs_of(
        query_grad_kernel,
        2 * OWN_ROWS,
        attended,
        attended_c,
        query_grad,
        one_low,
        pair_grads[1],
    )
    query_got = send(query_send, to_x, "query_x")
    merge_keep, merge_send = slabs_of(
        merge_grad_kernel, MERGE_ROWS + GAIN_ROWS, joined, joined_c, swapped, swapped_c
    )
    merge_got = send(merge_send, to_x, "merge_x")
    pair_keep, pair_send = slabs_of(
        pair_grad_kernel, 2 * OWN_ROWS, attended, attended_c, swapped, swapped_c
    )
    pair_got = send(pair_send, to_y, "pair_y")
    other_order = [blocks // 2 + at if at < blocks // 2 else at - blocks // 2 for at in range(blocks)]
    up_total = lax.psum(
        simple(copy_kernel, [shape(CHIPS, OWN_ROWS, chunk)], up_swapped, scalars=None),
        "blk",
        axis_index_groups=[other_order],
    )
    query_own, query_other = first_step(query_keep, query_got)
    query_y = send(query_other, to_y, "query_y")
    merge_own, merge_other = first_step(merge_keep, merge_got)
    merge_y = send(merge_other, to_y, "merge_y")
    pair_own, pair_other = first_step(pair_keep, pair_got)
    pair_x = send(pair_other, to_x, "pair_x")
    query_sum = add(query_own, query_y)
    merge_sum = add(merge_own, merge_y)
    pair_sum = add(pair_own, pair_x)
    sums = lax.psum((query_sum, merge_sum, pair_sum), "blk")
    meet()
    zero_back = [
        send(part, outward(other), "zero_out")
        for other, part in enumerate(
            simple(zero_kernel, [shape(rows, D)] * 2, swapped, scalars=None)
        )
    ]
    result_parts = simple(
        result_parts_kernel, [shape(tok, D)] * CHIPS, *activs, w_down, scalars=None
    )
    result_parts = [result_parts[0]] + [
        send(part, route, "result_around") for part, route in zip(result_parts[1:], over_plane)
    ]
    frames_grad, skipped_grad = simple(
        joined_grad_kernel, [shape(MB, rows, D, dtype=F32)] * 2, *zero_back, *mergers
    )
    rest()
    results = simple(
        result_kernel, [shape(rows, D)] * 2, *result_parts, hidden_one, scalars=None
    )
    results = [send(part, outward(other), "result_out") for other, part in enumerate(results)]
    rest()
    result_out = simple(by_micro_kernel, [shape(MB, rows, D)], *results)
    reducer_grad, expander_grad = simple(
        feed_total_kernel,
        [shape(*reducer.shape, dtype=F32), shape(*expander.shape, dtype=F32)],
        down_total,
        up_total,
        scalars=None,
    )
    merger_grad, projector_grad, combiner_grad, gain_grads = simple(
        total_kernel,
        [
            shape(*merger.shape, dtype=F32),
            shape(*projector.shape, dtype=F32),
            shape(*combiner.shape, dtype=F32),
            shape(8, OWN_ROWS, dtype=F32),
        ],
        *sums,
        scalars=None,
    )
    return (
        result_out,
        frames_grad,
        skipped_grad,
        merger_grad,
        projector_grad,
        combiner_grad,
        expander_grad,
        reducer_grad,
        gain_grads[0],
        gain_grads[1],
    )


def solution(mesh):
    tokens = P(None, ("fsdp", "blk"), None)
    weight = P("fsdp", None)
    gain = P("fsdp")
    return jax.shard_map(
        local,
        mesh=mesh,
        in_specs=(tokens, tokens, P(None, "fsdp", None))
        + (weight,) * 5
        + (gain, gain, tokens),
        out_specs=(tokens, tokens, tokens) + (weight,) * 5 + (gain, gain),
        check_vma=False,
    )
```

time: 449 us -> 420 us (0.935)
  Pallas kernels: 165 us -> 135 us
  waiting for transfers between devices: 174 us -> 163 us
  local copies, waits for them, and re-layouts: 15.4 us -> 25.6 us
    pallas_call x40 -> x39, Pallas kernels: 165 us -> 135 us  [call(): pl.pallas_call(passing, grid_spec=pltpu.PrefetchScalarGridSpec(num_scalar...]
    psum x1 -> x3, waiting for transfers between devices: 0.01 us -> 24.7 us  [the longest x1 24.7 us: local(): sums = lax.psum((query_sum, merge_sum, pair_sum), 'blk')]
    all_gather x1, waiting for transfers between devices: 37.3 us -> 14.3 us  [local(): lax.all_gather(jnp.concatenate([projector, combiner], 1), 'fsdp', axis=0)]
    ppermute x53 -> x42, waiting for transfers between devices: 137 us -> 124 us  [send(): return lax.ppermute(array, AXES, pairs)]
    all_to_all x0 -> x2, starting transfers between devices: none -> 8.68 us  [local(): lax.all_to_all(parts, 'fsdp', 0, 0, axis_index_groups=groups, tiled=True)]
    unnamed x94 -> x116, local copies, waits for them, and re-layouts: 13.2 us -> 21.8 us
    ppermute x53 -> x42, starting transfers between devices: 61.7 us -> 54.4 us  [send(): return lax.ppermute(array, AXES, pairs)]
  transfers between devices with their start and end apart: 55 -> 48, of which waited for: 20 -> 21; matrix products, arithmetic and copies ran while one was open for 3% -> 3% of each run, Pallas kernels for 37% -> 32%
where the time goes in v2:
time: 420 us; the launch traced here: 412 us
  waiting for transfers between devices  163 us (39%)
  Pallas kernels  135 us (32%)
  starting transfers between devices  63.2 us (15%)
  local copies, waits for them, and re-layouts  25.6 us (6%)
  between operations  15 us (4%)
  other arithmetic  9.72 us (2%)
    pallas_call x39, Pallas kernels, call(): pl.pallas_call(passing, grid_spec=pltpu.PrefetchScalarGridSpec(num_scalar...  135 us
    ppermute x42, waiting for transfers between devices, send(): return lax.ppermute(array, AXES, pairs)  124 us
    ppermute x42, starting transfers between devices, send(): return lax.ppermute(array, AXES, pairs)  54.4 us
    psum x1, waiting for transfers between devices, local(): sums = lax.psum((query_sum, merge_sum, pair_sum), 'blk')  24.7 us
    unnamed x116, local copies, waits for them, and re-layouts  21.8 us
    all_gather x1, waiting for transfers between devices, local(): lax.all_gather(jnp.concatenate([projector, combiner], 1), 'fsdp', axis=0)  14.3 us
    all_to_all x2, starting transfers between devices, local(): lax.all_to_all(parts, 'fsdp', 0, 0, axis_index_groups=groups, tiled=True)  8.68 us
  transfers between devices with their start and end apart: 48, of which 21 were waited for; matrix products, arithmetic and copies ran while one was open for 3% of the time, Pallas kernels for 32%

profile of v2, /device:TPU:0, one launch (start us, length us, event | category | flops | bytes accessed | tf_op | source)
XLA Modules:
  0.0 411.8 jit_solution(13274093007753622795)
XLA Ops:
  9.1 3.0 collective-permute-start.3
  14.1 2.0 pad_maximum_fusion
  20.4 1.9 multiply_cosine_fusion
  27.4 7.4 %collective-permute-start.1 = (bf16[128,3072]{1,0:T(8,128)(2,1)}, bf16[128,3072]{1,0:T(8,128)(2,1)}, u32[]{:S(2)}, u32[]{:S(2)}) collective-permute-start(bf16[128,3072]{1,0:T(8,128)(2,1)} %pad_maximum_fusion.1), channel_id=1, source_target_pairs={{0,0},{1,2},{2,4},{3,6},{4,1},{5,3},{6,5},{7,7},{8,8},{9,10},{10,1... | collective-permute-start | bytes 2359304 | tf_op jit(solution)/shard_map/tokens_in/ppermute | solution.py:565
  36.0 11.5 %collective-permute-done.5.refs_7_ = bf16[272,1024]{1,0:T(8,128)(2,1)} collective-permute-done((bf16[272,1024]{1,0:T(8,128)(2,1)S(1)}, bf16[272,1024]{1,0:T(8,128)(2,1)}, u32[]{:S(2)}, u32[]{:S(2)}) %collective-permute-start.5) | collective-permute-done | bytes 557088 | tf_op jit(solution)/shard_map/merger_around/ppermute | solution.py:565
  50.1 4.3 %collective-permute-done.2.refs_3_ = bf16[128,3072]{1,0:T(8,128)(2,1)} collective-permute-done((bf16[128,3072]{1,0:T(8,128)(2,1)}, bf16[128,3072]{1,0:T(8,128)(2,1)}, u32[]{:S(2)}, u32[]{:S(2)}) %collective-permute-start.2) | collective-permute-done | bytes 786464 | tf_op jit(solution)/shard_map/tokens_in/ppermute | solution.py:565
  54.4 6.0 %merge_kernel.1 = (f32[8,128]{1,0:T(8,128)S(1)}, f32[256,1024]{1,0:T(8,128)S(1)}, bf16[256,1024]{1,0:T(8,128)(2,1)S(1)}, bf16[256,2048]{1,0:T(8,128)(2,1)}, f32[...) custom-call(s32[8]{0:T(128)S(1)} %stack.53.refs_0_, ...), custom_call_target="tpu_custom_call", output_to_operand_aliasing={{0}: (1, {})} | custom-call | flops 999999995904 | tf_op jit(solution)/shard_map/merge_kernel/pallas_call | solution.py:500
  61.6 4.3 %all-to-all-start = ((bf16[4,128,1024]{2,1,0:T(8,128)(2,1)}), bf16[4,128,1024]{2,1,0:T(8,128)(2,1)}, u32[]{:S(2)}, u32[]{:S(2)}) async-start(bf16[4,128,1024]{2,1,0:T(8,128)(2,1)} %get-tuple-element.133), calls=%async_computation | async-start | bytes 2097152 | tf_op jit(solution)/shard_map/all_to_all | solution.py:702
  66.0 12.3 %collective-permute-start.26 = (bf16[256,2048]{1,0:T(8,128)(2,1)}, bf16[256,2048]{1,0:T(8,128)(2,1)}, u32[]{:S(2)}, u32[]{:S(2)}) collective-permute-start(bf16[256,2048]{1,0:T(8,128)(2,1)} %get-tuple-element.190.refs_2_), channel_id=1, source_target_pairs={{0,4},{1,5},{2,6},{3,7},{4,0},{5,1},{6,2},{7,3},{8,12},{9,13},{10,... | collective-permute-start | bytes 3145736 | tf_op jit(solution)/shard_map/joined_core/ppermute | solution.py:565
  78.2 14.3 %all-gather.3.cloned.1.call-done = bf16[1024,4096]{1,0:T(8,128)(2,1)} async-done(((bf16[128,4096]{1,0:T(8,128)(2,1)}), bf16[1024,4096]{1,0:T(8,128)(2,1)}) %all-gather.3.cloned.1.call-update) | async-done | bytes 8388624 | tf_op jit(solution)/shard_map/all_gather | solution.py:601
  92.6 3.4 copy-done.4
  95.9 4.7 %project_kernel.1 = (f32[8,128]{1,0:T(8,128)S(1)}, bf16[256,1024]{1,0:T(8,128)(2,1)S(1)}, bf16[256,1024]{1,0:T(8,128)(2,1)S(1)}, bf16[2,256,1024]{2,1,0:T(8,128)(2,1)}, bf16[256,1024]{1,0:T(8,128)(2,1)}) custom-call(f32[8,128]{1,0:T(8,128)S(1)} %get-tuple-element.128.refs_0_, ...), custom_call_target="tpu_custom_call", output_to_operand_aliasing={{0}: (0, {})} | custom-call | flops 999999995904 | tf_op jit(solution)/shard_map/project_kernel/pallas_call | solution.py:500
  101.5 1.7 collective-permute-start.14
  103.2 1.8 collective-permute-start.15
  105.0 2.4 copy_kernel.2
  109.1 8.7 %attend_kernel.1 = (f32[8,128]{1,0:T(8,128)S(1)}, bf16[2,256,1024]{2,1,0:T(8,128)(2,1)}, f32[256,1024]{1,0:T(8,128)S(1)}, bf16[256,1024]{1,0:T(8,128)(2,1)}, bf16[16,2,256,256]{3,2,1,0:T(8,128)(2,1)S(1)}) custom-call(f32[8,128]{1,0:T(8,128)S(1)} %get-tuple-element.134.refs_0_, ...), custom_call_target="tpu_custom_call", output_to_operand_aliasing={{0}: (0, {})} | custom-call | flops 999999995904 | tf_op jit(solution)/shard_map/attend_kernel/pallas_call | solution.py:500
  117.9 2.2 up_kernel.1
  120.2 1.8 collective-permute-start.17
  122.0 5.6 %collective-permute-done.14.refs_2_ = bf16[256,1024]{1,0:T(8,128)(2,1)} collective-permute-done((bf16[256,1024]{1,0:T(8,128)(2,1)}, bf16[256,1024]{1,0:T(8,128)(2,1)}, u32[]{:S(2)}, u32[]{:S(2)}) %collective-permute-start.14) | collective-permute-done | bytes 524320 | tf_op jit(solution)/shard_map/cot_around/ppermute | solution.py:565
  127.5 1.8 collective-permute-start.18
  131.4 3.3 feed_kernel.4
  134.7 4.4 %collective-permute-done.16.refs_1_.refs_3_ = bf16[256,1024]{1,0:T(8,128)(2,1)} collective-permute-done((bf16[256,1024]{1,0:T(8,128)(2,1)}, bf16[256,1024]{1,0:T(8,128)(2,1)}, u32[]{:S(2)}, u32[]{:S(2)}) %collective-permute-start.16) | collective-permute-done | bytes 524320 | tf_op jit(solution)/shard_map/act_around/ppermute | solution.py:565
  139.1 4.1 feed_kernel.5
  143.2 6.9 %collective-permute-done.17.refs_1_.refs_4_ = bf16[256,1024]{1,0:T(8,128)(2,1)} collective-permute-done((bf16[256,1024]{1,0:T(8,128)(2,1)}, bf16[256,1024]{1,0:T(8,128)(2,1)}, u32[]{:S(2)}, u32[]{:S(2)}) %collective-permute-start.17) | collective-permute-done | bytes 524320 | tf_op jit(solution)/shard_map/act_around/ppermute | solution.py:565
  150.1 4.3 %feed_kernel.6 = (f32[8,128]{1,0:T(8,128)S(1)}, bf16[256,1024]{1,0:T(8,128)(2,1)}, bf16[256,1024]{1,0:T(8,128)(2,1)S(1)}, bf16[256,1024]{1,0:T(8,128)(2,1)S(1)}) custom-call(f32[8,128]{1,0:T(8,128)S(1)} %get-tuple-element.149.refs_0_, bf16[256,1024]{1,0:T(8,128)(2,1)} %collective-permute-done.17.refs_1_.refs_4_, ...), custom_call_target="tpu_custom_call", output_to_operand_aliasing={{0}: (0, {})} | custom-call | flops 999999995904 | tf_op jit(solution)/shard_map/feed_kernel/pallas_call | solution.py:500
  155.5 4.2 %feed_kernel.7 = (f32[8,128]{1,0:T(8,128)S(1)}, bf16[256,1024]{1,0:T(8,128)(2,1)}, bf16[256,1024]{1,0:T(8,128)(2,1)S(1)}, bf16[256,1024]{1,0:T(8,128)(2,1)S(1)}) custom-call(f32[8,128]{1,0:T(8,128)S(1)} %get-tuple-element.151.refs_0_, bf16[256,1024]{1,0:T(8,128)(2,1)} %collective-permute-done.18.refs_1_.refs_5_, ...), custom_call_target="tpu_custom_call", output_to_operand_aliasing={{0}: (0, {})} | custom-call | flops 999999995904 | tf_op jit(solution)/shard_map/feed_kernel/pallas_call | solution.py:500
  160.5 3.9 down_grad_kernel.1
  164.4 5.4 %up_grad_kernel.1 = (f32[8,128]{1,0:T(8,128)S(1)}, bf16[4,128,1024]{2,1,0:T(8,128)(2,1)S(1)}, bf16[4,128,1024]{2,1,0:T(8,128)(2,1)}) custom-call(s32[8]{0:T(128)S(1)} %stack.53.refs_0_, f32[8,128]{1,0:T(8,128)S(1)} %get-tuple-element.158.refs_1_, bf16[256,1024]{1,0:T(8,128)(2,1)} %get-tuple-element.144.refs_1_.refs_2_, ...), custom_call_target="tpu_custom_call", output_to_operand_aliasing={{0}: (1, {})} | custom-call | flops 999999995904 | tf_op jit(solution)/shard_map/up_grad_kernel/pallas_call | solution.py:500
  173.3 9.8 %collective-permute-done.21.refs_12_ = bf16[256,1024]{1,0:T(8,128)(2,1)} collective-permute-done((bf16[256,1024]{1,0:T(8,128)(2,1)}, bf16[256,1024]{1,0:T(8,128)(2,1)}, u32[]{:S(2)}, u32[]{:S(2)}) %collective-permute-start.21) | collective-permute-done | bytes 524320 | tf_op jit(solution)/shard_map/second_around/ppermute | solution.py:565
  183.1 14.4 %attend_back_kernel.1 = (f32[8,128]{1,0:T(8,128)S(1)}, f32[256,1024]{1,0:T(8,128)S(1)}, bf16[256,1024]{1,0:T(8,128)(2,1)S(1)}, f32[1,1024]{1,0:T(1,128)S(1)}, bf...) custom-call(f32[8,128]{1,0:T(8,128)S(1)} %get-tuple-element.169.refs, ...), custom_call_target="tpu_custom_call", output_to_operand_aliasing={{0}: (0, {})} | custom-call | flops 999999995904 | tf_op jit(solution)/shard_map/attend_back_kernel/pallas_call | solution.py:500
  197.7 2.8 add_kernel.5
  202.1 3.4 copy-done.7
  207.8 6.9 %united_kernel.1 = (f32[8,128]{1,0:T(8,128)S(1)}, bf16[784,1024]{1,0:T(8,128)(2,1)}) custom-call(f32[8,128]{1,0:T(8,128)S(1)} %get-tuple-element.177.refs_0_, bf16[256,1024]{1,0:T(8,128)(2,1)S(1)} %copy-done.33, f32[1,1024]{1,0:T(1,128)S(1)} %get-tuple-element.179.refs_2_, ...), custom_call_target="tpu_custom_call", output_to_operand_aliasing={{0}: (0, {})} | custom-call | flops 999999995904 | tf_op jit(solution)/shard_map/united_kernel/pallas_call | solution.py:500
  214.9 2.5 add_kernel.6
  217.4 4.4 %all-to-all-start.1 = ((bf16[4,128,1024]{2,1,0:T(8,128)(2,1)}), bf16[4,128,1024]{2,1,0:T(8,128)(2,1)}, u32[]{:S(2)}, u32[]{:S(2)}) async-start(bf16[4,128,1024]{2,1,0:T(8,128)(2,1)} %get-tuple-element.194), calls=%async_computation.1 | async-start | bytes 2097152 | tf_op jit(solution)/shard_map/all_to_all | solution.py:702
  221.8 5.1 %query_grad_kernel.1 = (f32[8,128]{1,0:T(8,128)S(1)}, bf16[2,256,1024]{2,1,0:T(8,128)(2,1)S(1)}, bf16[2,256,1024]{2,1,0:T(8,128)(2,1)}) custom-call(s32[8]{0:T(128)S(1)} %stack.53.refs_0_, f32[8,128]{1,0:T(8,128)S(1)} %get-tuple-element.186.refs_1_, bf16[2,256,1024]{2,1,0:T(8,128)(2,1)} %get-tuple-element.187.refs_2_, ...), custom_call_target="tpu_custom_call", output_to_operand_aliasing={{0}: (1, {})} | custom-call | flops 999999995904 | tf_op jit(solution)/shard_map/query_grad_kernel/pallas_call | solution.py:500
  227.9 1.9 collective-permute-start.28
  229.9 5.5 %merge_grad_kernel.1 = (f32[8,128]{1,0:T(8,128)S(1)}, bf16[2,272,1024]{2,1,0:T(8,128)(2,1)S(1)}, bf16[2,272,1024]{2,1,0:T(8,128)(2,1)}) custom-call(s32[8]{0:T(128)S(1)} %stack.53.refs_0_, f32[8,128]{1,0:T(8,128)S(1)} %get-tuple-element.189.refs_1_, bf16[256,2048]{1,0:T(8,128)(2,1)} %get-tuple-element.190.refs_2_, ...), custom_call_target="tpu_custom_call", output_to_operand_aliasing={{0}: (1, {})} | custom-call | flops 999999995904 | tf_op jit(solution)/shard_map/merge_grad_kernel/pallas_call | solution.py:500
  235.4 5.4 %pair_grad_kernel.1 = (f32[8,128]{1,0:T(8,128)S(1)}, bf16[2,256,1024]{2,1,0:T(8,128)(2,1)S(1)}, bf16[2,256,1024]{2,1,0:T(8,128)(2,1)}) custom-call(s32[8]{0:T(128)S(1)} %stack.53.refs_0_, f32[8,128]{1,0:T(8,128)S(1)} %get-tuple-element.192.refs_1_, bf16[2,256,1024]{2,1,0:T(8,128)(2,1)} %get-tuple-element.187.refs_2_, ...), custom_call_target="tpu_custom_call", output_to_operand_aliasing={{0}: (1, {})} | custom-call | flops 999999995904 | tf_op jit(solution)/shard_map/pair_grad_kernel/pallas_call | solution.py:500
  240.7 1.9 collective-permute-start.30
  242.7 2.4 copy_kernel.3
  245.0 14.2 %collective-permute-done.28.refs_2_ = bf16[2,256,1024]{2,1,0:T(8,128)(2,1)} collective-permute-done((bf16[2,256,1024]{2,1,0:T(8,128)(2,1)}, bf16[2,256,1024]{2,1,0:T(8,128)(2,1)}, u32[]{:S(2)}, u32[]{:S(2)}) %collective-permute-start.28) | collective-permute-done | bytes 1048608 | tf_op jit(solution)/shard_map/query_x/ppermute | solution.py:565
  259.3 2.1 add_two_kernel.3
  263.8 18.8 %collective-permute-done.29.refs_2_ = bf16[2,272,1024]{2,1,0:T(8,128)(2,1)} collective-permute-done((bf16[2,272,1024]{2,1,0:T(8,128)(2,1)}, bf16[2,272,1024]{2,1,0:T(8,128)(2,1)}, u32[]{:S(2)}, u32[]{:S(2)}) %collective-permute-start.29) | collective-permute-done | bytes 1114144 | tf_op jit(solution)/shard_map/merge_x/ppermute | solution.py:565
  282.6 2.2 add_two_kernel.4
  286.3 2.2 add_two_kernel.5
  289.0 2.0 add_kernel.7
  291.0 8.2 %collective-permute-done.32.refs_2_ = bf16[272,1024]{1,0:T(8,128)(2,1)} collective-permute-done((bf16[272,1024]{1,0:T(8,128)(2,1)}, bf16[272,1024]{1,0:T(8,128)(2,1)}, u32[]{:S(2)}, u32[]{:S(2)}) %collective-permute-start.32) | collective-permute-done | bytes 557088 | tf_op jit(solution)/shard_map/merge_y/ppermute | solution.py:565
  299.2 2.0 add_kernel.8
  301.9 2.0 add_kernel.9
  305.0 2.4 zero_kernel.1
  307.4 3.6 collective-permute-start.35
  311.2 3.2 result_parts_kernel.1
  317.8 8.5 %collective-permute-done.36.refs_3_ = bf16[128,1024]{1,0:T(8,128)(2,1)} collective-permute-done((bf16[128,1024]{1,0:T(8,128)(2,1)}, bf16[128,1024]{1,0:T(8,128)(2,1)}, u32[]{:S(2)}, u32[]{:S(2)}) %collective-permute-start.36) | collective-permute-done | bytes 262176 | tf_op jit(solution)/shard_map/zero_out/ppermute | solution.py:565
  326.4 7.9 %joined_grad_kernel.1 = (f32[8,128]{1,0:T(8,128)S(1)}, f32[2,128,1024]{2,1,0:T(8,128)}, f32[2,128,1024]{2,1,0:T(8,128)}) custom-call(s32[8]{0:T(128)S(1)} %stack.53.refs_0_, f32[8,128]{1,0:T(8,128)S(1)} %get-tuple-element.215.refs_1_, bf16[128,1024]{1,0:T(8,128)(2,1)} %collective-permute-done.35.refs_2_, ...), custom_call_target="tpu_custom_call", output_to_operand_aliasing={{0}: (1, {})} | custom-call | flops 999999995904 | tf_op jit(solution)/shard_map/joined_grad_kernel/pallas_call | solution.py:500
  334.3 5.9 %collective-permute-done.38.refs_3_ = bf16[256,1024]{1,0:T(8,128)(2,1)} collective-permute-done((bf16[256,1024]{1,0:T(8,128)(2,1)}, bf16[256,1024]{1,0:T(8,128)(2,1)}, u32[]{:S(2)}, u32[]{:S(2)}) %collective-permute-start.38) | collective-permute-done | bytes 524320 | tf_op jit(solution)/shard_map/result_around/ppermute | solution.py:565
  340.2 2.5 collective-permute-done.39.refs_4_
  342.7 2.4 result_kernel.1
  345.0 3.6 collective-permute-start.40
  349.0 18.6 %collective-permute-done.41.refs_3_ = bf16[128,1024]{1,0:T(8,128)(2,1)} collective-permute-done((bf16[128,1024]{1,0:T(8,128)(2,1)}, bf16[128,1024]{1,0:T(8,128)(2,1)}, u32[]{:S(2)}, u32[]{:S(2)}) %collective-permute-start.41) | collective-permute-done | bytes 262176 | tf_op jit(solution)/shard_map/result_out/ppermute | solution.py:565
  367.6 2.4 by_micro_kernel.1
  372.6 2.2 feed_total_kernel.1
  374.8 24.7 %all-reduce.10.cloned.1.call-done = (bf16[256,1024]{1,0:T(8,128)(2,1)}, bf16[272,1024]{1,0:T(8,128)(2,1)}, bf16[256,1024]{1,0:T(8,128)(2,1)}) async-done(((bf16[256,1024]{1,0:T(8,128)(2,1)}, bf16[272,1024]{1,0:T(8,128)(2,1)}, bf16[256,1024]{1,0:T(8,128)(2,1)}), (bf16[256,1024]{1,0:T(8,128)(2,1)}, bf16[272,1024]{1,0:T(8,128)(2,1)}, bf16[256,1024]{1,0:T(8,128)(2,1)})) %all-reduce.10.cloned.1.call-update) | async-done | bytes 1605648 | tf_op jit(solution)/shard_map/psum | solution.py:894
  402.6 1.8 total_kernel.1
  (231 shorter events, 49.9 us)
Async XLA Ops:
  7.2 85.4 %all-gather.3.cloned.1.call-start = ((), (), s32[]{:S(2)}) async-start(), calls=%async_computation.4 | async-start | bytes 9437184 | tf_op jit(solution)/shard_map/all_gather | solution.py:601
  9.1 7.3 %copy-start.54 = (bf16[2,128,1024]{2,1,0:T(8,128)(2,1)S(1)}, bf16[2,128,1024]{2,1,0:T(8,128)(2,1)}, u32[]{:S(2)}) copy-start(bf16[2,128,1024]{2,1,0:T(8,128)(2,1)} %param.11) | copy-start | bytes 1572868
  9.1 18.4 %collective-permute-start.3 = (bf16[272,1024]{1,0:T(8,128)(2,1)S(1)}, bf16[272,1024]{1,0:T(8,128)(2,1)}, u32[]{:S(2)}, u32[]{:S(2)}) collective-permute-start(bf16[272,1024]{1,0:T(8,128)(2,1)S(1)} %pad_maximum_fusion.3.refs_4_), channel_id=1, source_target_pairs={{0,8},{1,9},{2,10},{3,11},{4,12},{5,13},{6,14},{7,15},{8,0},{9,1},... | collective-permute-start | bytes 1671176 | tf_op jit(solution)/shard_map/merger_around/ppermute | solution.py:565
  12.1 23.0 %collective-permute-start.4 = (bf16[272,1024]{1,0:T(8,128)(2,1)S(1)}, bf16[272,1024]{1,0:T(8,128)(2,1)}, u32[]{:S(2)}, u32[]{:S(2)}) collective-permute-start(bf16[272,1024]{1,0:T(8,128)(2,1)S(1)} %pad_maximum_fusion.3.refs_4_), channel_id=1, source_target_pairs={{0,16},{1,17},{2,18},{3,19},{4,20},{5,21},{6,22},{7,23},{8,24},{9,... | collective-permute-start | bytes 1671176 | tf_op jit(solution)/shard_map/merger_around/ppermute | solution.py:565
  13.6 33.9 %collective-permute-start.5 = (bf16[272,1024]{1,0:T(8,128)(2,1)S(1)}, bf16[272,1024]{1,0:T(8,128)(2,1)}, u32[]{:S(2)}, u32[]{:S(2)}) collective-permute-start(bf16[272,1024]{1,0:T(8,128)(2,1)S(1)} %pad_maximum_fusion.3.refs_4_), channel_id=1, source_target_pairs={{0,24},{1,25},{2,26},{3,27},{4,28},{5,29},{6,30},{7,31},{8,16},{9,... | collective-permute-start | bytes 1671176 | tf_op jit(solution)/shard_map/merger_around/ppermute | solution.py:565
  13.6 33.9 %collective-permute-start.6 = (bf16[272,1024]{1,0:T(8,128)(2,1)S(1)}, bf16[272,1024]{1,0:T(8,128)(2,1)}, u32[]{:S(2)}, u32[]{:S(2)}) collective-permute-start(bf16[272,1024]{1,0:T(8,128)(2,1)S(1)} %pad_maximum_fusion.3.refs_4_), channel_id=1, source_target_pairs={{0,4},{1,5},{2,6},{3,7},{4,0},{5,1},{6,2},{7,3},{8,12},{9,13},{10,... | collective-permute-start | bytes 1671176 | tf_op jit(solution)/shard_map/merger_core/ppermute | solution.py:565
  13.6 5.8 %collective-permute-start.10 = (s32[2,1,9]{2,1,0:T(1,128)}, s32[2,1,9]{2,1,0:T(1,128)S(1)}, u32[]{:S(2)}, u32[]{:S(2)}) collective-permute-start(s32[2,1,9]{2,1,0:T(1,128)} %param.13), channel_id=1, source_target_pairs={{0,4},{1,5},{2,6},{3,7},{4,0},{5,1},{6,2},{7,3},{8,12},{9,13},{10,... | collective-permute-start | bytes 224 | tf_op jit(solution)/shard_map/lengths_core/ppermute | solution.py:565
  19.4 28.6 %collective-permute-start = (bf16[512,1024]{1,0:T(8,128)(2,1)S(1)}, bf16[512,1024]{1,0:T(8,128)(2,1)S(1)}, u32[]{:S(2)}, u32[]{:S(2)}) collective-permute-start(bf16[512,1024]{1,0:T(8,128)(2,1)S(1)} %copy-done.8), channel_id=1, source_target_pairs={{0,4},{1,5},{2,6},{3,7},{4,0},{5,1},{6,2},{7,3},{8,12},{9,13},{10,... | collective-permute-start | bytes 3145736 | tf_op jit(solution)/shard_map/w_down_core/ppermute | solution.py:565
  27.4 22.7 %collective-permute-start.1 = (bf16[128,3072]{1,0:T(8,128)(2,1)}, bf16[128,3072]{1,0:T(8,128)(2,1)}, u32[]{:S(2)}, u32[]{:S(2)}) collective-permute-start(bf16[128,3072]{1,0:T(8,128)(2,1)} %pad_maximum_fusion.1), channel_id=1, source_target_pairs={{0,0},{1,2},{2,4},{3,6},{4,1},{5,3},{6,5},{7,7},{8,8},{9,10},{10,1... | collective-permute-start | bytes 2359304 | tf_op jit(solution)/shard_map/tokens_in/ppermute | solution.py:565
  35.1 19.3 %collective-permute-start.2 = (bf16[128,3072]{1,0:T(8,128)(2,1)}, bf16[128,3072]{1,0:T(8,128)(2,1)}, u32[]{:S(2)}, u32[]{:S(2)}) collective-permute-start(bf16[128,3072]{1,0:T(8,128)(2,1)} %pad_maximum_fusion.2), channel_id=1, source_target_pairs={{0,2},{1,0},{2,6},{3,4},{4,3},{5,1},{6,7},{7,5},{8,10},{9,8},{10,1... | collective-permute-start | bytes 2359304 | tf_op jit(solution)/shard_map/tokens_in/ppermute | solution.py:565
  47.5 6.9 %collective-permute-start.7 = (bf16[272,1024]{1,0:T(8,128)(2,1)}, bf16[272,1024]{1,0:T(8,128)(2,1)}, u32[]{:S(2)}, u32[]{:S(2)}) collective-permute-start(bf16[272,1024]{1,0:T(8,128)(2,1)} %collective-permute-done.3.refs_5_), channel_id=1, source_target_pairs={{0,4},{1,5},{2,6},{3,7},{4,0},{5,1},{6,2},{7,3},{8,12},{9,13},{10,... | collective-permute-start | bytes 1671176 | tf_op jit(solution)/shard_map/merger_core/ppermute | solution.py:565
  47.5 6.9 %collective-permute-start.8 = (bf16[272,1024]{1,0:T(8,128)(2,1)}, bf16[272,1024]{1,0:T(8,128)(2,1)}, u32[]{:S(2)}, u32[]{:S(2)}) collective-permute-start(bf16[272,1024]{1,0:T(8,128)(2,1)} %collective-permute-done.4.refs_6_), channel_id=1, source_target_pairs={{0,4},{1,5},{2,6},{3,7},{4,0},{5,1},{6,2},{7,3},{8,12},{9,13},{10,... | collective-permute-start | bytes 1671176 | tf_op jit(solution)/shard_map/merger_core/ppermute | solution.py:565
  48.0 6.4 %collective-permute-start.9 = (bf16[272,1024]{1,0:T(8,128)(2,1)}, bf16[272,1024]{1,0:T(8,128)(2,1)}, u32[]{:S(2)}, u32[]{:S(2)}) collective-permute-start(bf16[272,1024]{1,0:T(8,128)(2,1)} %collective-permute-done.5.refs_7_), channel_id=1, source_target_pairs={{0,4},{1,5},{2,6},{3,7},{4,0},{5,1},{6,2},{7,3},{8,12},{9,13},{10,... | collective-permute-start | bytes 1671176 | tf_op jit(solution)/shard_map/merger_core/ppermute | solution.py:565
  60.4 32.1 %copy-start.51 = (f32[1,1024]{1,0:T(1,128)}, f32[1,1024]{1,0:T(1,128)S(1)}, u32[]{:S(2)}) copy-start(f32[1,1024]{1,0:T(1,128)S(1)} %get-tuple-element.130.refs_2_.refs_8_) | copy-start | bytes 12292
  60.5 47.7 %copy-start.20 = (f32[256,1024]{1,0:T(8,128)}, f32[256,1024]{1,0:T(8,128)S(1)}, u32[]{:S(2)}) copy-start(f32[256,1024]{1,0:T(8,128)S(1)} %get-tuple-element.129.refs_1_.refs_8_.refs_6_) | copy-start | bytes 3145732
  60.5 100.0 %copy-start.26 = (bf16[256,1024]{1,0:T(8,128)(2,1)}, bf16[256,1024]{1,0:T(8,128)(2,1)S(1)}, u32[]{:S(2)}) copy-start(bf16[256,1024]{1,0:T(8,128)(2,1)S(1)} %get-tuple-element.131.refs_6_.refs_2_.refs_7_) | copy-start | bytes 1572868
  61.6 43.4 %all-to-all-start = ((bf16[4,128,1024]{2,1,0:T(8,128)(2,1)}), bf16[4,128,1024]{2,1,0:T(8,128)(2,1)}, u32[]{:S(2)}, u32[]{:S(2)}) async-start(bf16[4,128,1024]{2,1,0:T(8,128)(2,1)} %get-tuple-element.133), calls=%async_computation | async-start | bytes 2097152 | tf_op jit(solution)/shard_map/all_to_all | solution.py:702
  65.9 304.1 %all-reduce.6.cloned.1.call-start = ((), (), s32[]{:S(2)}) async-start(), calls=%async_computation.2 | async-start | bytes 2097152 | tf_op jit(solution)/shard_map/psum | solution.py:835
  66.0 163.9 %collective-permute-start.26 = (bf16[256,2048]{1,0:T(8,128)(2,1)}, bf16[256,2048]{1,0:T(8,128)(2,1)}, u32[]{:S(2)}, u32[]{:S(2)}) collective-permute-start(bf16[256,2048]{1,0:T(8,128)(2,1)} %get-tuple-element.190.refs_2_), channel_id=1, source_target_pairs={{0,4},{1,5},{2,6},{3,7},{4,0},{5,1},{6,2},{7,3},{8,12},{9,13},{10,... | collective-permute-start | bytes 3145736 | tf_op jit(solution)/shard_map/joined_core/ppermute | solution.py:565
  101.5 18.7 %collective-permute-start.13 = (bf16[256,1024]{1,0:T(8,128)(2,1)}, bf16[256,1024]{1,0:T(8,128)(2,1)}, u32[]{:S(2)}, u32[]{:S(2)}) collective-permute-start(bf16[256,1024]{1,0:T(8,128)(2,1)} %get-tuple-element.142), channel_id=1, source_target_pairs={{0,8},{1,9},{2,10},{3,11},{4,12},{5,13},{6,14},{7,15},{8,0},{9,1},... | collective-permute-start | bytes 1572872 | tf_op jit(solution)/shard_map/cot_around/ppermute | solution.py:565
  101.5 26.0 %collective-permute-start.14 = (bf16[256,1024]{1,0:T(8,128)(2,1)}, bf16[256,1024]{1,0:T(8,128)(2,1)}, u32[]{:S(2)}, u32[]{:S(2)}) collective-permute-start(bf16[256,1024]{1,0:T(8,128)(2,1)} %get-tuple-element.142), channel_id=1, source_target_pairs={{0,24},{1,25},{2,26},{3,27},{4,28},{5,29},{6,30},{7,31},{8,16},{9,... | collective-permute-start | bytes 1572872 | tf_op jit(solution)/shard_map/cot_around/ppermute | solution.py:565
  103.2 26.1 %collective-permute-start.15 = (bf16[256,1024]{1,0:T(8,128)(2,1)}, bf16[256,1024]{1,0:T(8,128)(2,1)}, u32[]{:S(2)}, u32[]{:S(2)}) collective-permute-start(bf16[256,1024]{1,0:T(8,128)(2,1)} %get-tuple-element.142), channel_id=1, source_target_pairs={{0,16},{1,17},{2,18},{3,19},{4,20},{5,21},{6,22},{7,23},{8,24},{9,... | collective-permute-start | bytes 1572872 | tf_op jit(solution)/shard_map/cot_around/ppermute | solution.py:565
  105.0 3.0 collective-permute-start.11
  108.0 9.9 %collective-permute-start.12 = (bf16[4,128,1024]{2,1,0:T(8,128)(2,1)}, bf16[4,128,1024]{2,1,0:T(8,128)(2,1)}, u32[]{:S(2)}, u32[]{:S(2)}) collective-permute-start(bf16[4,128,1024]{2,1,0:T(8,128)(2,1)} %get-tuple-element.140.refs_2_), channel_id=1, source_target_pairs={{0,4},{1,5},{2,6},{3,7},{4,0},{5,1},{6,2},{7,3},{8,12},{9,13},{10,... | collective-permute-start | bytes 3145736 | tf_op jit(solution)/shard_map/w_up_core/ppermute | solution.py:565
  117.8 65.3 %copy-start.18 = (f32[256,1024]{1,0:T(8,128)}, f32[256,1024]{1,0:T(8,128)S(1)}, u32[]{:S(2)}) copy-start(f32[256,1024]{1,0:T(8,128)S(1)} %get-tuple-element.171.refs_6_.refs_5_) | copy-start | bytes 3145732
  117.9 21.2 %collective-permute-start.16 = (bf16[256,1024]{1,0:T(8,128)(2,1)}, bf16[256,1024]{1,0:T(8,128)(2,1)}, u32[]{:S(2)}, u32[]{:S(2)}) collective-permute-start(bf16[256,1024]{1,0:T(8,128)(2,1)} %get-tuple-element.144.refs_1_.refs_2_), channel_id=1, source_target_pairs={{0,8},{1,9},{2,10},{3,11},{4,12},{5,13},{6,14},{7,15},{8,0},{9,1},... | collective-permute-start | bytes 1572872 | tf_op jit(solution)/shard_map/act_around/ppermute | solution.py:565
  120.2 29.9 %collective-permute-start.17 = (bf16[256,1024]{1,0:T(8,128)(2,1)}, bf16[256,1024]{1,0:T(8,128)(2,1)}, u32[]{:S(2)}, u32[]{:S(2)}) collective-permute-start(bf16[256,1024]{1,0:T(8,128)(2,1)} %get-tuple-element.144.refs_1_.refs_2_), channel_id=1, source_target_pairs={{0,24},{1,25},{2,26},{3,27},{4,28},{5,29},{6,30},{7,31},{8,16},{9,... | collective-permute-start | bytes 1572872 | tf_op jit(solution)/shard_map/act_around/ppermute | solution.py:565
  127.5 28.0 %collective-permute-start.18 = (bf16[256,1024]{1,0:T(8,128)(2,1)}, bf16[256,1024]{1,0:T(8,128)(2,1)}, u32[]{:S(2)}, u32[]{:S(2)}) collective-permute-start(bf16[256,1024]{1,0:T(8,128)(2,1)} %get-tuple-element.144.refs_1_.refs_2_), channel_id=1, source_target_pairs={{0,16},{1,17},{2,18},{3,19},{4,20},{5,21},{6,22},{7,23},{8,24},{9,... | collective-permute-start | bytes 1572872 | tf_op jit(solution)/shard_map/act_around/ppermute | solution.py:565
  129.3 92.5 %collective-permute-start.25 = (bf16[2,256,1024]{2,1,0:T(8,128)(2,1)}, bf16[2,256,1024]{2,1,0:T(8,128)(2,1)}, u32[]{:S(2)}, u32[]{:S(2)}) collective-permute-start(bf16[2,256,1024]{2,1,0:T(8,128)(2,1)} %get-tuple-element.187.refs_2_), channel_id=1, source_target_pairs={{0,4},{1,5},{2,6},{3,7},{4,0},{5,1},{6,2},{7,3},{8,12},{9,13},{10,... | collective-permute-start | bytes 3145736 | tf_op jit(solution)/shard_map/attended_core/ppermute | solution.py:565
  130.9 8.1 %copy-start.45 = (bf16[256,1024]{1,0:T(8,128)(2,1)}, bf16[256,1024]{1,0:T(8,128)(2,1)S(1)}, u32[]{:S(2)}) copy-start(bf16[256,1024]{1,0:T(8,128)(2,1)S(1)} %get-tuple-element.148.refs_2_.refs_7_) | copy-start | bytes 1572868
  130.9 19.1 %copy-start.47 = (bf16[256,1024]{1,0:T(8,128)(2,1)}, bf16[256,1024]{1,0:T(8,128)(2,1)S(1)}, u32[]{:S(2)}) copy-start(bf16[256,1024]{1,0:T(8,128)(2,1)S(1)} %get-tuple-element.150.refs_2_.refs_8_) | copy-start | bytes 1572868
  134.7 25.7 %copy-start.37 = (bf16[256,1024]{1,0:T(8,128)(2,1)}, bf16[256,1024]{1,0:T(8,128)(2,1)S(1)}, u32[]{:S(2)}) copy-start(bf16[256,1024]{1,0:T(8,128)(2,1)S(1)} %get-tuple-element.154.refs_2_.refs_1_) | copy-start | bytes 1572868
  143.2 17.3 %copy-start.39 = (bf16[256,1024]{1,0:T(8,128)(2,1)}, bf16[256,1024]{1,0:T(8,128)(2,1)S(1)}, u32[]{:S(2)}) copy-start(bf16[256,1024]{1,0:T(8,128)(2,1)S(1)} %get-tuple-element.155.refs_3_.refs_2_) | copy-start | bytes 1572868
  143.2 26.6 %collective-permute-start.19 = (bf16[256,1024]{1,0:T(8,128)(2,1)}, bf16[256,1024]{1,0:T(8,128)(2,1)}, u32[]{:S(2)}, u32[]{:S(2)}) collective-permute-start(bf16[256,1024]{1,0:T(8,128)(2,1)} %get-tuple-element.165), channel_id=1, source_target_pairs={{0,8},{1,9},{2,10},{3,11},{4,12},{5,13},{6,14},{7,15},{8,0},{9,1},... | collective-permute-start | bytes 1572872 | tf_op jit(solution)/shard_map/second_around/ppermute | solution.py:565
  154.3 17.6 %collective-permute-start.20 = (bf16[256,1024]{1,0:T(8,128)(2,1)}, bf16[256,1024]{1,0:T(8,128)(2,1)}, u32[]{:S(2)}, u32[]{:S(2)}) collective-permute-start(bf16[256,1024]{1,0:T(8,128)(2,1)} %get-tuple-element.168), channel_id=1, source_target_pairs={{0,24},{1,25},{2,26},{3,27},{4,28},{5,29},{6,30},{7,31},{8,16},{9,... | collective-permute-start | bytes 1572872 | tf_op jit(solution)/shard_map/second_around/ppermute | solution.py:565
  159.7 23.4 %collective-permute-start.21 = (bf16[256,1024]{1,0:T(8,128)(2,1)}, bf16[256,1024]{1,0:T(8,128)(2,1)}, u32[]{:S(2)}, u32[]{:S(2)}) collective-permute-start(bf16[256,1024]{1,0:T(8,128)(2,1)} %get-tuple-element.173), channel_id=1, source_target_pairs={{0,16},{1,17},{2,18},{3,19},{4,20},{5,21},{6,22},{7,23},{8,24},{9,... | collective-permute-start | bytes 1572872 | tf_op jit(solution)/shard_map/second_around/ppermute | solution.py:565
  169.8 27.9 %collective-permute-start.22 = (bf16[512,1024]{1,0:T(8,128)(2,1)}, bf16[512,1024]{1,0:T(8,128)(2,1)}, u32[]{:S(2)}, u32[]{:S(2)}) collective-permute-start(bf16[512,1024]{1,0:T(8,128)(2,1)} %get-tuple-element.176), channel_id=1, source_target_pairs={{0,4},{1,5},{2,6},{3,7},{4,0},{5,1},{6,2},{7,3},{8,12},{9,13},{10,... | collective-permute-start | bytes 3145736 | tf_op jit(solution)/shard_map/down_core/ppermute | solution.py:565
  172.0 42.9 %collective-permute-start.24 = (bf16[4,128,1024]{2,1,0:T(8,128)(2,1)}, bf16[4,128,1024]{2,1,0:T(8,128)(2,1)}, u32[]{:S(2)}, u32[]{:S(2)}) collective-permute-start(bf16[4,128,1024]{2,1,0:T(8,128)(2,1)} %get-tuple-element.185), channel_id=1, source_target_pairs={{0,4},{1,5},{2,6},{3,7},{4,0},{5,1},{6,2},{7,3},{8,12},{9,13},{10,... | collective-permute-start | bytes 3145736 | tf_op jit(solution)/shard_map/up_core/ppermute | solution.py:565
  172.0 11.1 %copy-start.1 = (f32[2,256,128]{2,1,0:T(8,128)S(1)}, f32[2,256,128]{2,1,0:T(8,128)}, u32[]{:S(2)}) copy-start(f32[2,256,128]{2,1,0:T(8,128)} %copy-done) | copy-start | bytes 786436
  172.0 11.1 %copy-start.6 = (bf16[1024,4096]{1,0:T(8,128)(2,1)S(1)}, bf16[1024,4096]{1,0:T(8,128)(2,1)}, u32[]{:S(2)}) copy-start(bf16[1024,4096]{1,0:T(8,128)(2,1)} %all-gather.3.cloned.1.call-done) | copy-start | bytes 25165828
  172.0 11.1 %copy-start.27 = (bf16[256,1024]{1,0:T(8,128)(2,1)S(1)}, bf16[256,1024]{1,0:T(8,128)(2,1)}, u32[]{:S(2)}) copy-start(bf16[256,1024]{1,0:T(8,128)(2,1)} %copy-done.26) | copy-start | bytes 1572868
  172.0 11.1 %copy-start.29 = (bf16[256,1024]{1,0:T(8,128)(2,1)S(1)}, bf16[256,1024]{1,0:T(8,128)(2,1)}, u32[]{:S(2)}) copy-start(bf16[256,1024]{1,0:T(8,128)(2,1)} %copy-done.28) | copy-start | bytes 1572868
  197.6 4.6 %collective-permute-start.23 = (bf16[4,256,1024]{2,1,0:T(8,128)(2,1)}, bf16[4,256,1024]{2,1,0:T(8,128)(2,1)}, u32[]{:S(2)}, u32[]{:S(2)}) collective-permute-start(bf16[4,256,1024]{2,1,0:T(8,128)(2,1)} %get-tuple-element.181), channel_id=1, source_target_pairs={{0,4},{1,5},{2,6},{3,7},{4,0},{5,1},{6,2},{7,3},{8,12},{9,13},{10,... | collective-permute-start | bytes 6291464 | tf_op jit(solution)/shard_map/pair_grads_core/ppermute | solution.py:565
  207.8 7.1 %copy-start.25 = (bf16[4,128,1024]{2,1,0:T(8,128)(2,1)S(1)}, bf16[4,128,1024]{2,1,0:T(8,128)(2,1)}, u32[]{:S(2)}) copy-start(bf16[4,128,1024]{2,1,0:T(8,128)(2,1)} %copy-done.24) | copy-start | bytes 3145732
  214.7 15.2 %collective-permute-start.27 = (bf16[784,1024]{1,0:T(8,128)(2,1)}, bf16[784,1024]{1,0:T(8,128)(2,1)}, u32[]{:S(2)}, u32[]{:S(2)}) collective-permute-start(bf16[784,1024]{1,0:T(8,128)(2,1)} %get-tuple-element.191.refs_4_.refs_1_), channel_id=1, source_target_pairs={{0,4},{1,5},{2,6},{3,7},{4,0},{5,1},{6,2},{7,3},{8,12},{9,13},{10,... | collective-permute-start | bytes 4816904 | tf_op jit(solution)/shard_map/zero_core/ppermute | solution.py:565
  217.4 25.3 %all-to-all-start.1 = ((bf16[4,128,1024]{2,1,0:T(8,128)(2,1)}), bf16[4,128,1024]{2,1,0:T(8,128)(2,1)}, u32[]{:S(2)}, u32[]{:S(2)}) async-start(bf16[4,128,1024]{2,1,0:T(8,128)(2,1)} %get-tuple-element.194), calls=%async_computation.1 | async-start | bytes 2097152 | tf_op jit(solution)/shard_map/all_to_all | solution.py:702
  221.8 148.3 %all-reduce.8.cloned.1.call-start = ((), (), s32[]{:S(2)}) async-start(), calls=%async_computation.3 | async-start | bytes 2097152 | tf_op jit(solution)/shard_map/psum | solution.py:880
  227.9 31.4 %collective-permute-start.28 = (bf16[2,256,1024]{2,1,0:T(8,128)(2,1)}, bf16[2,256,1024]{2,1,0:T(8,128)(2,1)}, u32[]{:S(2)}, u32[]{:S(2)}) collective-permute-start(bf16[2,256,1024]{2,1,0:T(8,128)(2,1)} %get-tuple-element.197), channel_id=1, source_target_pairs={{0,8},{1,9},{2,10},{3,11},{4,12},{5,13},{6,14},{7,15},{8,0},{9,1},... | collective-permute-start | bytes 3145736 | tf_op jit(solution)/shard_map/query_x/ppermute | solution.py:565
  235.4 47.2 %collective-permute-start.29 = (bf16[2,272,1024]{2,1,0:T(8,128)(2,1)}, bf16[2,272,1024]{2,1,0:T(8,128)(2,1)}, u32[]{:S(2)}, u32[]{:S(2)}) collective-permute-start(bf16[2,272,1024]{2,1,0:T(8,128)(2,1)} %get-tuple-element.200), channel_id=1, source_target_pairs={{0,8},{1,9},{2,10},{3,11},{4,12},{5,13},{6,14},{7,15},{8,0},{9,1},... | collective-permute-start | bytes 3342344 | tf_op jit(solution)/shard_map/merge_x/ppermute | solution.py:565
  240.7 45.5 %collective-permute-start.30 = (bf16[2,256,1024]{2,1,0:T(8,128)(2,1)}, bf16[2,256,1024]{2,1,0:T(8,128)(2,1)}, u32[]{:S(2)}, u32[]{:S(2)}) collective-permute-start(bf16[2,256,1024]{2,1,0:T(8,128)(2,1)} %get-tuple-element.203), channel_id=1, source_target_pairs={{0,16},{1,17},{2,18},{3,19},{4,20},{5,21},{6,22},{7,23},{8,24},{9,... | collective-permute-start | bytes 3145736 | tf_op jit(solution)/shard_map/pair_y/ppermute | solution.py:565
  242.7 16.6 %copy-start.23 = (bf16[2,256,1024]{2,1,0:T(8,128)(2,1)S(1)}, bf16[2,256,1024]{2,1,0:T(8,128)(2,1)}, u32[]{:S(2)}) copy-start(bf16[2,256,1024]{2,1,0:T(8,128)(2,1)} %copy-done.22) | copy-start | bytes 3145732
  262.2 26.8 %collective-permute-start.31 = (bf16[256,1024]{1,0:T(8,128)(2,1)}, bf16[256,1024]{1,0:T(8,128)(2,1)}, u32[]{:S(2)}, u32[]{:S(2)}) collective-permute-start(bf16[256,1024]{1,0:T(8,128)(2,1)} %get-tuple-element.206), channel_id=1, source_target_pairs={{0,16},{1,17},{2,18},{3,19},{4,20},{5,21},{6,22},{7,23},{8,24},{9,... | collective-permute-start | bytes 1572872 | tf_op jit(solution)/shard_map/query_y/ppermute | solution.py:565
  263.7 135.7 %all-reduce.10.cloned.1.call-start = ((), (), s32[]{:S(2)}) async-start(), calls=%async_computation.5 | async-start | bytes 3211264 | tf_op jit(solution)/shard_map/psum | solution.py:894
  284.8 14.4 %collective-permute-start.32 = (bf16[272,1024]{1,0:T(8,128)(2,1)}, bf16[272,1024]{1,0:T(8,128)(2,1)}, u32[]{:S(2)}, u32[]{:S(2)}) collective-permute-start(bf16[272,1024]{1,0:T(8,128)(2,1)} %get-tuple-element.209), channel_id=1, source_target_pairs={{0,16},{1,17},{2,18},{3,19},{4,20},{5,21},{6,22},{7,23},{8,24},{9,... | collective-permute-start | bytes 1671176 | tf_op jit(solution)/shard_map/merge_y/ppermute | solution.py:565
  288.5 13.4 %collective-permute-start.33 = (bf16[256,1024]{1,0:T(8,128)(2,1)}, bf16[256,1024]{1,0:T(8,128)(2,1)}, u32[]{:S(2)}, u32[]{:S(2)}) collective-permute-start(bf16[256,1024]{1,0:T(8,128)(2,1)} %get-tuple-element.212), channel_id=1, source_target_pairs={{0,8},{1,9},{2,10},{3,11},{4,12},{5,13},{6,14},{7,15},{8,0},{9,1},... | collective-permute-start | bytes 1572872 | tf_op jit(solution)/shard_map/pair_x/ppermute | solution.py:565
  303.8 1.2 collective-permute-start.34
  307.4 10.4 %collective-permute-start.35 = (bf16[128,1024]{1,0:T(8,128)(2,1)}, bf16[128,1024]{1,0:T(8,128)(2,1)}, u32[]{:S(2)}, u32[]{:S(2)}) collective-permute-start(bf16[128,1024]{1,0:T(8,128)(2,1)} %get-tuple-element.216), channel_id=1, source_target_pairs={{0,0},{1,4},{2,1},{3,5},{4,2},{5,6},{6,3},{7,7},{8,8},{9,12},{10,9... | collective-permute-start | bytes 786440 | tf_op jit(solution)/shard_map/zero_out/ppermute | solution.py:565
  311.0 15.4 %collective-permute-start.36 = (bf16[128,1024]{1,0:T(8,128)(2,1)}, bf16[128,1024]{1,0:T(8,128)(2,1)}, u32[]{:S(2)}, u32[]{:S(2)}) collective-permute-start(bf16[128,1024]{1,0:T(8,128)(2,1)} %get-tuple-element.217), channel_id=1, source_target_pairs={{0,1},{1,5},{2,0},{3,4},{4,3},{5,7},{6,2},{7,6},{8,9},{9,13},{10,8... | collective-permute-start | bytes 786440 | tf_op jit(solution)/shard_map/zero_out/ppermute | solution.py:565
  314.4 19.9 %collective-permute-start.37 = (bf16[256,1024]{1,0:T(8,128)(2,1)}, bf16[256,1024]{1,0:T(8,128)(2,1)}, u32[]{:S(2)}, u32[]{:S(2)}) collective-permute-start(bf16[256,1024]{1,0:T(8,128)(2,1)} %get-tuple-element.220), channel_id=1, source_target_pairs={{0,8},{1,9},{2,10},{3,11},{4,12},{5,13},{6,14},{7,15},{8,0},{9,1},... | collective-permute-start | bytes 1572872 | tf_op jit(solution)/shard_map/result_around/ppermute | solution.py:565
  314.9 25.3 %collective-permute-start.38 = (bf16[256,1024]{1,0:T(8,128)(2,1)}, bf16[256,1024]{1,0:T(8,128)(2,1)}, u32[]{:S(2)}, u32[]{:S(2)}) collective-permute-start(bf16[256,1024]{1,0:T(8,128)(2,1)} %get-tuple-element.221), channel_id=1, source_target_pairs={{0,24},{1,25},{2,26},{3,27},{4,28},{5,29},{6,30},{7,31},{8,16},{9,... | collective-permute-start | bytes 1572872 | tf_op jit(solution)/shard_map/result_around/ppermute | solution.py:565
  316.6 26.1 %collective-permute-start.39 = (bf16[256,1024]{1,0:T(8,128)(2,1)}, bf16[256,1024]{1,0:T(8,128)(2,1)}, u32[]{:S(2)}, u32[]{:S(2)}) collective-permute-start(bf16[256,1024]{1,0:T(8,128)(2,1)} %get-tuple-element.222), channel_id=1, source_target_pairs={{0,16},{1,17},{2,18},{3,19},{4,20},{5,21},{6,22},{7,23},{8,24},{9,... | collective-permute-start | bytes 1572872 | tf_op jit(solution)/shard_map/result_around/ppermute | solution.py:565
  334.3 8.4 %copy-start.19 = (f32[256,1024]{1,0:T(8,128)S(1)}, f32[256,1024]{1,0:T(8,128)}, u32[]{:S(2)}) copy-start(f32[256,1024]{1,0:T(8,128)} %copy-done.18) | copy-start | bytes 3145732
  345.0 4.0 collective-permute-start.40
  348.6 19.0 %collective-permute-start.41 = (bf16[128,1024]{1,0:T(8,128)(2,1)}, bf16[128,1024]{1,0:T(8,128)(2,1)}, u32[]{:S(2)}, u32[]{:S(2)}) collective-permute-start(bf16[128,1024]{1,0:T(8,128)(2,1)} %get-tuple-element.225), channel_id=1, source_target_pairs={{0,1},{1,5},{2,0},{3,4},{4,3},{5,7},{6,2},{7,6},{8,9},{9,13},{10,8... | collective-permute-start | bytes 786440 | tf_op jit(solution)/shard_map/result_out/ppermute | solution.py:565
  (42 other events, 137.8 us)
Sparse Core Ops, SparseCore 0:
  16.3 76.2 all-gather.2
  200.6 51.4 all-reduce.5
  263.8 54.3 all-reduce.7
  321.3 78.1 all-reduce.9
